TPU v7x, 256 devices: a whole 4x4x8 slice. The times are simulated.
256 devices in a mesh: frame: 16 (over z, x_lo), row: 16 (over y, x_hi, core).
Axes of the slice: x: 4 (x_hi: 2, x_lo: 2; x = x_hi * 2 + x_lo), y: 4, z: 8, core: 2. Of those that a mesh axis runs over, the one named last changes fastest.
Arguments:
- latents: bfloat16 [16, 64, 128, 320], P('frame', 'row'), may hold values from -6 to 6
- conv_weight: bfloat16 [3, 3, 320, 320], replicated, may hold values from -0.109375 to 0.109375
- query_weight: bfloat16 [320, 320], replicated, may hold values from -0.3125 to 0.3125
- key_weight: bfloat16 [320, 320], replicated, may hold values from -0.3125 to 0.3125
- value_weight: bfloat16 [320, 320], replicated, may hold values from -0.3125 to 0.3125
- out_weight: bfloat16 [320, 320], replicated, may hold values from -0.3125 to 0.3125
- norm_gain: float32 [320], replicated, may hold values from 0.1 to 1.9
- out_grad: bfloat16 [16, 64, 128, 320], P('frame', 'row'), may hold values from -6 to 6
Outputs:
- block_out: bfloat16 [16, 64, 128, 320], P('frame', 'row')
- latents_grad: bfloat16 [16, 64, 128, 320], P('frame', 'row')
- conv_grad: float32 [3, 3, 320, 320], replicated
- query_grad: float32 [320, 320], replicated
- key_grad: float32 [320, 320], replicated
- value_grad: float32 [320, 320], replicated
- out_weight_grad: float32 [320, 320], replicated
- gain_grad: float32 [320], replicated
All inputs are finite; a program needn't handle non-finite values.
Results may differ from a plain program's by a relative error of at most 0.02.
Values may be sent and summed in bfloat16 or wider, within the bound.
A program may use at most 64 MiB of HBM per device.

v0:
```python
import jax
import jax.numpy as jnp
from jax import lax
from jax.sharding import PartitionSpec as P

HEADS = 5


EPS = 1e-06


def padded_2(cells, sides, width):
    for axis, dim in sides:
        count = lax.axis_size(axis)
        ends = count - 1
        head = lax.slice_in_dim(cells, 0, width, axis=dim)
        tail = lax.slice_in_dim(cells, cells.shape[dim] - width, cells.shape[dim], axis=dim)
        cells = jnp.concatenate(
            [
                lax.ppermute(tail, axis, [(i, (i + 1) % count) for i in range(ends)]),
                cells,
                lax.ppermute(head, axis, [((i + 1) % count, i) for i in range(ends)]),
            ],
            axis=dim,
        )
    return cells


def pad_rows(field):
    rimmed = padded_2(field, (("row", 1),), 1)
    return jnp.pad(rimmed, ((0, 0), (0, 0), (1, 1), (0, 0)))


def to_pixels(stacked):
    return lax.all_to_all(stacked, "frame", split_axis=3, concat_axis=1, tiled=True)


def to_frames(stacked):
    return lax.all_to_all(stacked, "frame", split_axis=1, concat_axis=3, tiled=True)


def conv_apply(padded, weight, rows, width):
    total = None
    for row_off in range(3):
        for col_off in range(3):
            piece = padded[:, row_off : row_off + rows, col_off : col_off + width, :]
            term = jnp.dot(piece, weight[row_off, col_off], preferred_element_type=jnp.float32)
            total = term if total is None else total + term
    return total


def outer_sum(left, right):
    left_flat = left.reshape(-1, left.shape[-1])
    right_flat = right.reshape(-1, right.shape[-1])
    return lax.dot_general(
        left_flat, right_flat, (((0,), (0,)), ((), ())), preferred_element_type=jnp.float32
    )


def back_dot(field, weight):
    return lax.dot_general(
        field, weight, (((field.ndim - 1,), (1,)), ((), ())), preferred_element_type=jnp.float32
    )


def conv_weight_grad(padded, grad, rows, width):
    taps = []
    for row_off in range(3):
        for col_off in range(3):
            piece = padded[:, row_off : row_off + rows, col_off : col_off + width, :]
            taps.append(outer_sum(piece, grad))
    chan = grad.shape[-1]
    return jnp.stack(taps).reshape(3, 3, chan, chan)


def conv_input_grad(grad_pad, weight, rows, width):
    total = None
    for row_off in range(3):
        for col_off in range(3):
            piece = grad_pad[
                :, 2 - row_off : 2 - row_off + rows, 2 - col_off : 2 - col_off + width, :
            ]
            term = back_dot(piece, weight[row_off, col_off])
            total = term if total is None else total + term
    return total


def split_heads(field):
    frames, rows, width, chan = field.shape
    return field.reshape(frames, rows, width, HEADS, chan // HEADS)


def attend(queries, key_rows, value_rows):
    frames, rows, width, chan = queries.shape
    factor = (chan // HEADS) ** (-0.5)
    scores = (
        jnp.einsum(
            "frwhd,grwhd->rwhfg",
            split_heads(queries),
            split_heads(key_rows),
            preferred_element_type=jnp.float32,
        )
        * factor
    )
    expo = jnp.exp(scores)
    probs = expo / jnp.sum(expo, axis=-1, keepdims=True)
    probs_b = probs.astype(jnp.bfloat16)
    mixed = jnp.einsum(
        "rwhfg,grwhd->frwhd", probs_b, split_heads(value_rows), preferred_element_type=jnp.float32
    )
    return (probs, probs_b, mixed.reshape(frames, rows, width, chan).astype(jnp.bfloat16))


def attend_back(probs, probs_b, queries, key_rows, value_rows, mixed_grad):
    frames, rows, width, chan = queries.shape
    factor = (chan // HEADS) ** (-0.5)
    grad_heads = split_heads(mixed_grad)
    prob_grad = jnp.einsum(
        "frwhd,grwhd->rwhfg",
        grad_heads,
        split_heads(value_rows),
        preferred_element_type=jnp.float32,
    )
    score_grad = probs * (prob_grad - jnp.sum(probs * prob_grad, axis=-1, keepdims=True)) * factor
    score_b = score_grad.astype(jnp.bfloat16)
    query_part = jnp.einsum(
        "rwhfg,grwhd->frwhd", score_b, split_heads(key_rows), preferred_element_type=jnp.float32
    )
    key_part = jnp.einsum(
        "rwhfg,frwhd->grwhd", score_b, split_heads(queries), preferred_element_type=jnp.float32
    )
    value_part = jnp.einsum(
        "rwhfg,frwhd->grwhd", probs_b, grad_heads, preferred_element_type=jnp.float32
    )
    shape = (frames, rows, width, chan)
    return (
        query_part.reshape(shape).astype(jnp.bfloat16),
        key_part.reshape(shape).astype(jnp.bfloat16),
        value_part.reshape(shape).astype(jnp.bfloat16),
    )


def project(normed, weight):
    return jnp.dot(normed, weight, preferred_element_type=jnp.float32).astype(jnp.bfloat16)


def on_device(
    latents, conv_weight, query_weight, key_weight, value_weight, out_weight, norm_gain, out_grad
):
    frames, rows, width, chan = latents.shape
    cells_all = frames * rows * width * lax.axis_size("frame") * lax.axis_size("row")
    latent_f = latents.astype(jnp.float32)
    sigma = jax.nn.sigmoid(latent_f)
    act = (latent_f * sigma).astype(jnp.bfloat16)
    padded = pad_rows(act)
    resid = (latent_f + conv_apply(padded, conv_weight, rows, width)).astype(jnp.bfloat16)
    resid_f = resid.astype(jnp.float32)
    inv_rms = lax.rsqrt(jnp.mean(resid_f * resid_f, axis=-1, keepdims=True) + EPS)
    normed = (resid_f * inv_rms * norm_gain).astype(jnp.bfloat16)
    local_qkv = jnp.stack(
        [project(normed, query_weight), project(normed, key_weight), project(normed, value_weight)]
    )
    moved = to_pixels(local_qkv)
    queries, key_rows, value_rows = (moved[0], moved[1], moved[2])
    probs, probs_b, mixed_pix = attend(queries, key_rows, value_rows)
    mixed = to_frames(mixed_pix[None])[0]
    block_out = (resid_f + jnp.dot(mixed, out_weight, preferred_element_type=jnp.float32)).astype(
        jnp.bfloat16
    )
    grad_out_w = outer_sum(mixed, out_grad)
    mixed_grad = back_dot(out_grad, out_weight).astype(jnp.bfloat16)
    mixed_grad_pix = to_pixels(mixed_grad[None])[0]
    query_part, key_part, value_part = attend_back(
        probs, probs_b, queries, key_rows, value_rows, mixed_grad_pix
    )
    returned = to_frames(jnp.stack([query_part, key_part, value_part]))
    query_back, key_back, value_back = (returned[0], returned[1], returned[2])
    grad_query = outer_sum(normed, query_back)
    grad_key = outer_sum(normed, key_back)
    grad_value = outer_sum(normed, value_back)
    normed_grad = (
        back_dot(query_back, query_weight)
        + back_dot(key_back, key_weight)
        + back_dot(value_back, value_weight)
    ).astype(jnp.bfloat16)
    normed_gf = normed_grad.astype(jnp.float32)
    grad_gain = jnp.sum((normed_gf * resid_f * inv_rms).reshape(-1, chan), axis=0)
    tangent = normed_gf * norm_gain
    resid_part = inv_rms * tangent - resid_f * inv_rms**3 * jnp.mean(
        tangent * resid_f, axis=-1, keepdims=True
    )
    resid_grad = (out_grad.astype(jnp.float32) + resid_part).astype(jnp.bfloat16)
    grad_conv = conv_weight_grad(padded, resid_grad, rows, width)
    grad_pad = pad_rows(resid_grad)
    act_grad = conv_input_grad(grad_pad, conv_weight, rows, width)
    latents_grad = (
        resid_grad.astype(jnp.float32) + act_grad * sigma * (1.0 + latent_f * (1.0 - sigma))
    ).astype(jnp.bfloat16)
    summed = lax.psum(
        (grad_conv, grad_query, grad_key, grad_value, grad_out_w, grad_gain), ("frame", "row")
    )
    factor = cells_all ** (-0.5)
    return (
        block_out,
        latents_grad,
        summed[0] * factor,
        summed[1] * factor,
        summed[2] * factor,
        summed[3] * factor,
        summed[4] * factor,
        summed[5] * factor,
    )


def solution(mesh):
    return jax.shard_map(
        on_device,
        mesh=mesh,
        in_specs=(
            P("frame", "row", None, None),
            P(),
            P(),
            P(),
            P(),
            P(),
            P(),
            P("frame", "row", None, None),
        ),
        out_specs=(
            P("frame", "row", None, None),
            P("frame", "row", None, None),
            P(),
            P(),
            P(),
            P(),
            P(),
            P(),
        ),
        check_vma=False,
    )
```

profile of v0, /device:TPU:1, one launch (start us, length us, event | category | flops | bytes accessed | tf_op | source)
XLA Modules:
  0.0 550.9 jit_solution(5751552829313286797)
XLA Ops:
  8.4 6.0 %collective-permute-start = (bf16[1,1,128,320]{2,3,1,0:T(8,128)(2,1)S(1)}, bf16[1,1,128,320]{2,3,1,0:T(8,128)(2,1)S(1)}, u32[]{:S(2)}, u32[]{:S(2)}) collective-permute-start(bf16[1,1,128,320]{2,3,1,0:T(8,128)(2,1)S(1)} %get-tuple-element.23), channel_id=1, source_target_pairs={{0,1},{1,2},{2,3},{3,4},{4,5},{5,6},{6,7},{7,8},{8,9},{9,10},{10,1... | collective-permute-start | bytes 245768 | tf_op jit(solution)/shard_map/ppermute | solution.py:20
  18.8 8.4 %all-to-all-start.2 = ((bf16[1,1,4,128,320]{4,2,1,0,3:T(4,128)(2,1)}), bf16[1,1,4,128,320]{4,2,1,0,3:T(4,128)(2,1)}, u32[]{:S(2)}, u32[]{:S(2)}) async-start(bf16[1,1,4,128,320]{4,2,1,0,3:T(4,128)(2,1)} %copy.122), calls=%async_computation.2 | async-start | bytes 786432 | tf_op jit(solution)/shard_map/all_to_all | solution.py:35
  37.4 2.8 all-to-all-done.2
  40.3 4.7 all-to-all-start
  48.3 27.2 %all-to-all-done = bf16[3,1,4,128,320]{4,2,1,0,3:T(4,128)(2,1)} async-done(((bf16[3,1,4,128,320]{4,2,1,0,3:T(4,128)(2,1)}), bf16[3,1,4,128,320]{4,2,1,0,3:T(4,128)(2,1)}, u32[]{:S(2)}, u32[]{:S(2)}) %all-to-all-start) | async-done | bytes 983072 | tf_op jit(solution)/shard_map/all_to_all | solution.py:35
  78.0 2.3 reshape.363
  82.7 2.3 reshape.362
  85.0 3.8 fusion.59
  88.8 3.4 fusion.68
  93.7 4.7 fusion.9
  98.4 2.3 copy.131
  100.7 2.4 convert_element_type.150
  103.1 2.3 copy.117
  105.4 2.4 convert_element_type.140
  107.8 4.2 all-to-all-start.1
  112.0 4.7 fusion.8
  116.7 2.4 copy.129
  119.1 2.4 convert_element_type.147
  127.6 7.5 %all-to-all-start.3 = ((bf16[3,16,4,8,320]{4,3,2,0,1:T(8,128)(2,1)}), bf16[3,16,4,8,320]{4,3,2,0,1:T(8,128)(2,1)}, u32[]{:S(2)}, u32[]{:S(2)}) async-start(bf16[3,16,4,8,320]{4,3,2,0,1:T(8,128)(2,1)} %copy.134), calls=%async_computation.3 | async-start | bytes 2359296 | tf_op jit(solution)/shard_map/all_to_all | solution.py:39
  140.0 25.2 %all-to-all-done.3 = bf16[3,16,4,8,320]{4,3,2,0,1:T(8,128)(2,1)} async-done(((bf16[3,16,4,8,320]{4,3,2,0,1:T(8,128)(2,1)}), bf16[3,16,4,8,320]{4,3,2,0,1:T(8,128)(2,1)}, u32[]{:S(2)}, u32[]{:S(2)}) %all-to-all-start.3) | async-done | bytes 983072 | tf_op jit(solution)/shard_map/all_to_all | solution.py:39
  173.3 75.0 %psum.47 = f32[320]{0:T(512)S(1)} all-reduce(f32[320]{0:T(512)S(1)} %get-tuple-element.8), channel_id=1, replica_groups=mesh['frame'=16,'row'=16] {'frame','row'}, use_global_device_ids=true, to_apply=%region_10.11 | all-reduce | flops 320 | bytes 2560 | tf_op jit(solution)/shard_map/psum | solution.py:199
  248.3 3.6 collective-permute-start.2
  269.4 267.3 %all-reduce.5.cloned.1.call-done = (f32[3,3,320,320]{3,2,1,0:T(8,128)}, f32[320,320]{1,0:T(8,128)}, f32[320,320]{1,0:T(8,128)}, f32[320,320]{1,0:T(8,128)}, f32[320,320]{1,0:T(8,128)}) async-done(((f32[3,3,320,320]{3,2,1,0:T(8,128)}, f32[320,320]{1,0:T(8,128)}, f32[320,320]{1,0:T(8,128)}, f32[320,320]{1,0:T(8,128)}, f32[320,320]{1,0:T(8,128)}), (f32[3,3,320,320]{3,2,1,0:T(8,128)}, f32[320,320]{1,0:T(8,128)}, ...) | async-done | bytes 5324816 | tf_op jit(solution)/shard_map/psum | solution.py:199
  536.7 4.8 broadcast_multiply_fusion
  (123 shorter events, 64.0 us)
Async XLA Ops:
  7.2 27.4 %copy-start = (bf16[320,320]{1,0:T(8,128)(2,1)S(1)}, bf16[320,320]{1,0:T(8,128)(2,1)}, u32[]{:S(2)}) copy-start(bf16[320,320]{1,0:T(8,128)(2,1)} %param.12) | copy-start | bytes 614404
  8.4 18.8 %collective-permute-start = (bf16[1,1,128,320]{2,3,1,0:T(8,128)(2,1)S(1)}, bf16[1,1,128,320]{2,3,1,0:T(8,128)(2,1)S(1)}, u32[]{:S(2)}, u32[]{:S(2)}) collective-permute-start(bf16[1,1,128,320]{2,3,1,0:T(8,128)(2,1)S(1)} %get-tuple-element.23), channel_id=1, source_target_pairs={{0,1},{1,2},{2,3},{3,4},{4,5},{5,6},{6,7},{7,8},{8,9},{9,10},{10,1... | collective-permute-start | bytes 245768 | tf_op jit(solution)/shard_map/ppermute | solution.py:20
  14.5 12.7 %collective-permute-start.1 = (bf16[1,1,128,320]{2,3,1,0:T(8,128)(2,1)S(1)}, bf16[1,1,128,320]{2,3,1,0:T(8,128)(2,1)S(1)}, u32[]{:S(2)}, u32[]{:S(2)}) collective-permute-start(bf16[1,1,128,320]{2,3,1,0:T(8,128)(2,1)S(1)} %get-tuple-element.24), channel_id=1, source_target_pairs={{1,0},{2,1},{3,2},{4,3},{5,4},{6,5},{7,6},{8,7},{9,8},{10,9},{11,1... | collective-permute-start | bytes 245768 | tf_op jit(solution)/shard_map/ppermute | solution.py:22
  18.8 21.5 %all-to-all-start.2 = ((bf16[1,1,4,128,320]{4,2,1,0,3:T(4,128)(2,1)}), bf16[1,1,4,128,320]{4,2,1,0,3:T(4,128)(2,1)}, u32[]{:S(2)}, u32[]{:S(2)}) async-start(bf16[1,1,4,128,320]{4,2,1,0,3:T(4,128)(2,1)} %copy.122), calls=%async_computation.2 | async-start | bytes 786432 | tf_op jit(solution)/shard_map/all_to_all | solution.py:35
  27.2 3.4 copy-start.1
  27.2 3.4 copy-start.14
  27.2 6.0 %copy-start.12 = (bf16[1,1,128,320]{2,3,1,0:T(8,128)(2,1)}, bf16[1,1,128,320]{2,3,1,0:T(8,128)(2,1)S(1)}, u32[]{:S(2)}) copy-start(bf16[1,1,128,320]{2,3,1,0:T(8,128)(2,1)S(1)} %collective-permute-done.1) | copy-start | bytes 245764
  33.2 1.7 copy-start.9
  40.3 35.3 %all-to-all-start = ((bf16[3,1,4,128,320]{4,2,1,0,3:T(4,128)(2,1)}), bf16[3,1,4,128,320]{4,2,1,0,3:T(4,128)(2,1)}, u32[]{:S(2)}, u32[]{:S(2)}) async-start(bf16[3,1,4,128,320]{4,2,1,0,3:T(4,128)(2,1)} %copy.108), calls=%async_computation | async-start | bytes 2359296 | tf_op jit(solution)/shard_map/all_to_all | solution.py:35
  88.8 3.4 copy-start.3
  88.8 3.5 copy-start.4
  107.8 19.8 %all-to-all-start.1 = ((bf16[1,16,4,8,320]{4,3,2,0,1:T(8,128)(2,1)}), bf16[1,16,4,8,320]{4,3,2,0,1:T(8,128)(2,1)}, u32[]{:S(2)}, u32[]{:S(2)}) async-start(bf16[1,16,4,8,320]{4,3,2,0,1:T(8,128)(2,1)} %bitcast.384), calls=%async_computation.1 | async-start | bytes 786432 | tf_op jit(solution)/shard_map/all_to_all | solution.py:39
  126.5 8.7 %copy-start.5 = (bf16[1,4,128,320]{2,3,1,0:T(8,128)(2,1)S(1)}, bf16[1,4,128,320]{2,3,1,0:T(8,128)(2,1)}, u32[]{:S(2)}) copy-start(bf16[1,4,128,320]{2,3,1,0:T(8,128)(2,1)} %param.15) | copy-start | bytes 983044
  127.6 37.6 %all-to-all-start.3 = ((bf16[3,16,4,8,320]{4,3,2,0,1:T(8,128)(2,1)}), bf16[3,16,4,8,320]{4,3,2,0,1:T(8,128)(2,1)}, u32[]{:S(2)}, u32[]{:S(2)}) async-start(bf16[3,16,4,8,320]{4,3,2,0,1:T(8,128)(2,1)} %copy.134), calls=%async_computation.3 | async-start | bytes 2359296 | tf_op jit(solution)/shard_map/all_to_all | solution.py:39
  135.1 2.8 copy-start.8
  135.1 401.6 %all-reduce.5.cloned.1.call-start = ((), (), s32[]{:S(2)}) async-start(), calls=%async_computation.4 | async-start | bytes 12779520 | tf_op jit(solution)/shard_map/psum | solution.py:199
  169.9 83.9 %copy-start.15 = (bf16[1,1,128,320]{2,3,1,0:T(8,128)(2,1)S(1)}, bf16[1,1,128,320]{2,3,1,0:T(8,128)(2,1)}, u32[]{:S(2)}) copy-start(bf16[1,1,128,320]{2,3,1,0:T(8,128)(2,1)} %copy-done.14) | copy-start | bytes 245764
  173.3 84.0 %copy-start.7 = (bf16[1,4,128,320]{2,3,1,0:T(8,128)(2,1)S(1)}, bf16[1,4,128,320]{2,3,1,0:T(8,128)(2,1)}, u32[]{:S(2)}) copy-start(bf16[1,4,128,320]{2,3,1,0:T(8,128)(2,1)} %param.8) | copy-start | bytes 983044
  248.3 15.4 %collective-permute-start.2 = (bf16[1,1,128,320]{2,3,1,0:T(8,128)(2,1)S(1)}, bf16[1,1,128,320]{2,3,1,0:T(8,128)(2,1)S(1)}, u32[]{:S(2)}, u32[]{:S(2)}) collective-permute-start(bf16[1,1,128,320]{2,3,1,0:T(8,128)(2,1)S(1)} %get-tuple-element.21), channel_id=1, source_target_pairs={{0,1},{1,2},{2,3},{3,4},{4,5},{5,6},{6,7},{7,8},{8,9},{9,10},{10,1... | collective-permute-start | bytes 245768 | tf_op jit(solution)/shard_map/ppermute | solution.py:20
  251.9 11.7 %collective-permute-start.3 = (bf16[1,1,128,320]{2,3,1,0:T(8,128)(2,1)S(1)}, bf16[1,1,128,320]{2,3,1,0:T(8,128)(2,1)S(1)}, u32[]{:S(2)}, u32[]{:S(2)}) collective-permute-start(bf16[1,1,128,320]{2,3,1,0:T(8,128)(2,1)S(1)} %get-tuple-element.22), channel_id=1, source_target_pairs={{1,0},{2,1},{3,2},{4,3},{5,4},{6,5},{7,6},{8,7},{9,8},{10,9},{11,1... | collective-permute-start | bytes 245768 | tf_op jit(solution)/shard_map/ppermute | solution.py:22
  258.4 2.3 copy-start.13
  263.1 2.5 copy-start.2
  536.7 4.8 copy-start.18
  536.7 4.8 copy-start.19
  (6 other events, 6.4 us)
Sparse Core Ops, SparseCore 0:
  263.2 273.4 all-reduce.4
where the time goes:
time: 553 us; the launch traced here: 551 us
  waiting for transfers between devices  323 us (58%)
  blocking collectives  75 us (14%)
  matrix products  51.6 us (9%)
  starting transfers between devices  38.3 us (7%)
  local copies, waits for them, and re-layouts  37.1 us (7%)
  between operations  14.6 us (3%)
  other arithmetic  11.6 us (2%)
    psum x1, waiting for transfers between devices, on_device(): lax.psum((grad_conv, grad_query, grad_key, grad_value, grad_out_w, grad_g...  267 us
    psum x1, blocking collectives, on_device(): lax.psum((grad_conv, grad_query, grad_key, grad_value, grad_out_w, grad_g...  75 us
    all_to_all x2, waiting for transfers between devices, to_pixels(): lax.all_to_all(stacked, 'frame', split_axis=3, concat_axis=1, tiled=True)  30 us
    all_to_all x2, waiting for transfers between devices, to_frames(): lax.all_to_all(stacked, 'frame', split_axis=1, concat_axis=3, tiled=True)  25.3 us
    dot_general x13, matrix products, outer_sum(): lax.dot_general(left_flat, right_flat, (((0,), (0,)), ((), ())), preferre...  14.8 us
    all_to_all x2, starting transfers between devices, to_pixels(): lax.all_to_all(stacked, 'frame', split_axis=3, concat_axis=1, tiled=True)  13.1 us
    all_to_all x2, starting transfers between devices, to_frames(): lax.all_to_all(stacked, 'frame', split_axis=1, concat_axis=3, tiled=True)  11.7 us
  transfers between devices with their start and end apart: 9, of which 4 were waited for; matrix products, arithmetic and copies ran while one was open for 9% of the time, Pallas kernels for 0%

commit v1 on v0

--- a/solution.py
+++ b/solution.py
@@ -1,9 +1,16 @@
+import functools
+
 import jax
 import jax.numpy as jnp
 from jax import lax
+from jax.experimental import pallas as pl
+from jax.experimental.pallas import tpu as pltpu
 from jax.sharding import PartitionSpec as P
 
 HEADS = 5
+MESH = pl.DeviceIdType.MESH
+ORDERS = ("xyz", "yxz", "zxy")
+TILE = (16, 128)
 
 
 EPS = 1e-06
@@ -31,14 +38,6 @@
     return jnp.pad(rimmed, ((0, 0), (0, 0), (1, 1), (0, 0)))
 
 
-def to_pixels(stacked):
-    return lax.all_to_all(stacked, "frame", split_axis=3, concat_axis=1, tiled=True)
-
-
-def to_frames(stacked):
-    return lax.all_to_all(stacked, "frame", split_axis=1, concat_axis=3, tiled=True)
-
-
 def conv_apply(padded, weight, rows, width):
     total = None
     for row_off in range(3):
@@ -138,6 +137,217 @@
         key_part.reshape(shape).astype(jnp.bfloat16),
         value_part.reshape(shape).astype(jnp.bfloat16),
     )
+
+
+def chip_sizes():
+    return {"c": 2, "x": 4, "y": lax.axis_size("row") // 4, "z": lax.axis_size("frame") // 2}
+
+
+def my_place():
+    frame, row = lax.axis_index("frame"), lax.axis_index("row")
+    return {
+        "z": frame // 2,
+        "x": lax.rem(row // 2, 2) * 2 + lax.rem(frame, 2),
+        "y": row // 4,
+        "c": lax.rem(row, 2),
+    }
+
+
+def device_of(place):
+    return (
+        place["z"] * 2 + lax.rem(place["x"], 2),
+        (place["y"] * 2 + place["x"] // 2) * 2 + place["c"],
+    )
+
+
+def along(place, axis, step, sizes):
+    moved = dict(place)
+    moved[axis] = lax.rem(place[axis] + step, sizes[axis])
+    return device_of(moved)
+
+
+def axis_partners(place, sizes):
+    return [
+        along(place, axis, step, sizes) for axis in "cxyz" for step in range(1, sizes[axis])
+    ]
+
+
+def greet(partners):
+    barrier = pltpu.get_barrier_semaphore()
+    for partner in partners:
+        pl.semaphore_signal(barrier, inc=1, device_id=partner, device_id_type=MESH)
+    pl.semaphore_wait(barrier, len(partners))
+
+
+def send(source, target, sems, slot, device):
+    copy = pltpu.make_async_remote_copy(
+        src_ref=source,
+        dst_ref=target,
+        send_sem=sems[0].at[slot],
+        recv_sem=sems[1].at[slot],
+        device_id=device,
+        device_id_type=MESH,
+    )
+    copy.start()
+    return copy
+
+
+def add_up(target, own, received):
+    def body(at, carry):
+        total = own[at].astype(jnp.float32)
+        for part in received:
+            total = total + part[at].astype(jnp.float32)
+        target[at] = total.astype(target.dtype)
+        return carry
+
+    lax.fori_loop(0, target.shape[0], body, 0)
+
+
+class Summer:
+    def __init__(self, order, place, sizes, term, total, scratch, sems):
+        self.order, self.place, self.sizes = order, place, sizes
+        self.term, self.total, self.sems = term, total, sems
+        self.core_in, self.held, self.inbox = scratch[0], scratch[1:4], scratch[4:7]
+        self.slot = 0
+        self.sent = []
+        self.wait = []
+
+    def push(self, source, target, axis, step):
+        device = along(self.place, axis, step, self.sizes)
+        copy = send(source, target, self.sems, self.slot, device)
+        self.slot += 1
+        self.sent.append(copy)
+        self.wait.append(copy)
+
+    def arrive(self):
+        for copy in self.wait:
+            copy.wait_recv()
+        self.wait = []
+
+    def core_start(self):
+        self.push(self.term.at[1 - self.place["c"]], self.core_in, "c", 1)
+
+    def core_end(self):
+        self.arrive()
+        add_up(self.held[0], self.term.at[self.place["c"]], [self.core_in])
+
+    def scatter_start(self, level):
+        axis = self.order[level]
+        for step in range(1, self.sizes[axis]):
+            peer = lax.rem(self.place[axis] + step, self.sizes[axis])
+            self.push(self.held[level].at[peer], self.inbox[level].at[step - 1], axis, step)
+
+    def scatter_end(self, level):
+        self.arrive()
+        axis = self.order[level]
+        received = [self.inbox[level].at[step] for step in range(self.sizes[axis] - 1)]
+        own = self.held[level].at[self.place[axis]]
+        if level < 2:
+            add_up(self.held[level + 1], own, received)
+        else:
+            total = own[...].astype(jnp.float32)
+            for part in received:
+                total = total + part[...].astype(jnp.float32)
+            self.mine(3)[...] = total.astype(self.total.dtype)
+
+    def mine(self, levels):
+        view = self.total.at[self.place["c"]]
+        for level in range(levels):
+            view = view.at[self.place[self.order[level]]]
+        return view
+
+    def gather_start(self, level):
+        axis = self.order[level]
+        for step in range(1, self.sizes[axis]):
+            self.push(self.mine(level + 1), self.mine(level + 1), axis, step)
+
+    def core_back(self):
+        self.push(self.mine(0), self.mine(0), "c", 1)
+
+    def finish(self):
+        for copy in self.sent:
+            copy.wait_send()
+
+
+def summer_scratch(order, sizes, rows):
+    n1, n2, n3 = (sizes[axis] for axis in order)
+    shapes = [
+        (n1, n2, n3, rows, 128),
+        (n1, n2, n3, rows, 128),
+        (n2, n3, rows, 128),
+        (n3, rows, 128),
+        (n1 - 1, n2, n3, rows, 128),
+        (n2 - 1, n3, rows, 128),
+        (n3 - 1, rows, 128),
+    ]
+    copies = 2 * (1 + n1 + n2 + n3 - 3)
+    return [pltpu.VMEM(shape, jnp.bfloat16) for shape in shapes] + [
+        pltpu.SemaphoreType.DMA((copies,)),
+        pltpu.SemaphoreType.DMA((copies,)),
+    ]
+
+
+def sum_kernel(sizes, *refs):
+    count = len(ORDERS)
+    terms, totals, rest = refs[:count], refs[count : 2 * count], refs[2 * count :]
+    place = my_place()
+    greet(axis_partners(place, sizes))
+    parts = []
+    for at, order in enumerate(ORDERS):
+        scratch = rest[9 * at : 9 * at + 9]
+        parts.append(
+            Summer(order, place, sizes, terms[at], totals[at], scratch[:7], scratch[7:])
+        )
+    for part in parts:
+        part.core_start()
+    for part in parts:
+        part.core_end()
+        part.scatter_start(0)
+    for level in range(3):
+        for part in parts:
+            part.scatter_end(level)
+            if level < 2:
+                part.scatter_start(level + 1)
+            else:
+                part.gather_start(2)
+    for level in (1, 0):
+        for part in parts:
+            part.arrive()
+            part.gather_start(level)
+    for part in parts:
+        part.arrive()
+        part.core_back()
+    for part in parts:
+        part.arrive()
+        part.finish()
+
+
+def sum_everywhere(terms):
+    sizes = chip_sizes()
+    shapes = [(2,) + tuple(sizes[axis] for axis in order) + TILE for order in ORDERS]
+    each = 2 * sizes["x"] * sizes["y"] * sizes["z"] * TILE[0] * TILE[1]
+    flat = jnp.concatenate([term.astype(jnp.bfloat16).reshape(-1) for term in terms])
+    flat = jnp.pad(flat, (0, each * len(ORDERS) - flat.size))
+    cut = [flat[at * each : (at + 1) * each].reshape(shape) for at, shape in enumerate(shapes)]
+    scratch = []
+    for order in ORDERS:
+        scratch += summer_scratch(order, sizes, TILE[0])
+    totals = pl.pallas_call(
+        functools.partial(sum_kernel, sizes),
+        out_shape=[jax.ShapeDtypeStruct(shape, jnp.bfloat16) for shape in shapes],
+        in_specs=[pl.BlockSpec(memory_space=pltpu.VMEM)] * len(ORDERS),
+        out_specs=[pl.BlockSpec(memory_space=pltpu.VMEM)] * len(ORDERS),
+        scratch_shapes=scratch,
+        compiler_params=pltpu.CompilerParams(
+            collective_id=0, has_side_effects=True, vmem_limit_bytes=48 << 20
+        ),
+    )(*cut)
+    back = jnp.concatenate([total.reshape(-1) for total in totals])
+    out, start = [], 0
+    for term in terms:
+        out.append(back[start : start + term.size].reshape(term.shape).astype(jnp.float32))
+        start += term.size
+    return out
 
 
 def project(normed, weight):
@@ -157,32 +367,36 @@
     resid_f = resid.astype(jnp.float32)
     inv_rms = lax.rsqrt(jnp.mean(resid_f * resid_f, axis=-1, keepdims=True) + EPS)
     normed = (resid_f * inv_rms * norm_gain).astype(jnp.bfloat16)
-    local_qkv = jnp.stack(
-        [project(normed, query_weight), project(normed, key_weight), project(normed, value_weight)]
-    )
-    moved = to_pixels(local_qkv)
-    queries, key_rows, value_rows = (moved[0], moved[1], moved[2])
+    side = lax.axis_size("frame")
+
+    def exchange(field):
+        cut = field.reshape(side, -1, chan)
+        return lax.all_to_all(cut, "frame", split_axis=0, concat_axis=0, tiled=True)
+
+    out_grad_pix = exchange(out_grad)
+    normed_pix = exchange(normed)[:, :, None]
+    queries = project(normed_pix, query_weight)
+    key_rows = project(normed_pix, key_weight)
+    value_rows = project(normed_pix, value_weight)
     probs, probs_b, mixed_pix = attend(queries, key_rows, value_rows)
-    mixed = to_frames(mixed_pix[None])[0]
+    mixed = exchange(mixed_pix).reshape(frames, rows, width, chan)
     block_out = (resid_f + jnp.dot(mixed, out_weight, preferred_element_type=jnp.float32)).astype(
         jnp.bfloat16
     )
     grad_out_w = outer_sum(mixed, out_grad)
-    mixed_grad = back_dot(out_grad, out_weight).astype(jnp.bfloat16)
-    mixed_grad_pix = to_pixels(mixed_grad[None])[0]
+    mixed_grad_pix = back_dot(out_grad_pix, out_weight).astype(jnp.bfloat16)[:, :, None]
     query_part, key_part, value_part = attend_back(
         probs, probs_b, queries, key_rows, value_rows, mixed_grad_pix
     )
-    returned = to_frames(jnp.stack([query_part, key_part, value_part]))
-    query_back, key_back, value_back = (returned[0], returned[1], returned[2])
-    grad_query = outer_sum(normed, query_back)
-    grad_key = outer_sum(normed, key_back)
-    grad_value = outer_sum(normed, value_back)
-    normed_grad = (
-        back_dot(query_back, query_weight)
-        + back_dot(key_back, key_weight)
-        + back_dot(value_back, value_weight)
+    grad_query = outer_sum(normed_pix, query_part)
+    grad_key = outer_sum(normed_pix, key_part)
+    grad_value = outer_sum(normed_pix, value_part)
+    normed_grad_pix = (
+        back_dot(query_part, query_weight)
+        + back_dot(key_part, key_weight)
+        + back_dot(value_part, value_weight)
     ).astype(jnp.bfloat16)
+    normed_grad = exchange(normed_grad_pix).reshape(frames, rows, width, chan)
     normed_gf = normed_grad.astype(jnp.float32)
     grad_gain = jnp.sum((normed_gf * resid_f * inv_rms).reshape(-1, chan), axis=0)
     tangent = normed_gf * norm_gain
@@ -196,8 +410,8 @@
     latents_grad = (
         resid_grad.astype(jnp.float32) + act_grad * sigma * (1.0 + latent_f * (1.0 - sigma))
     ).astype(jnp.bfloat16)
-    summed = lax.psum(
-        (grad_conv, grad_query, grad_key, grad_value, grad_out_w, grad_gain), ("frame", "row")
+    summed = sum_everywhere(
+        [grad_conv, grad_query, grad_key, grad_value, grad_out_w, grad_gain]
     )
     factor = cells_all ** (-0.5)
     return (

time: 553 us -> 229 us (0.41)
  waiting for transfers between devices: 323 us -> 29.9 us
  blocking collectives: 75 us -> 0 us
  Pallas kernels: 0 us -> 49.8 us
  between operations: 14.6 us -> 1.3 us
  local copies, waits for them, and re-layouts: 37.1 us -> 47.4 us
  matrix products: 51.6 us -> 57.6 us
    psum x1 -> x0, waiting for transfers between devices: 267 us -> none  [on_device(): lax.psum((grad_conv, grad_query, grad_key, grad_value, grad_out_w, grad_g...]
    psum x1 -> x0, blocking collectives: 75 us -> none  [on_device(): lax.psum((grad_conv, grad_query, grad_key, grad_value, grad_out_w, grad_g...]
    pallas_call x0 -> x1, Pallas kernels: none -> 49.8 us  [sum_everywhere(): pl.pallas_call(functools.partial(sum_kernel, sizes), out_shape=[jax.Shape...]
    all_to_all x4, waiting for transfers between devices: 55.3 us -> 29.9 us  [exchange(): return lax.all_to_all(cut, 'frame', split_axis=0, concat_axis=0, tiled=True)]
    mul x0 -> x5, local copies, waits for them, and re-layouts: none -> 9.26 us  [the longest x1 5.4 us: on_device(): summed[0] * factor]
    another operation x6 -> x4, local copies, waits for them, and re-layouts: 11.6 us -> 7.51 us  [the longest x4 8.5 us: split_heads(): return field.reshape(frames, rows, width, HEADS, chan // HEADS)]
  transfers between devices with their start and end apart: 9 -> 8, of which waited for: 4 -> 4; matrix products, arithmetic and copies ran while one was open for 9% -> 24% of each run, Pallas kernels for 0% -> 22%
where the time goes in v1:
time: 229 us; the launch traced here: 228 us
  matrix products  57.6 us (25%)
  Pallas kernels  49.8 us (22%)
  local copies, waits for them, and re-layouts  47.4 us (21%)
  starting transfers between devices  33.6 us (15%)
  waiting for transfers between devices  29.9 us (13%)
  other arithmetic  7.93 us (3%)
    pallas_call x1, Pallas kernels, sum_everywhere(): pl.pallas_call(functools.partial(sum_kernel, sizes), out_shape=[jax.Shape...  49.8 us
    all_to_all x4, waiting for transfers between devices, exchange(): return lax.all_to_all(cut, 'frame', split_axis=0, concat_axis=0, tiled=True)  29.9 us
    all_to_all x4, starting transfers between devices, exchange(): return lax.all_to_all(cut, 'frame', split_axis=0, concat_axis=0, tiled=True)  20.7 us
    dot_general x13, matrix products, outer_sum(): lax.dot_general(left_flat, right_flat, (((0,), (0,)), ((), ())), preferre...  15.1 us
    dot_general x13, matrix products, back_dot(): lax.dot_general(field, weight, (((field.ndim - 1,), (1,)), ((), ())), pre...  11.5 us
    ppermute x2, starting transfers between devices, padded_2(): lax.ppermute(tail, axis, [(i, (i + 1) % count) for i in range(ends)])  7.95 us
    another operation x4, local copies, waits for them, and re-layouts  7.51 us
    unnamed x69, local copies, waits for them, and re-layouts  5.74 us
  transfers between devices with their start and end apart: 8, of which 4 were waited for; matrix products, arithmetic and copies ran while one was open for 24% of the time, Pallas kernels for 22%

profile of v1, /device:TPU:1, one launch (start us, length us, event | category | flops | bytes accessed | tf_op | source)
XLA Modules:
  0.0 227.6 jit_solution(11453493778694144414)
XLA Ops:
  2.0 6.0 %collective-permute-start = (bf16[1,1,128,320]{2,3,1,0:T(8,128)(2,1)S(1)}, bf16[1,1,128,320]{2,3,1,0:T(8,128)(2,1)S(1)}, u32[]{:S(2)}, u32[]{:S(2)}) collective-permute-start(bf16[1,1,128,320]{2,3,1,0:T(8,128)(2,1)S(1)} %get-tuple-element.24), channel_id=1, source_target_pairs={{0,1},{1,2},{2,3},{3,4},{4,5},{5,6},{6,7},{7,8},{8,9},{9,10},{10,1... | collective-permute-start | bytes 245768 | tf_op jit(solution)/shard_map/ppermute | solution.py:27
  11.9 8.4 %all-to-all-start.2 = ((bf16[16,32,320]{2,1,0:T(8,128)(2,1)}), bf16[16,32,320]{2,1,0:T(8,128)(2,1)}, u32[]{:S(2)}, u32[]{:S(2)}) async-start(bf16[16,32,320]{2,1,0:T(8,128)(2,1)} %bitcast.37), calls=%async_computation.2 | async-start | bytes 786432 | tf_op jit(solution)/shard_map/all_to_all | solution.py:374
  28.5 4.9 %all-to-all-done.2 = bf16[16,32,320]{2,1,0:T(8,128)(2,1)} async-done(((bf16[16,32,320]{2,1,0:T(8,128)(2,1)}), bf16[16,32,320]{2,1,0:T(8,128)(2,1)}, u32[]{:S(2)}, u32[]{:S(2)}) %all-to-all-start.2) | async-done | bytes 327712 | tf_op jit(solution)/shard_map/all_to_all | solution.py:374
  33.4 3.6 %all-to-all-start = ((bf16[16,32,320]{2,1,0:T(8,128)(2,1)}), bf16[16,32,320]{2,1,0:T(8,128)(2,1)S(1)}, u32[]{:S(2)}, u32[]{:S(2)}) async-start(bf16[16,32,320]{2,1,0:T(8,128)(2,1)} %bitcast.28), calls=%async_computation | async-start | bytes 786432 | tf_op jit(solution)/shard_map/all_to_all | solution.py:374
  40.7 11.4 %all-to-all-done = bf16[16,32,320]{2,1,0:T(8,128)(2,1)S(1)} async-done(((bf16[16,32,320]{2,1,0:T(8,128)(2,1)}), bf16[16,32,320]{2,1,0:T(8,128)(2,1)S(1)}, u32[]{:S(2)}, u32[]{:S(2)}) %all-to-all-start) | async-done | bytes 327712 | tf_op jit(solution)/shard_map/all_to_all | solution.py:374
  55.9 2.3 %reshape.423 = bf16[16,32,5,64]{3,2,1,0:T(8,128)(2,1)} reshape(bf16[16,32,320]{2,1,0:T(8,128)(2,1)} %convolution_convert_fusion.6) | data formatting | bytes 655360 | tf_op jit(solution)/shard_map/reshape.26
  58.2 2.1 convolution_convert_fusion.5
  60.3 2.3 %reshape.424 = bf16[16,32,5,64]{3,2,1,0:T(8,128)(2,1)} reshape(bf16[16,32,320]{2,1,0:T(8,128)(2,1)} %convolution_convert_fusion.5) | data formatting | bytes 655360 | tf_op jit(solution)/shard_map/reshape.27
  62.6 3.8 %fusion.72 = f32[32,5,16,16]{2,3,1,0:T(8,128)} fusion(bf16[16,32,5,64]{3,2,1,0:T(8,128)(2,1)} %reshape.424, bf16[16,32,5,64]{3,2,1,0:T(8,128)(2,1)} %reshape.423), kind=kOutput, calls=%fused_computation.128 | convolution fusion | flops 5327375 | bytes 819200 | tf_op jit(solution)/shard_map/div | solution.py:105
  66.3 3.2 %fusion.10 = bf16[16,32,1,5,64]{4,0,3,1,2:T(8,128)(2,1)} fusion(bf16[16,32,5,64]{3,2,1,0:T(8,128)(2,1)} %reshape.427, f32[32,5,16,16]{2,3,1,0:T(8,128)} %fusion.72), kind=kOutput, calls=%fused_computation.28 | convolution fusion | flops 5447680 | bytes 819200 | tf_op jit(solution)/shard_map/rwhfg,frwhd->grwhd/dot_general | solution.py:131
  69.6 2.1 fusion.76
  71.6 4.7 %fusion.8 = bf16[16,32,1,5,64]{4,0,3,1,2:T(8,128)(2,1)} fusion(f32[32,5,16,16]{2,3,1,0:T(8,128)} %fusion.72, f32[32,5,16,16]{2,3,1,0:T(8,128)} %fusion.76, bf16[16,32,5,64]{3,2,1,0:T(8,128)(2,1)} %reshape.424), kind=kOutput, calls=%fused_computation.26 | convolution fusion | flops 5614095 | bytes 983040 | tf_op jit(solution)/shard_map/rwhfg,grwhd->frwhd/dot_general | solution.py:125
  76.3 4.3 %fusion.9 = bf16[16,32,1,5,64]{4,0,3,1,2:T(8,128)(2,1)} fusion(f32[32,5,16,16]{2,3,1,0:T(8,128)} %fusion.72, f32[32,5,16,16]{2,3,1,0:T(8,128)} %fusion.76, bf16[16,32,5,64]{3,2,1,0:T(8,128)(2,1)S(1)} %copy-done.18), kind=kOutput, calls=%fused_computation.27 | convolution fusion | flops 5614095 | bytes 983040 | tf_op jit(solution)/shard_map/rwhfg,frwhd->grwhd/dot_general | solution.py:128
  99.0 4.6 %all-to-all-start.3 = ((bf16[16,32,320]{2,1,0:T(8,128)(2,1)}), bf16[16,32,320]{2,1,0:T(8,128)(2,1)}, u32[]{:S(2)}, u32[]{:S(2)}) async-start(bf16[16,32,320]{2,1,0:T(8,128)(2,1)} %fusion.18), calls=%async_computation.3 | async-start | bytes 786432 | tf_op jit(solution)/shard_map/all_to_all | solution.py:374
  111.2 7.4 %all-to-all-done.3 = bf16[16,32,320]{2,1,0:T(8,128)(2,1)} async-done(((bf16[16,32,320]{2,1,0:T(8,128)(2,1)}), bf16[16,32,320]{2,1,0:T(8,128)(2,1)}, u32[]{:S(2)}, u32[]{:S(2)}) %all-to-all-start.3) | async-done | bytes 327712 | tf_op jit(solution)/shard_map/all_to_all | solution.py:374
  118.6 4.2 %all-to-all-start.1 = ((bf16[16,32,320]{2,1,0:T(8,128)(2,1)}), bf16[16,32,320]{2,1,0:T(8,128)(2,1)}, u32[]{:S(2)}, u32[]{:S(2)}) async-start(bf16[16,32,320]{2,1,0:T(8,128)(2,1)} %convert_element_type.217), calls=%async_computation.1 | async-start | bytes 786432 | tf_op jit(solution)/shard_map/all_to_all | solution.py:374
  127.1 3.0 %collective-permute-start.3 = (bf16[1,1,128,320]{2,3,1,0:T(8,128)(2,1)}, bf16[1,1,128,320]{2,3,1,0:T(8,128)(2,1)}, u32[]{:S(2)}, u32[]{:S(2)}) collective-permute-start(bf16[1,1,128,320]{2,3,1,0:T(8,128)(2,1)} %get-tuple-element.23), channel_id=1, source_target_pairs={{1,0},{2,1},{3,2},{4,3},{5,4},{6,5},{7,6},{8,7},{9,8},{10,9},{11,1... | collective-permute-start | bytes 245768 | tf_op jit(solution)/shard_map/ppermute | solution.py:29
  131.2 6.3 %all-to-all-done.1 = bf16[16,32,320]{2,1,0:T(8,128)(2,1)} async-done(((bf16[16,32,320]{2,1,0:T(8,128)(2,1)}), bf16[16,32,320]{2,1,0:T(8,128)(2,1)}, u32[]{:S(2)}, u32[]{:S(2)}) %all-to-all-start.1) | async-done | bytes 327712 | tf_op jit(solution)/shard_map/all_to_all | solution.py:374
  140.0 2.1 fusion.23
  150.6 4.3 %convert_element_type.240 = bf16[921600]{0:T(1024)(128)(2,1)S(1)} reshape(bf16[9,320,320]{2,1,0:T(8,128)(2,1)} %fusion.34) | data formatting | bytes 3686400 | tf_op jit(solution)/shard_map/convert_element_type | solution.py:329
  157.9 49.8 %shard_map.143 = (bf16[2,4,4,8,16,128]{5,4,3,2,1,0:T(8,128)(2,1)S(1)}, bf16[2,4,4,8,16,128]{5,4,3,2,1,0:T(8,128)(2,1)S(1)}, bf16[2,8,4,4,16,128]{5,4,3,2,1,0:T(8,128)(2,1)S(1)}) custom-call(bf16[2,4,4,8,16,128]{5,4,3,2,1,0:T(8,128)(2,1)S(1)} %bitcast.395, bf16[2,4,4,8,16,128]{5,4,3,2,1,0:T(8,128)(2,1)S(1)} %bitcast.394, bf16[2,8,4,4,16,128]{5,4,3,2,1,0:T(8,128)(2,1)} %bitcast.402), custom_call_target="tpu_custom_call" | custom-call | tf_op jit(solution)/shard_map/pallas_call | solution.py:335
  207.8 2.1 convert_multiply_fusion
  214.3 5.4 %mul.170 = f32[3,3,320,320]{3,2,1,0:T(8,128)} reshape(f32[921600]{0:T(1024)} %convert_multiply_fusion) | data formatting | bytes 7372800 | tf_op jit(solution)/shard_map/mul | solution.py:420
  225.4 2.1 fusion.22
  (150 shorter events, 76.1 us)
Async XLA Ops:
  0.6 54.1 %copy-start = (bf16[320,320]{1,0:T(8,128)(2,1)S(1)}, bf16[320,320]{1,0:T(8,128)(2,1)}, u32[]{:S(2)}) copy-start(bf16[320,320]{1,0:T(8,128)(2,1)} %param.10) | copy-start | bytes 614404
  0.6 21.8 %copy-start.2 = (bf16[3,3,320,320]{3,2,1,0:T(8,128)(2,1)S(1)}, bf16[3,3,320,320]{3,2,1,0:T(8,128)(2,1)}, u32[]{:S(2)}) copy-start(bf16[3,3,320,320]{3,2,1,0:T(8,128)(2,1)} %param.9) | copy-start | bytes 5529604
  2.0 18.3 %copy-start.4 = (bf16[1,4,128,320]{2,3,1,0:T(8,128)(2,1)}, bf16[1,4,128,320]{2,3,1,0:T(8,128)(2,1)S(1)}, u32[]{:S(2)}) copy-start(bf16[1,4,128,320]{2,3,1,0:T(8,128)(2,1)S(1)} %fusion.59) | copy-start | bytes 983044
  2.0 18.2 %collective-permute-start = (bf16[1,1,128,320]{2,3,1,0:T(8,128)(2,1)S(1)}, bf16[1,1,128,320]{2,3,1,0:T(8,128)(2,1)S(1)}, u32[]{:S(2)}, u32[]{:S(2)}) collective-permute-start(bf16[1,1,128,320]{2,3,1,0:T(8,128)(2,1)S(1)} %get-tuple-element.24), channel_id=1, source_target_pairs={{0,1},{1,2},{2,3},{3,4},{4,5},{5,6},{6,7},{7,8},{8,9},{9,10},{10,1... | collective-permute-start | bytes 245768 | tf_op jit(solution)/shard_map/ppermute | solution.py:27
  8.1 12.8 %collective-permute-start.1 = (bf16[1,1,128,320]{2,3,1,0:T(8,128)(2,1)S(1)}, bf16[1,1,128,320]{2,3,1,0:T(8,128)(2,1)S(1)}, u32[]{:S(2)}, u32[]{:S(2)}) collective-permute-start(bf16[1,1,128,320]{2,3,1,0:T(8,128)(2,1)S(1)} %get-tuple-element.25), channel_id=1, source_target_pairs={{1,0},{2,1},{3,2},{4,3},{5,4},{6,5},{7,6},{8,7},{9,8},{10,9},{11,1... | collective-permute-start | bytes 245768 | tf_op jit(solution)/shard_map/ppermute | solution.py:29
  11.9 21.5 %all-to-all-start.2 = ((bf16[16,32,320]{2,1,0:T(8,128)(2,1)}), bf16[16,32,320]{2,1,0:T(8,128)(2,1)}, u32[]{:S(2)}, u32[]{:S(2)}) async-start(bf16[16,32,320]{2,1,0:T(8,128)(2,1)} %bitcast.37), calls=%async_computation.2 | async-start | bytes 786432 | tf_op jit(solution)/shard_map/all_to_all | solution.py:374
  20.9 5.0 %copy-start.25 = (bf16[1,1,128,320]{2,3,1,0:T(8,128)(2,1)}, bf16[1,1,128,320]{2,3,1,0:T(8,128)(2,1)S(1)}, u32[]{:S(2)}) copy-start(bf16[1,1,128,320]{2,3,1,0:T(8,128)(2,1)S(1)} %collective-permute-done.1) | copy-start | bytes 245764
  25.9 11.0 %copy-start.12 = (bf16[1,4,128,320]{2,3,1,0:T(8,128)(2,1)S(1)}, bf16[1,4,128,320]{2,3,1,0:T(8,128)(2,1)}, u32[]{:S(2)}) copy-start(bf16[1,4,128,320]{2,3,1,0:T(8,128)(2,1)} %param.15) | copy-start | bytes 983044
  25.9 12.0 %copy-start.21 = (bf16[320,320]{1,0:T(8,128)(2,1)S(1)}, bf16[320,320]{1,0:T(8,128)(2,1)}, u32[]{:S(2)}) copy-start(bf16[320,320]{1,0:T(8,128)(2,1)} %param.13) | copy-start | bytes 614404
  27.5 24.5 %copy-start.19 = (bf16[320,320]{1,0:T(8,128)(2,1)S(1)}, bf16[320,320]{1,0:T(8,128)(2,1)}, u32[]{:S(2)}) copy-start(bf16[320,320]{1,0:T(8,128)(2,1)} %param.12) | copy-start | bytes 614404
  33.4 18.7 %all-to-all-start = ((bf16[16,32,320]{2,1,0:T(8,128)(2,1)}), bf16[16,32,320]{2,1,0:T(8,128)(2,1)S(1)}, u32[]{:S(2)}, u32[]{:S(2)}) async-start(bf16[16,32,320]{2,1,0:T(8,128)(2,1)} %bitcast.28), calls=%async_computation | async-start | bytes 786432 | tf_op jit(solution)/shard_map/all_to_all | solution.py:374
  54.7 14.8 %copy-start.9 = (bf16[16,32,5,64]{3,2,1,0:T(8,128)(2,1)}, bf16[16,32,5,64]{3,2,1,0:T(8,128)(2,1)S(1)}, u32[]{:S(2)}) copy-start(bf16[16,32,5,64]{3,2,1,0:T(8,128)(2,1)S(1)} %reshape.422) | copy-start | bytes 983044
  71.6 4.7 %copy-start.18 = (bf16[16,32,5,64]{3,2,1,0:T(8,128)(2,1)S(1)}, bf16[16,32,5,64]{3,2,1,0:T(8,128)(2,1)}, u32[]{:S(2)}) copy-start(bf16[16,32,5,64]{3,2,1,0:T(8,128)(2,1)} %reshape.423) | copy-start | bytes 983044
  99.0 8.6 %copy-start.10 = (bf16[16,32,5,64]{3,2,1,0:T(8,128)(2,1)S(1)}, bf16[16,32,5,64]{3,2,1,0:T(8,128)(2,1)}, u32[]{:S(2)}) copy-start(bf16[16,32,5,64]{3,2,1,0:T(8,128)(2,1)} %copy-done.9) | copy-start | bytes 983044
  99.0 19.5 %all-to-all-start.3 = ((bf16[16,32,320]{2,1,0:T(8,128)(2,1)}), bf16[16,32,320]{2,1,0:T(8,128)(2,1)}, u32[]{:S(2)}, u32[]{:S(2)}) async-start(bf16[16,32,320]{2,1,0:T(8,128)(2,1)} %fusion.18), calls=%async_computation.3 | async-start | bytes 786432 | tf_op jit(solution)/shard_map/all_to_all | solution.py:374
  118.6 18.9 %all-to-all-start.1 = ((bf16[16,32,320]{2,1,0:T(8,128)(2,1)}), bf16[16,32,320]{2,1,0:T(8,128)(2,1)}, u32[]{:S(2)}, u32[]{:S(2)}) async-start(bf16[16,32,320]{2,1,0:T(8,128)(2,1)} %convert_element_type.217), calls=%async_computation.1 | async-start | bytes 786432 | tf_op jit(solution)/shard_map/all_to_all | solution.py:374
  124.2 15.7 %copy-start.22 = (bf16[320,320]{1,0:T(8,128)(2,1)S(1)}, bf16[320,320]{1,0:T(8,128)(2,1)}, u32[]{:S(2)}) copy-start(bf16[320,320]{1,0:T(8,128)(2,1)} %param.13) | copy-start | bytes 614404
  124.5 25.1 %copy-start.7 = (bf16[1,4,128,320]{2,3,1,0:T(8,128)(2,1)}, bf16[1,4,128,320]{2,3,1,0:T(8,128)(2,1)S(1)}, u32[]{:S(2)}) copy-start(bf16[1,4,128,320]{2,3,1,0:T(8,128)(2,1)S(1)} %fusion.67) | copy-start | bytes 983044
  124.5 17.6 %copy-start.6 = (bf16[1,4,128,320]{2,3,1,0:T(8,128)(2,1)S(1)}, bf16[1,4,128,320]{2,3,1,0:T(8,128)(2,1)}, u32[]{:S(2)}) copy-start(bf16[1,4,128,320]{2,3,1,0:T(8,128)(2,1)} %copy-done.4) | copy-start | bytes 983044
  124.5 17.6 %copy-start.29 = (bf16[1,1,128,320]{2,3,1,0:T(8,128)(2,1)S(1)}, bf16[1,1,128,320]{2,3,1,0:T(8,128)(2,1)}, u32[]{:S(2)}) copy-start(bf16[1,1,128,320]{2,3,1,0:T(8,128)(2,1)} %copy-done.27) | copy-start | bytes 245764
  125.2 94.6 %collective-permute-start.2 = (bf16[1,1,128,320]{2,3,1,0:T(8,128)(2,1)}, bf16[1,1,128,320]{2,3,1,0:T(8,128)(2,1)}, u32[]{:S(2)}, u32[]{:S(2)}) collective-permute-start(bf16[1,1,128,320]{2,3,1,0:T(8,128)(2,1)} %get-tuple-element.22), channel_id=1, source_target_pairs={{0,1},{1,2},{2,3},{3,4},{4,5},{5,6},{6,7},{7,8},{8,9},{9,10},{10,1... | collective-permute-start | bytes 245768 | tf_op jit(solution)/shard_map/ppermute | solution.py:27
  127.1 92.7 %collective-permute-start.3 = (bf16[1,1,128,320]{2,3,1,0:T(8,128)(2,1)}, bf16[1,1,128,320]{2,3,1,0:T(8,128)(2,1)}, u32[]{:S(2)}, u32[]{:S(2)}) collective-permute-start(bf16[1,1,128,320]{2,3,1,0:T(8,128)(2,1)} %get-tuple-element.23), channel_id=1, source_target_pairs={{1,0},{2,1},{3,2},{4,3},{5,4},{6,5},{7,6},{8,7},{9,8},{10,9},{11,1... | collective-permute-start | bytes 245768 | tf_op jit(solution)/shard_map/ppermute | solution.py:29
  140.0 5.3 %copy-start.16 = (bf16[1,4,128,320]{2,3,1,0:T(8,128)(2,1)S(1)}, bf16[1,4,128,320]{2,3,1,0:T(8,128)(2,1)}, u32[]{:S(2)}) copy-start(bf16[1,4,128,320]{2,3,1,0:T(8,128)(2,1)} %param.8) | copy-start | bytes 983044
  214.3 7.0 %copy-start.3 = (bf16[3,3,320,320]{3,2,1,0:T(8,128)(2,1)S(1)}, bf16[3,3,320,320]{3,2,1,0:T(8,128)(2,1)}, u32[]{:S(2)}) copy-start(bf16[3,3,320,320]{3,2,1,0:T(8,128)(2,1)} %param.9) | copy-start | bytes 5529604
  (15 other events, 30.5 us)

commit v2 on v0

v2 whole, which is shorter than its diff:
```python
import functools

import jax
import jax.numpy as jnp
from jax import lax
from jax.experimental import pallas as pl
from jax.experimental.pallas import tpu as pltpu
from jax.sharding import PartitionSpec as P

EPS = 1e-06
MESH = pl.DeviceIdType.MESH
CHAN = 320
WIDE = 384
COLS = 128
ROWS = 4
HALF = 256
CONV_TILES = 512
SMALL_TILES = 256
PART = 256
MATRIX_TILES = 50
GAIN_TILE = 450
BLOCK = 16
F32 = jnp.float32
BF16 = jnp.bfloat16


def chip_sizes():
    return {"c": 2, "x": 4, "y": lax.axis_size("row") // 4, "z": lax.axis_size("frame") // 2}


def my_place():
    frame, row = lax.axis_index("frame"), lax.axis_index("row")
    return {
        "z": frame // 2,
        "x": lax.rem(row // 2, 2) * 2 + lax.rem(frame, 2),
        "y": row // 4,
        "c": lax.rem(row, 2),
    }


def device_of(place):
    return (
        place["z"] * 2 + lax.rem(place["x"], 2),
        (place["y"] * 2 + place["x"] // 2) * 2 + place["c"],
    )


def along(place, axis, step, sizes):
    moved = dict(place)
    moved[axis] = lax.rem(place[axis] + step, sizes[axis])
    return device_of(moved)


def remote(source, target, send_sem, recv_sem, device):
    copy = pltpu.make_async_remote_copy(
        src_ref=source,
        dst_ref=target,
        send_sem=send_sem,
        recv_sem=recv_sem,
        device_id=device,
        device_id_type=MESH,
    )
    copy.start()
    return copy


def dot(left, right):
    return jnp.dot(left, right, preferred_element_type=F32)


def dot_nt(left, right):
    return lax.dot_general(left, right, (((1,), (1,)), ((), ())), preferred_element_type=F32)


def dot_tn(left, right):
    return lax.dot_general(left, right, (((0,), (0,)), ((), ())), preferred_element_type=F32)


def add_up(target, start, own, own_start, received):
    count = own.shape[0] if own_start is None else received[0].shape[0]
    step = min(count, BLOCK)
    own_start = 0 if own_start is None else own_start

    def body(at, carry):
        at = at * step
        total = own[pl.ds(own_start + at, step)].astype(F32)
        for part in received:
            total = total + part[pl.ds(at, step)].astype(F32)
        target[pl.ds(start + at, step)] = total.astype(BF16)
        return carry

    lax.fori_loop(0, count // step, body, 0)


class Summer:
    def __init__(self, order, place, sizes, term, total, base, scratch):
        self.order, self.place, self.sizes = order, place, sizes
        self.term, self.total, self.base = term, total, base
        self.core_in, self.held, self.inbox = scratch[0], scratch[1:4], scratch[4:7]
        self.send_sems, self.recv_sems = scratch[7], scratch[8]
        self.spans = [PART // 2]
        for axis in order:
            self.spans.append(self.spans[-1] // sizes[axis])
        self.slot = 0
        self.sent = []
        self.wait = []

    def push(self, source, target, axis, step):
        device = along(self.place, axis, step, self.sizes)
        copy = remote(
            source, target, self.send_sems.at[self.slot], self.recv_sems.at[self.slot], device
        )
        self.slot += 1
        self.sent.append(copy)
        self.wait.append(copy)

    def arrive(self):
        for copy in self.wait:
            copy.wait_recv()
        self.wait = []

    def core_start(self):
        other = self.base + (1 - self.place["c"]) * self.spans[0]
        self.push(self.term.at[pl.ds(other, self.spans[0])], self.core_in, "c", 1)

    def core_end(self):
        self.arrive()
        mine = self.base + self.place["c"] * self.spans[0]
        add_up(self.held[0], 0, self.term, mine, [self.core_in])

    def scatter_start(self, level):
        axis, span = self.order[level], self.spans[level + 1]
        for step in range(1, self.sizes[axis]):
            peer = lax.rem(self.place[axis] + step, self.sizes[axis])
            self.push(
                self.held[level].at[pl.ds(peer * span, span)],
                self.inbox[level].at[step - 1],
                axis,
                step,
            )

    def scatter_end(self, level):
        self.arrive()
        axis, span = self.order[level], self.spans[level + 1]
        received = [self.inbox[level].at[step] for step in range(self.sizes[axis] - 1)]
        mine = self.place[axis] * span
        if level < 2:
            add_up(self.held[level + 1], 0, self.held[level], mine, received)
        else:
            add_up(self.total, self.start_of(3), self.held[level], mine, received)

    def start_of(self, levels):
        start = self.base + self.place["c"] * self.spans[0]
        for level in range(levels):
            start = start + self.place[self.order[level]] * self.spans[level + 1]
        return start

    def gather_start(self, level):
        axis = self.order[level]
        mine = self.total.at[pl.ds(self.start_of(level + 1), self.spans[level + 1])]
        for step in range(1, self.sizes[axis]):
            self.push(mine, mine, axis, step)

    def core_back(self):
        mine = self.total.at[pl.ds(self.start_of(0), self.spans[0])]
        self.push(mine, mine, "c", 1)

    def finish(self):
        for copy in self.sent:
            copy.wait_send()


def summer_scratch(order, sizes):
    spans = [PART // 2]
    for axis in order:
        spans.append(spans[-1] // sizes[axis])
    shapes = [(spans[0], 16, 128)]
    shapes += [(span, 16, 128) for span in spans[:3]]
    shapes += [(sizes[axis] - 1, span, 16, 128) for axis, span in zip(order, spans[1:])]
    copies = 2 * (1 + sum(sizes[axis] - 1 for axis in order))
    return [pltpu.VMEM(shape, BF16) for shape in shapes] + [
        pltpu.SemaphoreType.DMA((copies,)),
        pltpu.SemaphoreType.DMA((copies,)),
    ]


def pack(matrix, tiles, base):
    held = matrix.astype(BF16)
    for block in range(2):
        cut = held[:, block * 128 : block * 128 + 128]
        tiles[pl.ds(base + 20 * block, 20)] = cut.reshape(20, 16, 128)
    low, high = held[:160, 256:], held[160:, 256:]
    tail = jnp.concatenate([low, high], axis=1)
    tiles[pl.ds(base + 40, 10)] = tail.reshape(10, 16, 128)


def unpack(tiles, base, target, row):
    for block in range(2):
        cut = tiles[pl.ds(base + 20 * block, 20)].reshape(320, 128)
        target[pl.ds(row, 320), block * 128 : block * 128 + 128] = cut
    tail = tiles[pl.ds(base + 40, 10)].reshape(160, 128)
    target[pl.ds(row, 160), 256:] = tail[:, :64]
    target[pl.ds(row + 160, 160), 256:] = tail[:, 64:]


def shifts(cells):
    column = lax.broadcasted_iota(jnp.int32, cells.shape, 0)
    left = jnp.where(column == 0, 0.0, pltpu.roll(cells, 1, 0))
    right = jnp.where(column == COLS - 1, 0.0, pltpu.roll(cells, COLS - 1, 0))
    return [left, cells, right]


class Swap:
    def __init__(self, source, target, send_sems, recv_sems, peers, me):
        self.source, self.target, self.peers, self.me = source, target, peers, me
        self.send_sems, self.recv_sems = send_sems, recv_sems

    def start(self, half):
        for frame, device in self.peers:
            remote(
                self.source.at[half, frame],
                self.target.at[half, self.me],
                self.send_sems.at[half],
                self.recv_sems.at[half],
                device,
            )
        self.target[half, self.me] = self.source[half, self.me]

    def wait(self, half):
        span = self.target.at[half, pl.ds(0, len(self.peers))]
        pltpu.make_async_copy(span, span, self.recv_sems.at[half]).wait()

    def finish(self):
        for half in range(2):
            span = self.source.at[half, pl.ds(0, len(self.peers))]
            pltpu.make_async_copy(span, span, self.send_sems.at[half]).wait()


def norm_of(resid):
    return lax.rsqrt(jnp.mean(resid * resid, axis=-1, keepdims=True) + EPS)


def cell_start(half, at):
    if half == 0:
        return COLS + at * 64
    return jnp.where(at < 2, at * 64, HALF + at * 64)


def attention(q_s, k_s, v_s, d_s, bias, mixed_s, qp_s, kp_s, vp_s):
    lane = lax.broadcasted_iota(jnp.int32, (1, 128), 1)
    low = lane < 64
    masks = [jnp.where(low, 1.0, 0.0).astype(BF16), jnp.where(low, 0.0, 1.0).astype(BF16)]

    def tile(at, carry):
        span = pl.ds(pl.multiple_of(at * 128, 128), 128)
        queries, keys, values, grads = q_s[:, span], k_s[:, span], v_s[:, span], d_s[:, span]
        found = []
        for mask in masks:
            scores = dot_nt(queries * mask, keys) * 0.125 + bias[...]
            expo = jnp.exp(scores)
            probs = expo * (1.0 / jnp.sum(expo, axis=-1, keepdims=True))
            probs_b = probs.astype(BF16)
            mixed = dot(probs_b, values)
            prob_grad = dot_nt(grads * mask, values)
            inner = jnp.sum(probs * prob_grad, axis=-1, keepdims=True)
            score_b = (probs * (prob_grad - inner) * 0.125).astype(BF16)
            found.append(
                (mixed, dot(score_b, keys), dot_tn(score_b, queries), dot_tn(probs_b, grads))
            )
        for target, first, second in zip((mixed_s, qp_s, kp_s, vp_s), *found):
            target[:, span] = jnp.where(low, first, second).astype(BF16)
        return carry

    lax.fori_loop(0, 3, tile, 0)


def block_kernel(sizes, latents, conv_w, query_w, key_w, value_w, out_w, gain, out_grad, *refs):
    (block_out, latents_grad, conv_sum, small_sum, gain_sum), refs = refs[:5], refs[5:]
    (
        lat, grad, weights, wq, wk, wv, wo, gain_v, in_sems,
        padded, halo, halo_send, halo_recv, acc, resid, act_t,
        normed_out, normed_in, og_out, og_in, ng_out, ng_in, mix_out, mix_in,
        swap_send, swap_recv,
        q_s, k_s, v_s, d_s, bias, mixed_s, qp_s, kp_s, vp_s, parts, flip,
        resid_grad, grad_pad, gain_acc, conv_terms, conv_total, small_terms, small_total,
    ), refs = refs[:44], refs[44:]
    frames = lax.axis_size("frame")
    rows_n = lax.axis_size("row")
    chunk = HALF // frames
    me, row = lax.axis_index("frame"), lax.axis_index("row")
    place = my_place()
    peers = []
    for step in range(1, frames):
        frame = lax.rem(me + step, frames)
        peers.append((frame, (frame, row)))
    above = (me, lax.rem(row + rows_n - 1, rows_n))
    below = (me, lax.rem(row + 1, rows_n))

    barrier = pltpu.get_barrier_semaphore()
    partners = [device for _, device in peers] + [above, below]
    for axis in "cxy":
        partners += [along(place, axis, step, sizes) for step in range(1, sizes[axis])]
    for device in partners:
        pl.semaphore_signal(barrier, inc=1, device_id=device, device_id_type=MESH)

    loads = []
    pairs = (
        (latents, lat), (out_grad, grad), (conv_w, weights), (gain, gain_v),
        (out_w, wo), (query_w, wq), (key_w, wk), (value_w, wv),
    )
    for at, (source, target) in enumerate(pairs):
        loads.append(pltpu.make_async_copy(source, target, in_sems.at[at]))
        loads[-1].start()

    loads[0].wait()

    def activate(at, carry):
        cells = lat[pl.ds(at * COLS, COLS)].astype(F32)
        act = (cells * jax.nn.sigmoid(cells)).astype(BF16).astype(F32)
        for shift, copy in enumerate(shifts(act)):
            padded[shift, pl.ds((at + 1) * COLS, COLS)] = copy.astype(BF16)
        return carry

    lax.fori_loop(0, ROWS, activate, 0)
    pl.semaphore_wait(barrier, len(partners))

    def halo_start(source, kind):
        return [
            remote(source.at[pl.ds(COLS, COLS)], halo.at[kind, 1],
                   halo_send.at[kind, 0], halo_recv.at[kind, 0], above),
            remote(source.at[pl.ds(ROWS * COLS, COLS)], halo.at[kind, 0],
                   halo_send.at[kind, 1], halo_recv.at[kind, 1], below),
        ]

    def halo_end(copies, kind, target):
        for copy in copies:
            copy.wait_recv()
        ends = (row > 0, row < rows_n - 1)
        for side, inside in enumerate(ends):
            keep = jnp.where(inside, 1.0, 0.0).astype(F32)
            cells = halo[kind, side].astype(F32) * keep
            for shift, copy in enumerate(shifts(cells)):
                target[shift, pl.ds(side * (ROWS + 1) * COLS, COLS)] = copy.astype(BF16)

    act_halo = halo_start(padded.at[1], 0)

    swaps = []
    buffers = ((og_out, og_in), (normed_out, normed_in), (ng_out, ng_in), (mix_out, mix_in))
    for at, (source, target) in enumerate(buffers):
        swaps.append(Swap(source, target, swap_send.at[at], swap_recv.at[at], peers, me))
    og_swap, normed_swap, ng_swap, mix_swap = swaps

    loads[1].wait()
    og_out[0] = grad[COLS : COLS + HALF].reshape(frames, chunk, CHAN)
    og_out[1, : frames // 2] = grad[:COLS].reshape(frames // 2, chunk, CHAN)
    og_out[1, frames // 2 :] = grad[COLS + HALF :].reshape(frames // 2, chunk, CHAN)
    loads[2].wait()
    loads[3].wait()

    def conv_half(half):
        acc[pl.ds(0, HALF)] = jnp.zeros((HALF, CHAN), F32)

        def tap(at, carry):
            a, b = at // 3, lax.rem(at, 3)
            if half == 0:
                cells = padded[b, pl.ds((a + 1) * COLS, HALF)]
            else:
                cells = jnp.concatenate(
                    [padded[b, pl.ds(a * COLS, COLS)], padded[b, pl.ds((a + 3) * COLS, COLS)]]
                )
            acc[pl.ds(0, HALF)] += dot(cells, weights[at])
            return carry

        lax.fori_loop(0, 9, tap, 0)
        count = 64 // chunk

        def finish(at, carry):
            cells = lat[pl.ds(pl.multiple_of(cell_start(half, at), 64), 64)].astype(F32)
            held = (cells + acc[pl.ds(at * 64, 64)]).astype(BF16)
            resid[half, pl.ds(at * 64, 64)] = held
            held = held.astype(F32)
            normed = (held * norm_of(held) * gain_v[...]).astype(BF16)
            normed_out[half, pl.ds(at * count, count)] = normed.reshape(count, chunk, CHAN)
            return carry

        lax.fori_loop(0, 4, finish, 0)

    conv_half(0)
    normed_swap.start(0)
    og_swap.start(0)
    halo_end(act_halo, 0, padded)
    conv_half(1)
    normed_swap.start(1)
    og_swap.start(1)

    position = lax.broadcasted_iota(jnp.int32, (HALF, HALF), 0)
    other = lax.broadcasted_iota(jnp.int32, (HALF, HALF), 1)
    same = lax.rem(position, chunk) == lax.rem(other, chunk)
    bias[...] = jnp.where(same, 0.0, -1e30)
    for field in (q_s, k_s, v_s, d_s):
        field[:, 256:] = jnp.zeros((HALF, 128), BF16)
    for shift in range(3):
        act_t[shift] = padded[shift].astype(F32).T.astype(BF16)
    for load in loads[4:]:
        load.wait()

    for half in range(2):
        og_swap.wait(half)
        d_s[:, :CHAN] = dot_nt(og_in[half].reshape(HALF, CHAN), wo[...]).astype(BF16)
        normed_swap.wait(half)
        normed = normed_in[half].reshape(HALF, CHAN)
        q_s[:, :CHAN] = dot(normed, wq[...]).astype(BF16)
        k_s[:, :CHAN] = dot(normed, wk[...]).astype(BF16)
        v_s[:, :CHAN] = dot(normed, wv[...]).astype(BF16)
        attention(q_s, k_s, v_s, d_s, bias, mixed_s, qp_s, kp_s, vp_s)
        back = dot_nt(qp_s[:, :CHAN], wq[...])
        back = back + dot_nt(kp_s[:, :CHAN], wk[...])
        back = back + dot_nt(vp_s[:, :CHAN], wv[...])
        ng_out[half] = back.astype(BF16).reshape(frames, chunk, CHAN)
        ng_swap.start(half)
        mix_out[half] = mixed_s[:, :CHAN].reshape(frames, chunk, CHAN)
        mix_swap.start(half)
        for at, field in enumerate((qp_s, kp_s, vp_s)):
            parts[at, pl.ds(half * HALF, HALF)] = field[:, :CHAN]

    flip[0] = normed_in[...].reshape(2 * HALF, CHAN).astype(F32).T.astype(BF16)
    flip[1] = mix_out[...].reshape(2 * HALF, CHAN).astype(F32).T.astype(BF16)
    for at in range(3):
        pack(dot(flip[0], parts[at]), small_terms, at * MATRIX_TILES)
    pack(dot(flip[1], og_in[...].reshape(2 * HALF, CHAN)), small_terms, 3 * MATRIX_TILES)
    spare = SMALL_TILES - 4 * MATRIX_TILES
    small_terms[pl.ds(4 * MATRIX_TILES, spare)] = jnp.zeros((spare, 16, 128), BF16)

    summers = []
    for at, order in enumerate(("xyz", "yxz", "zxy")):
        scratch = refs[9 * at : 9 * at + 9]
        if at < 2:
            summers.append(
                Summer(order, place, sizes, conv_terms, conv_total, at * PART, scratch)
            )
        else:
            summers.append(Summer(order, place, sizes, small_terms, small_total, 0, scratch))
    first, second, small = summers
    small.core_start()

    gain_acc[...] = jnp.zeros((8, CHAN), F32)
    for half in range(2):
        ng_swap.wait(half)

        def undo_norm(at, carry, half=half):
            count = 64 // chunk
            begin = pl.multiple_of(cell_start(half, at), 64)
            held = resid[half, pl.ds(at * 64, 64)].astype(F32)
            back = ng_in[half, pl.ds(at * count, count)].reshape(64, CHAN).astype(F32)
            inv = norm_of(held)
            product = back * held
            total = jnp.sum((product * inv).reshape(8, 8, CHAN), axis=0)
            gain_acc[...] += total
            tangent = back * gain_v[...]
            mean = jnp.mean(product * gain_v[...], axis=-1, keepdims=True)
            value = grad[pl.ds(begin, 64)].astype(F32) + (
                inv * tangent - held * (inv * inv * inv) * mean
            )
            resid_grad[pl.ds(begin, 64)] = value.astype(BF16)
            return carry

        lax.fori_loop(0, 4, undo_norm, 0)
    small.core_end()
    small.scatter_start(0)

    def pad_grad(at, carry):
        cells = resid_grad[pl.ds(at * COLS, COLS)].astype(F32)
        for shift, copy in enumerate(shifts(cells)):
            grad_pad[shift, pl.ds((at + 1) * COLS, COLS)] = copy.astype(BF16)
        return carry

    lax.fori_loop(0, ROWS, pad_grad, 0)
    grad_halo = halo_start(grad_pad.at[1], 1)

    def conv_tap(at, carry):
        a, b = at // 3, lax.rem(at, 3)
        cells = act_t[b, :, pl.ds(pl.multiple_of(a * COLS, COLS), ROWS * COLS)]
        pack(dot(cells, resid_grad[...]), conv_terms, at * MATRIX_TILES)
        return carry

    lax.fori_loop(0, 6, conv_tap, 0)
    first.core_start()
    spare = CONV_TILES - GAIN_TILE
    conv_terms[pl.ds(GAIN_TILE, spare)] = jnp.zeros((spare, 16, 128), BF16)
    gains = jnp.sum(gain_acc[...], axis=0, keepdims=True)
    line = lax.broadcasted_iota(jnp.int32, (16, 128), 0)
    gain_tile = jnp.where(line == 0, gains[:, :128], jnp.where(line == 1, gains[:, 128:256], 0.0))
    conv_terms[GAIN_TILE] = gain_tile.astype(BF16)
    tail = jnp.where(line[:, :64] == 0, gains[:, 256:], 0.0)
    conv_terms[GAIN_TILE + 1, :, :64] = tail.astype(BF16)
    lax.fori_loop(6, 9, conv_tap, 0)
    second.core_start()
    small.scatter_end(0)
    small.scatter_start(1)
    first.core_end()
    first.scatter_start(0)
    second.core_end()
    second.scatter_start(0)
    small.scatter_end(1)
    small.scatter_start(2)

    for half in range(2):
        mix_swap.wait(half)
        acc[pl.ds(0, HALF)] = dot(mix_in[half].reshape(HALF, CHAN), wo[...])

        def write_out(at, carry, half=half):
            begin = pl.multiple_of(cell_start(half, at), 64)
            held = resid[half, pl.ds(at * 64, 64)].astype(F32)
            block_out[pl.ds(begin, 64)] = (held + acc[pl.ds(at * 64, 64)]).astype(BF16)
            return carry

        lax.fori_loop(0, 4, write_out, 0)
    for part in (first, second):
        part.scatter_end(0)
        part.scatter_start(1)
    small.scatter_end(2)
    small.gather_start(2)
    halo_end(grad_halo, 1, grad_pad)
    acc[...] = jnp.zeros((2 * HALF, CHAN), F32)

    def back_tap(at, carry):
        a, b = at // 3, lax.rem(at, 3)
        cells = grad_pad[2 - b, pl.ds((2 - a) * COLS, ROWS * COLS)]
        acc[...] += dot_nt(cells, weights[at])
        return carry

    lax.fori_loop(0, 4, back_tap, 0)
    for part in (first, second):
        part.scatter_end(1)
        part.scatter_start(2)
    small.arrive()
    small.gather_start(1)
    lax.fori_loop(4, 9, back_tap, 0)
    for part in (first, second):
        part.scatter_end(2)
        part.gather_start(2)
    small.arrive()
    small.gather_start(0)

    def write_back(at, carry):
        cells = lat[pl.ds(at * COLS, COLS)].astype(F32)
        sigma = jax.nn.sigmoid(cells)
        slope = sigma * (1.0 + cells * (1.0 - sigma))
        value = resid_grad[pl.ds(at * COLS, COLS)].astype(F32) + acc[pl.ds(at * COLS, COLS)] * slope
        latents_grad[pl.ds(at * COLS, COLS)] = value.astype(BF16)
        return carry

    lax.fori_loop(0, ROWS, write_back, 0)
    for part in (first, second):
        part.arrive()
        part.gather_start(1)
    small.arrive()
    small.core_back()
    for part in (first, second):
        part.arrive()
        part.gather_start(0)
    small.arrive()

    def small_out(at, carry):
        unpack(small_total, at * MATRIX_TILES, small_sum, at * CHAN)
        return carry

    lax.fori_loop(0, 4, small_out, 0)
    for part in (first, second):
        part.arrive()
        part.core_back()
    for part in (first, second):
        part.arrive()

    def conv_out(at, carry):
        unpack(conv_total, at * MATRIX_TILES, conv_sum, at * CHAN)
        return carry

    lax.fori_loop(0, 9, conv_out, 0)
    gain_sum[...] = conv_total[GAIN_TILE : GAIN_TILE + 2]
    for part in summers:
        part.finish()
    for swap in swaps:
        swap.finish()
    for copy in act_halo + grad_halo:
        copy.wait_send()


def block_scratch(sizes, frames):
    chunk = HALF // frames
    field = (2, frames, chunk, CHAN)
    vmem = pltpu.VMEM
    dma = pltpu.SemaphoreType.DMA
    weight = vmem((CHAN, CHAN), BF16)
    shapes = [
        vmem((ROWS * COLS, CHAN), BF16), vmem((ROWS * COLS, CHAN), BF16),
        vmem((9, CHAN, CHAN), BF16), weight, weight, weight, weight, vmem((1, CHAN), F32), dma((8,)),
        vmem((3, (ROWS + 2) * COLS, CHAN), BF16), vmem((2, 2, COLS, CHAN), BF16),
        dma((2, 2)), dma((2, 2)), vmem((2 * HALF, CHAN), F32), vmem((2, HALF, CHAN), BF16),
        vmem((3, CHAN, (ROWS + 2) * COLS), BF16),
    ]
    shapes += [vmem(field, BF16)] * 8 + [dma((4, 2)), dma((4, 2))]
    shapes += [vmem((HALF, WIDE), BF16)] * 4 + [vmem((HALF, HALF), F32)]
    shapes += [vmem((HALF, WIDE), BF16)] * 4
    shapes += [vmem((3, 2 * HALF, CHAN), BF16), vmem((2, CHAN, 2 * HALF), BF16)]
    shapes += [vmem((ROWS * COLS, CHAN), BF16), vmem((3, (ROWS + 2) * COLS, CHAN), BF16)]
    shapes += [vmem((8, CHAN), F32)]
    shapes += [vmem((CONV_TILES, 16, 128), BF16)] * 2 + [vmem((SMALL_TILES, 16, 128), BF16)] * 2
    for order in ("xyz", "yxz", "zxy"):
        shapes += summer_scratch(order, sizes)
    return shapes


def on_device(
    latents, conv_weight, query_weight, key_weight, value_weight, out_weight, norm_gain, out_grad
):
    shape = latents.shape
    cells = ROWS * COLS
    sizes = chip_sizes()
    frames = lax.axis_size("frame")
    anywhere = pl.BlockSpec(memory_space=pl.ANY)
    inside = pl.BlockSpec(memory_space=pltpu.VMEM)
    block_out, latents_grad, conv_sum, small_sum, gain_sum = pl.pallas_call(
        functools.partial(block_kernel, sizes),
        out_shape=[
            jax.ShapeDtypeStruct((cells, CHAN), BF16),
            jax.ShapeDtypeStruct((cells, CHAN), BF16),
            jax.ShapeDtypeStruct((9 * CHAN, CHAN), BF16),
            jax.ShapeDtypeStruct((4 * CHAN, CHAN), BF16),
            jax.ShapeDtypeStruct((2, 16, 128), BF16),
        ],
        in_specs=[anywhere] * 8,
        out_specs=[inside] * 5,
        scratch_shapes=block_scratch(sizes, frames),
        compiler_params=pltpu.CompilerParams(
            collective_id=0, has_side_effects=True, vmem_limit_bytes=56 << 20
        ),
    )(
        latents.reshape(cells, CHAN),
        conv_weight.reshape(9, CHAN, CHAN),
        query_weight,
        key_weight,
        value_weight,
        out_weight,
        norm_gain.reshape(1, CHAN),
        out_grad.reshape(cells, CHAN),
    )
    factor = (cells * frames * lax.axis_size("row")) ** (-0.5)
    small = [
        small_sum[at * CHAN : (at + 1) * CHAN].astype(F32) * factor for at in range(4)
    ]
    gains = jnp.concatenate([gain_sum[0, 0], gain_sum[0, 1], gain_sum[1, 0, :64]])
    return (
        block_out.reshape(shape),
        latents_grad.reshape(shape),
        conv_sum.astype(F32).reshape(3, 3, CHAN, CHAN) * factor,
        *small,
        gains.astype(F32) * factor,
    )


def solution(mesh):
    split = P("frame", "row", None, None)
    return jax.shard_map(
        on_device,
        mesh=mesh,
        in_specs=(split, P(), P(), P(), P(), P(), P(), split),
        out_specs=(split, split, P(), P(), P(), P(), P(), P()),
        check_vma=False,
    )
```

time: 553 us -> 122 us (0.22)
  waiting for transfers between devices: 323 us -> 0 us
  Pallas kernels: 0 us -> 104 us
  blocking collectives: 75 us -> 0 us
  matrix products: 51.6 us -> 0 us
  starting transfers between devices: 38.3 us -> 0 us
  local copies, waits for them, and re-layouts: 37.1 us -> 10.3 us
  between operations: 14.6 us -> 0.65 us
  other arithmetic: 11.6 us -> 6 us
    psum x1 -> x0, waiting for transfers between devices: 267 us -> none  [on_device(): lax.psum((grad_conv, grad_query, grad_key, grad_value, grad_out_w, grad_g...]
    pallas_call x0 -> x1, Pallas kernels: none -> 104 us  [on_device(): pl.pallas_call(functools.partial(block_kernel, sizes), out_shape=[jax.Sha...]
    psum x1 -> x0, blocking collectives: 75 us -> none  [on_device(): lax.psum((grad_conv, grad_query, grad_key, grad_value, grad_out_w, grad_g...]
    all_to_all x4 -> x0, waiting for transfers between devices: 55.3 us -> none  [the longest x2 30 us: to_pixels(): lax.all_to_all(stacked, 'frame', split_axis=3, concat_axis=1, tiled=True)]
    dot_general x44 -> x0, matrix products: 47.9 us -> none  [the longest x13 14.8 us: outer_sum(): lax.dot_general(left_flat, right_flat, (((0,), (0,)), ((), ())), preferre...]
    all_to_all x4 -> x0, starting transfers between devices: 24.8 us -> none  [the longest x2 13.1 us: to_pixels(): lax.all_to_all(stacked, 'frame', split_axis=3, concat_axis=1, tiled=True)]
    convert_element_type x9 -> x0, local copies, waits for them, and re-layouts: 16 us -> none  [the longest x2 4.72 us: attend_back(): query_part.reshape(shape).astype(jnp.bfloat16)]
    ppermute x4 -> x0, starting transfers between devices: 13.5 us -> none  [the longest x2 9.68 us: padded_2(): lax.ppermute(tail, axis, [(i, (i + 1) % count) for i in range(ends)])]
  transfers between devices with their start and end apart: 9 -> 0, of which waited for: 4 -> 0; matrix products, arithmetic and copies ran while one was open for 9% -> 0% of each run, Pallas kernels for 0% -> 0%
where the time goes in v2:
time: 122 us; the launch traced here: 121 us
  Pallas kernels  104 us (85%)
  local copies, waits for them, and re-layouts  10.3 us (8%)
  other arithmetic  6 us (5%)
    pallas_call x1, Pallas kernels, on_device(): pl.pallas_call(functools.partial(block_kernel, sizes), out_shape=[jax.Sha...  104 us
    unnamed x6, local copies, waits for them, and re-layouts  7.65 us
    mul x1, other arithmetic, on_device(): conv_sum.astype(F32).reshape(3, 3, CHAN, CHAN) * factor  4.1 us

profile of v2, /device:TPU:1, one launch (start us, length us, event | category | flops | bytes accessed | tf_op | source)
XLA Modules:
  0.0 121.3 jit_solution(13975787713845358845)
XLA Ops:
  0.6 1.9 %copy.16 = bf16[1,4,128,320]{3,2,1,0:T(8,128)(2,1)} copy(bf16[1,4,128,320]{2,3,1,0:T(8,128)(2,1)} %param.8) | data formatting | bytes 655360 | tf_op args[0]
  2.5 1.2 %reshape.39.gain = f32[1,320]{1,0:T(1,128)} reshape(f32[320]{0:T(512)} %param.14) | data formatting | bytes 2560 | tf_op jit(solution)/shard_map/reshape | solution.py:645
  3.8 1.9 %copy.17 = bf16[1,4,128,320]{3,2,1,0:T(8,128)(2,1)} copy(bf16[1,4,128,320]{2,3,1,0:T(8,128)(2,1)} %param.15) | data formatting | bytes 655360 | tf_op args[7]
  5.7 104.4 %shard_map.143 = (bf16[512,320]{1,0:T(8,128)(2,1)}, bf16[512,320]{1,0:T(8,128)(2,1)}, bf16[2880,320]{1,0:T(8,128)(2,1)}, bf16[1280,320]{1,0:T(8,128)(2,1)}, bf16[2,16,128]{2,1,0:T(8,128)(2,1)}) custom-call(bf16[512,320]{1,0:T(8,128)(2,1)} %bitcast.14, bf16[9,320,320]{2,1,0:T(8,128)(2,1)} %bitcast.13, bf16[320,320]{1,0:T(8,128)(2,1)} %query_w.1, ...), custom_call_target="tpu_custom_call" | custom-call | tf_op jit(solution)/shard_map/pallas_call | solution.py:623
  110.0 0.0 copy-start
  110.0 2.0 %copy.18 = bf16[1,4,128,320]{2,3,1,0:T(8,128)(2,1)} copy(bf16[1,4,128,320]{3,2,1,0:T(8,128)(2,1)} %bitcast.17) | data formatting | bytes 655360
  112.0 1.9 %copy.19 = bf16[1,4,128,320]{2,3,1,0:T(8,128)(2,1)} copy(bf16[1,4,128,320]{3,2,1,0:T(8,128)(2,1)} %bitcast.16) | data formatting | bytes 655360
  113.9 4.1 %convert_multiply_fusion = f32[2880,320]{1,0:T(8,128)} fusion(bf16[2880,320]{1,0:T(8,128)(2,1)} %get-tuple-element.15), kind=kLoop, calls=%fused_computation | loop fusion | flops 1843200 | bytes 5529600 | tf_op jit(solution)/shard_map/mul | solution.py:656
  118.0 0.0 copy-done
  118.0 1.3 %convert_multiply_fusion.1 = (f32[320,320]{1,0:T(8,128)}, f32[320,320]{1,0:T(8,128)}, f32[320,320]{1,0:T(8,128)}, f32[320,320]{1,0:T(8,128)}) fusion(bf16[1280,320]{1,0:T(8,128)(2,1)S(1)} %copy-done), kind=kLoop, calls=%fused_computation.1 | loop fusion | flops 819200 | bytes 2457600 | tf_op jit(solution)/shard_map/mul | solution.py:650
  119.3 0.7 slice_bitcast_fusion
  120.0 0.7 slice_bitcast_fusion.2
  120.7 0.6 convert_multiply_fusion.5
Async XLA Ops:
  110.0 8.0 %copy-start = (bf16[1280,320]{1,0:T(8,128)(2,1)S(1)}, bf16[1280,320]{1,0:T(8,128)(2,1)}, u32[]{:S(2)}) copy-start(bf16[1280,320]{1,0:T(8,128)(2,1)} %get-tuple-element.16) | copy-start | bytes 2457604

commit v3 on v2

--- a/solution.py
+++ b/solution.py
@@ -77,9 +77,8 @@
 
 
 def add_up(target, start, own, own_start, received):
-    count = own.shape[0] if own_start is None else received[0].shape[0]
+    count = received[0].shape[0]
     step = min(count, BLOCK)
-    own_start = 0 if own_start is None else own_start
 
     def body(at, carry):
         at = at * step
@@ -90,6 +89,197 @@
         return carry
 
     lax.fori_loop(0, count // step, body, 0)
+
+
+def wait_bytes(span, sem):
+    pltpu.make_async_copy(span, span, sem).wait()
+
+
+class ConvSummer:
+    ORDERS = ("xy", "yx")
+
+    def __init__(self, place, sizes, terms, total, scratch):
+        self.place, self.sizes, self.terms, self.total = place, sizes, terms, total
+        (
+            self.core_in, self.held0, self.inbox0, self.held1, self.inbox1, self.held2, self.inbox2,
+            self.core_sems, self.scatter0, self.scatter1, self.scatter2,
+            self.gather2, self.gather1, self.gather0, self.back, self.sends,
+        ) = scratch
+        self.unit = PART // (2 * sizes["x"] * sizes["y"] * sizes["z"])
+        self.group = self.unit * sizes["z"]
+        self.n1 = [sizes[order[0]] for order in self.ORDERS]
+        self.n2 = [sizes[order[1]] for order in self.ORDERS]
+
+    def at(self, part, axis):
+        return self.place[self.ORDERS[part][axis]]
+
+    def peer(self, part, axis, step):
+        return lax.rem(self.at(part, axis) + step, self.sizes[self.ORDERS[part][axis]])
+
+    def device(self, axis, step):
+        return along(self.place, axis, step, self.sizes)
+
+    def tile(self, part, chunk, core, group, unit=0):
+        span = self.n2[part] * self.group
+        return part * PART + (chunk * 2 + core) * span + group * self.group + unit * self.unit
+
+    def core_start(self, piece):
+        n1, span = self.n1[0], self.n2[0] * self.group
+        start = piece * 2 * span + (1 - self.place["c"]) * span
+        remote(
+            self.terms.at[pl.ds(start, span)],
+            self.core_in.at[pl.ds(piece * span, span)],
+            self.sends.at[0],
+            self.core_sems.at[piece],
+            self.device("c", 1),
+        )
+
+    def core_wait(self, part, chunk):
+        span = self.n2[part] * self.group
+        wait_bytes(self.core_in.at[pl.ds(0, span)], self.core_sems.at[part * self.n1[part] + chunk])
+
+    def core_sum(self, part, chunk, group):
+        own = self.tile(part, chunk, self.place["c"], group)
+        there = (part * self.n1[part] + chunk) * self.n2[part] * self.group + group * self.group
+        total = self.terms[pl.ds(own, self.group)].astype(F32)
+        return total + self.core_in[pl.ds(there, self.group)].astype(F32)
+
+    def scatter_first(self):
+        for step2 in range(self.n2[0]):
+            step2 = (step2 + 1) % self.n2[0]
+            for step in range(1, self.n1[0]):
+                for part in range(2):
+                    chunk, group = self.peer(part, 0, step), self.peer(part, 1, step2)
+                    if step2 == 1:
+                        self.core_wait(part, chunk)
+                    slot = part * self.n1[part] * self.n2[part] + chunk * self.n2[part] + group
+                    held = self.held0.at[pl.ds(slot * self.group, self.group)]
+                    held[...] = self.core_sum(part, chunk, group).astype(BF16)
+                    remote(
+                        held,
+                        self.inbox0.at[part, group, pl.ds((step - 1) * self.group, self.group)],
+                        self.sends.at[1],
+                        self.scatter0.at[part, step2],
+                        self.device(self.ORDERS[part][0], step),
+                    )
+
+    def scatter_second(self):
+        for step2 in range(self.n2[0]):
+            step2 = (step2 + 1) % self.n2[0]
+            for part in range(2):
+                chunk, group = self.at(part, 0), self.peer(part, 1, step2)
+                if step2 == 1:
+                    self.core_wait(part, chunk)
+                wait_bytes(self.inbox0.at[part, group], self.scatter0.at[part, step2])
+                total = self.core_sum(part, chunk, group)
+                for step in range(self.n1[part] - 1):
+                    span = pl.ds(step * self.group, self.group)
+                    total = total + self.inbox0[part, group, span].astype(F32)
+                held = self.held1.at[part, group]
+                held[...] = total.astype(BF16)
+                if step2 > 0:
+                    remote(
+                        held,
+                        self.inbox1.at[part, pl.ds((step2 - 1) * self.group, self.group)],
+                        self.sends.at[2],
+                        self.scatter1.at[part],
+                        self.device(self.ORDERS[part][1], step2),
+                    )
+
+    def scatter_third(self):
+        for part in range(2):
+            wait_bytes(self.inbox1.at[part], self.scatter1.at[part])
+            total = self.held1[part, self.at(part, 1)].astype(F32)
+            for step in range(self.n2[part] - 1):
+                total = total + self.inbox1[part, pl.ds(step * self.group, self.group)].astype(F32)
+            self.held2[part] = total.astype(BF16)
+            for step in range(1, self.sizes["z"]):
+                peer = lax.rem(self.place["z"] + step, self.sizes["z"])
+                remote(
+                    self.held2.at[part, pl.ds(peer * self.unit, self.unit)],
+                    self.inbox2.at[part, pl.ds((step - 1) * self.unit, self.unit)],
+                    self.sends.at[3],
+                    self.scatter2.at[part],
+                    self.device("z", step),
+                )
+
+    def gather_third(self):
+        for part in range(2):
+            wait_bytes(self.inbox2.at[part], self.scatter2.at[part])
+            z = self.place["z"]
+            total = self.held2[part, pl.ds(z * self.unit, self.unit)].astype(F32)
+            for step in range(self.sizes["z"] - 1):
+                total = total + self.inbox2[part, pl.ds(step * self.unit, self.unit)].astype(F32)
+            mine = self.tile(part, self.at(part, 0), self.place["c"], self.at(part, 1), z)
+            self.total[pl.ds(mine, self.unit)] = total.astype(BF16)
+            span = self.total.at[pl.ds(mine, self.unit)]
+            for step in range(1, self.sizes["z"]):
+                remote(
+                    span, span, self.sends.at[4], self.gather2.at[part], self.device("z", step)
+                )
+
+    def spread(self, part, chunk, group, axis, steps, send, sem):
+        span = self.total.at[pl.ds(self.tile(part, chunk, self.place["c"], group), self.group)]
+        for step in steps:
+            remote(span, span, self.sends.at[send], sem, self.device(axis, step))
+
+    def gather_rest(self):
+        n1, n2 = self.n1[0], self.n2[0]
+        for part in range(2):
+            wait_bytes(
+                self.total.at[pl.ds(0, (self.sizes["z"] - 1) * self.unit)], self.gather2.at[part]
+            )
+            first, second = self.ORDERS[part]
+            chunk, group = self.at(part, 0), self.at(part, 1)
+            for step in range(1, n2):
+                sem = self.gather1.at[part, step]
+                self.spread(part, chunk, group, second, [step], 5, sem)
+            self.spread(part, chunk, group, first, range(1, n1), 6, self.gather0.at[part, 0])
+            self.spread(part, chunk, group, "c", [1], 7, self.back.at[0])
+        for step2 in range(1, n2):
+            for part in range(2):
+                first = self.ORDERS[part][0]
+                chunk = self.at(part, 0)
+                group = self.peer(part, 1, n2 - step2)
+                wait_bytes(self.total.at[pl.ds(0, self.group)], self.gather1.at[part, step2])
+                self.spread(
+                    part, chunk, group, first, range(1, n1), 6, self.gather0.at[part, step2]
+                )
+                self.spread(part, chunk, group, "c", [1], 7, self.back.at[0])
+        for step2 in range(n2):
+            for part in range(2):
+                wait_bytes(
+                    self.total.at[pl.ds(0, (n1 - 1) * self.group)], self.gather0.at[part, step2]
+                )
+                group = self.peer(part, 1, n2 - step2)
+                for step in range(1, n1):
+                    chunk = self.peer(part, 0, n1 - step)
+                    self.spread(part, chunk, group, "c", [1], 7, self.back.at[0])
+
+    def finish(self):
+        wait_bytes(self.total.at[pl.ds(0, PART)], self.back.at[0])
+        n1, n2, nz = self.n1[0], self.n2[0], self.sizes["z"]
+        counts = (
+            PART, 2 * n2 * (n1 - 1) * self.group, 2 * (n2 - 1) * self.group,
+            2 * (nz - 1) * self.unit, 2 * (nz - 1) * self.unit, 2 * (n2 - 1) * self.group,
+            2 * n2 * (n1 - 1) * self.group, PART,
+        )
+        for at, count in enumerate(counts):
+            wait_bytes(self.total.at[pl.ds(0, count)], self.sends.at[at])
+
+
+def conv_summer_scratch(sizes):
+    unit = PART // (2 * sizes["x"] * sizes["y"] * sizes["z"])
+    group = unit * sizes["z"]
+    n1, n2 = sizes["x"], sizes["y"]
+    tiles = [
+        (PART,), (PART,), (2, n2, (n1 - 1) * group), (2, n2, group), (2, (n2 - 1) * group),
+        (2, group), (2, (sizes["z"] - 1) * unit),
+    ]
+    sems = [(2 * n1,), (2, n2), (2,), (2,), (2,), (2, n2), (2, n2), (1,), (8,)]
+    return [pltpu.VMEM(shape + (16, 128), BF16) for shape in tiles] + [
+        pltpu.SemaphoreType.DMA(shape) for shape in sems
+    ]
 
 
 class Summer:
@@ -194,13 +384,64 @@
     tiles[pl.ds(base + 40, 10)] = tail.reshape(10, 16, 128)
 
 
-def unpack(tiles, base, target, row):
+def unpack(tiles, base, target, at, factor):
     for block in range(2):
-        cut = tiles[pl.ds(base + 20 * block, 20)].reshape(320, 128)
-        target[pl.ds(row, 320), block * 128 : block * 128 + 128] = cut
-    tail = tiles[pl.ds(base + 40, 10)].reshape(160, 128)
-    target[pl.ds(row, 160), 256:] = tail[:, :64]
-    target[pl.ds(row + 160, 160), 256:] = tail[:, 64:]
+        cut = tiles[pl.ds(base + 20 * block, 20)].reshape(CHAN, 128)
+        target[at, :, block * 128 : block * 128 + 128] = cut.astype(F32) * factor
+    tail = tiles[pl.ds(base + 40, 10)].reshape(160, 128).astype(F32) * factor
+    target[at, :160, 256:] = tail[:, :64]
+    target[at, 160:, 256:] = tail[:, 64:]
+
+
+def finish_kernel(factor, block_in, back_in, conv_in, small_in, *refs):
+    (block_out, back_out, conv_out), small_outs, gain_out = refs[:3], refs[3:7], refs[7]
+    conv, small, wide, fields, through, load_sems, store_sems = refs[8:]
+    moves = []
+    for at, (source, target) in enumerate(((block_in, block_out), (back_in, back_out))):
+        moves.append(
+            (
+                pltpu.make_async_copy(source, fields.at[at], through.at[at]),
+                pltpu.make_async_copy(fields.at[at], target, through.at[at + 2]),
+            )
+        )
+        moves[-1][0].start()
+
+    def load(at, source, target):
+        span = pl.ds(at * MATRIX_TILES, MATRIX_TILES)
+        return source.at[span], target.at[span]
+
+    for at in range(4):
+        pltpu.make_async_copy(*load(at, small_in, small), load_sems.at[9 + at]).start()
+    for at in range(9):
+        pltpu.make_async_copy(*load(at, conv_in, conv), load_sems.at[at]).start()
+    last = pl.ds(GAIN_TILE, 2)
+    gain_load = pltpu.make_async_copy(conv_in.at[last], conv.at[last], load_sems.at[13])
+    gain_load.start()
+    for at in range(4):
+        pltpu.make_async_copy(*load(at, small_in, small), load_sems.at[9 + at]).wait()
+        unpack(small, at * MATRIX_TILES, wide, 9 + at, factor)
+        pltpu.make_async_copy(wide.at[9 + at], small_outs[at], store_sems.at[9 + at]).start()
+
+    def conv_tap(at, carry):
+        pltpu.make_async_copy(*load(at, conv_in, conv), load_sems.at[at]).wait()
+        unpack(conv, at * MATRIX_TILES, wide, at, factor)
+        pltpu.make_async_copy(wide.at[at], conv_out.at[at], store_sems.at[at]).start()
+        return carry
+
+    for move in moves:
+        move[0].wait()
+        move[1].start()
+    lax.fori_loop(0, 9, conv_tap, 0)
+    gain_load.wait()
+    gain_out[0:128] = (conv[GAIN_TILE].astype(F32) * factor)[0]
+    gain_out[128:256] = (conv[GAIN_TILE].astype(F32) * factor)[1]
+    gain_out[256:] = (conv[GAIN_TILE + 1].astype(F32) * factor)[0, :64]
+    for move in moves:
+        move[1].wait()
+    for at in range(9):
+        pltpu.make_async_copy(wide.at[at], conv_out.at[at], store_sems.at[at]).wait()
+    for at in range(4):
+        pltpu.make_async_copy(wide.at[9 + at], small_outs[at], store_sems.at[9 + at]).wait()
 
 
 def shifts(cells):
@@ -275,14 +516,14 @@
 
 
 def block_kernel(sizes, latents, conv_w, query_w, key_w, value_w, out_w, gain, out_grad, *refs):
-    (block_out, latents_grad, conv_sum, small_sum, gain_sum), refs = refs[:5], refs[5:]
+    (block_out, latents_grad, conv_total, small_total), refs = refs[:4], refs[4:]
     (
-        lat, grad, weights, wq, wk, wv, wo, gain_v, in_sems,
+        lat_in, grad_in, lat, grad, weights, wq, wk, wv, wo, gain_v, in_sems,
         padded, halo, halo_send, halo_recv, acc, resid, act_t,
         normed_out, normed_in, og_out, og_in, ng_out, ng_in, mix_out, mix_in,
         swap_send, swap_recv,
         q_s, k_s, v_s, d_s, bias, mixed_s, qp_s, kp_s, vp_s, parts, flip,
-        resid_grad, grad_pad, gain_acc, conv_terms, conv_total, small_terms, small_total,
+        resid_grad, grad_pad, gain_acc, conv_terms, small_terms,
     ), refs = refs[:44], refs[44:]
     frames = lax.axis_size("frame")
     rows_n = lax.axis_size("row")
@@ -305,7 +546,7 @@
 
     loads = []
     pairs = (
-        (latents, lat), (out_grad, grad), (conv_w, weights), (gain, gain_v),
+        (latents, lat_in), (out_grad, grad_in), (conv_w, weights), (gain, gain_v),
         (out_w, wo), (query_w, wq), (key_w, wk), (value_w, wv),
     )
     for at, (source, target) in enumerate(pairs):
@@ -315,7 +556,9 @@
     loads[0].wait()
 
     def activate(at, carry):
-        cells = lat[pl.ds(at * COLS, COLS)].astype(F32)
+        span = pl.ds(at * COLS, COLS)
+        cells = lat_in[at].astype(F32).T
+        lat[span] = cells.astype(BF16)
         act = (cells * jax.nn.sigmoid(cells)).astype(BF16).astype(F32)
         for shift, copy in enumerate(shifts(act)):
             padded[shift, pl.ds((at + 1) * COLS, COLS)] = copy.astype(BF16)
@@ -351,9 +594,17 @@
     og_swap, normed_swap, ng_swap, mix_swap = swaps
 
     loads[1].wait()
+
+    def flip_grad(at, carry):
+        grad[pl.ds(at * COLS, COLS)] = grad_in[at].astype(F32).T.astype(BF16)
+        return carry
+
+    lax.fori_loop(0, ROWS, flip_grad, 0)
     og_out[0] = grad[COLS : COLS + HALF].reshape(frames, chunk, CHAN)
     og_out[1, : frames // 2] = grad[:COLS].reshape(frames // 2, chunk, CHAN)
     og_out[1, frames // 2 :] = grad[COLS + HALF :].reshape(frames // 2, chunk, CHAN)
+    og_swap.start(0)
+    og_swap.start(1)
     loads[2].wait()
     loads[3].wait()
 
@@ -379,7 +630,7 @@
             held = (cells + acc[pl.ds(at * 64, 64)]).astype(BF16)
             resid[half, pl.ds(at * 64, 64)] = held
             held = held.astype(F32)
-            normed = (held * norm_of(held) * gain_v[...]).astype(BF16)
+            normed = (held * norm_of(held) * gain_v[...].reshape(1, CHAN)).astype(BF16)
             normed_out[half, pl.ds(at * count, count)] = normed.reshape(count, chunk, CHAN)
             return carry
 
@@ -387,11 +638,9 @@
 
     conv_half(0)
     normed_swap.start(0)
-    og_swap.start(0)
     halo_end(act_halo, 0, padded)
     conv_half(1)
     normed_swap.start(1)
-    og_swap.start(1)
 
     position = lax.broadcasted_iota(jnp.int32, (HALF, HALF), 0)
     other = lax.broadcasted_iota(jnp.int32, (HALF, HALF), 1)
@@ -431,16 +680,8 @@
     spare = SMALL_TILES - 4 * MATRIX_TILES
     small_terms[pl.ds(4 * MATRIX_TILES, spare)] = jnp.zeros((spare, 16, 128), BF16)
 
-    summers = []
-    for at, order in enumerate(("xyz", "yxz", "zxy")):
-        scratch = refs[9 * at : 9 * at + 9]
-        if at < 2:
-            summers.append(
-                Summer(order, place, sizes, conv_terms, conv_total, at * PART, scratch)
-            )
-        else:
-            summers.append(Summer(order, place, sizes, small_terms, small_total, 0, scratch))
-    first, second, small = summers
+    conv = ConvSummer(place, sizes, conv_terms, conv_total, refs[9:])
+    small = Summer("yxz", place, sizes, small_terms, small_total, 0, refs[:9])
     small.core_start()
 
     gain_acc[...] = jnp.zeros((8, CHAN), F32)
@@ -456,8 +697,8 @@
             product = back * held
             total = jnp.sum((product * inv).reshape(8, 8, CHAN), axis=0)
             gain_acc[...] += total
-            tangent = back * gain_v[...]
-            mean = jnp.mean(product * gain_v[...], axis=-1, keepdims=True)
+            tangent = back * gain_v[...].reshape(1, CHAN)
+            mean = jnp.mean(product * gain_v[...].reshape(1, CHAN), axis=-1, keepdims=True)
             value = grad[pl.ds(begin, 64)].astype(F32) + (
                 inv * tangent - held * (inv * inv * inv) * mean
             )
@@ -477,14 +718,7 @@
     lax.fori_loop(0, ROWS, pad_grad, 0)
     grad_halo = halo_start(grad_pad.at[1], 1)
 
-    def conv_tap(at, carry):
-        a, b = at // 3, lax.rem(at, 3)
-        cells = act_t[b, :, pl.ds(pl.multiple_of(a * COLS, COLS), ROWS * COLS)]
-        pack(dot(cells, resid_grad[...]), conv_terms, at * MATRIX_TILES)
-        return carry
-
-    lax.fori_loop(0, 6, conv_tap, 0)
-    first.core_start()
+    span = 2 * (PART // 8)
     spare = CONV_TILES - GAIN_TILE
     conv_terms[pl.ds(GAIN_TILE, spare)] = jnp.zeros((spare, 16, 128), BF16)
     gains = jnp.sum(gain_acc[...], axis=0, keepdims=True)
@@ -493,33 +727,36 @@
     conv_terms[GAIN_TILE] = gain_tile.astype(BF16)
     tail = jnp.where(line[:, :64] == 0, gains[:, 256:], 0.0)
     conv_terms[GAIN_TILE + 1, :, :64] = tail.astype(BF16)
-    lax.fori_loop(6, 9, conv_tap, 0)
-    second.core_start()
+
+    def conv_tap(at, carry):
+        a, b = at // 3, lax.rem(at, 3)
+        cells = act_t[b, :, pl.ds(pl.multiple_of(a * COLS, COLS), ROWS * COLS)]
+        pack(dot(cells, resid_grad[...]), conv_terms, at * MATRIX_TILES)
+        done = ((at + 1) * MATRIX_TILES) // span
+
+        @pl.when(done > (at * MATRIX_TILES) // span)
+        def _():
+            conv.core_start(done - 1)
+
+        return carry
+
+    lax.fori_loop(0, 9, conv_tap, 0)
+    conv.core_start(7)
+    conv.scatter_first()
     small.scatter_end(0)
     small.scatter_start(1)
-    first.core_end()
-    first.scatter_start(0)
-    second.core_end()
-    second.scatter_start(0)
-    small.scatter_end(1)
-    small.scatter_start(2)
-
     for half in range(2):
         mix_swap.wait(half)
         acc[pl.ds(0, HALF)] = dot(mix_in[half].reshape(HALF, CHAN), wo[...])
 
         def write_out(at, carry, half=half):
-            begin = pl.multiple_of(cell_start(half, at), 64)
-            held = resid[half, pl.ds(at * 64, 64)].astype(F32)
-            block_out[pl.ds(begin, 64)] = (held + acc[pl.ds(at * 64, 64)]).astype(BF16)
+            held = resid[half, pl.ds(at * COLS, COLS)].astype(F32)
+            total = held + acc[pl.ds(at * COLS, COLS)]
+            row_at = at + 1 if half == 0 else at * 3
+            block_out[row_at] = total.T.astype(BF16)
             return carry
 
-        lax.fori_loop(0, 4, write_out, 0)
-    for part in (first, second):
-        part.scatter_end(0)
-        part.scatter_start(1)
-    small.scatter_end(2)
-    small.gather_start(2)
+        lax.fori_loop(0, 2, write_out, 0)
     halo_end(grad_halo, 1, grad_pad)
     acc[...] = jnp.zeros((2 * HALF, CHAN), F32)
 
@@ -529,57 +766,35 @@
         acc[...] += dot_nt(cells, weights[at])
         return carry
 
-    lax.fori_loop(0, 4, back_tap, 0)
-    for part in (first, second):
-        part.scatter_end(1)
-        part.scatter_start(2)
-    small.arrive()
-    small.gather_start(1)
-    lax.fori_loop(4, 9, back_tap, 0)
-    for part in (first, second):
-        part.scatter_end(2)
-        part.gather_start(2)
-    small.arrive()
-    small.gather_start(0)
-
+    conv.scatter_second()
+    small.scatter_end(1)
+    small.scatter_start(2)
+    lax.fori_loop(0, 3, back_tap, 0)
+    conv.scatter_third()
+    lax.fori_loop(3, 7, back_tap, 0)
+    conv.gather_third()
+    small.scatter_end(2)
+    small.gather_start(2)
+    lax.fori_loop(7, 9, back_tap, 0)
     def write_back(at, carry):
         cells = lat[pl.ds(at * COLS, COLS)].astype(F32)
         sigma = jax.nn.sigmoid(cells)
         slope = sigma * (1.0 + cells * (1.0 - sigma))
         value = resid_grad[pl.ds(at * COLS, COLS)].astype(F32) + acc[pl.ds(at * COLS, COLS)] * slope
-        latents_grad[pl.ds(at * COLS, COLS)] = value.astype(BF16)
+        latents_grad[at] = value.T.astype(BF16)
         return carry
 
     lax.fori_loop(0, ROWS, write_back, 0)
-    for part in (first, second):
-        part.arrive()
-        part.gather_start(1)
+    small.arrive()
+    small.gather_start(1)
+    conv.gather_rest()
+    small.arrive()
+    small.gather_start(0)
     small.arrive()
     small.core_back()
-    for part in (first, second):
-        part.arrive()
-        part.gather_start(0)
     small.arrive()
-
-    def small_out(at, carry):
-        unpack(small_total, at * MATRIX_TILES, small_sum, at * CHAN)
-        return carry
-
-    lax.fori_loop(0, 4, small_out, 0)
-    for part in (first, second):
-        part.arrive()
-        part.core_back()
-    for part in (first, second):
-        part.arrive()
-
-    def conv_out(at, carry):
-        unpack(conv_total, at * MATRIX_TILES, conv_sum, at * CHAN)
-        return carry
-
-    lax.fori_loop(0, 9, conv_out, 0)
-    gain_sum[...] = conv_total[GAIN_TILE : GAIN_TILE + 2]
-    for part in summers:
-        part.finish()
+    small.finish()
+    conv.finish()
     for swap in swaps:
         swap.finish()
     for copy in act_halo + grad_halo:
@@ -593,8 +808,9 @@
     dma = pltpu.SemaphoreType.DMA
     weight = vmem((CHAN, CHAN), BF16)
     shapes = [
+        vmem((ROWS, CHAN, COLS), BF16), vmem((ROWS, CHAN, COLS), BF16),
         vmem((ROWS * COLS, CHAN), BF16), vmem((ROWS * COLS, CHAN), BF16),
-        vmem((9, CHAN, CHAN), BF16), weight, weight, weight, weight, vmem((1, CHAN), F32), dma((8,)),
+        vmem((9, CHAN, CHAN), BF16), weight, weight, weight, weight, vmem((CHAN,), F32), dma((8,)),
         vmem((3, (ROWS + 2) * COLS, CHAN), BF16), vmem((2, 2, COLS, CHAN), BF16),
         dma((2, 2)), dma((2, 2)), vmem((2 * HALF, CHAN), F32), vmem((2, HALF, CHAN), BF16),
         vmem((3, CHAN, (ROWS + 2) * COLS), BF16),
@@ -605,57 +821,75 @@
     shapes += [vmem((3, 2 * HALF, CHAN), BF16), vmem((2, CHAN, 2 * HALF), BF16)]
     shapes += [vmem((ROWS * COLS, CHAN), BF16), vmem((3, (ROWS + 2) * COLS, CHAN), BF16)]
     shapes += [vmem((8, CHAN), F32)]
-    shapes += [vmem((CONV_TILES, 16, 128), BF16)] * 2 + [vmem((SMALL_TILES, 16, 128), BF16)] * 2
-    for order in ("xyz", "yxz", "zxy"):
-        shapes += summer_scratch(order, sizes)
-    return shapes
+    shapes += [vmem((CONV_TILES, 16, 128), BF16), vmem((SMALL_TILES, 16, 128), BF16)]
+    return shapes + summer_scratch("yxz", sizes) + conv_summer_scratch(sizes)
 
 
 def on_device(
     latents, conv_weight, query_weight, key_weight, value_weight, out_weight, norm_gain, out_grad
 ):
-    shape = latents.shape
-    cells = ROWS * COLS
     sizes = chip_sizes()
     frames = lax.axis_size("frame")
     anywhere = pl.BlockSpec(memory_space=pl.ANY)
     inside = pl.BlockSpec(memory_space=pltpu.VMEM)
-    block_out, latents_grad, conv_sum, small_sum, gain_sum = pl.pallas_call(
+    field = jax.ShapeDtypeStruct((ROWS, CHAN, COLS), BF16)
+    block_out, latents_grad, conv_sum, small_sum = pl.pallas_call(
         functools.partial(block_kernel, sizes),
         out_shape=[
-            jax.ShapeDtypeStruct((cells, CHAN), BF16),
-            jax.ShapeDtypeStruct((cells, CHAN), BF16),
-            jax.ShapeDtypeStruct((9 * CHAN, CHAN), BF16),
-            jax.ShapeDtypeStruct((4 * CHAN, CHAN), BF16),
-            jax.ShapeDtypeStruct((2, 16, 128), BF16),
+            field,
+            field,
+            jax.ShapeDtypeStruct((CONV_TILES, 16, 128), BF16),
+            jax.ShapeDtypeStruct((SMALL_TILES, 16, 128), BF16),
         ],
         in_specs=[anywhere] * 8,
-        out_specs=[inside] * 5,
+        out_specs=[inside] * 4,
         scratch_shapes=block_scratch(sizes, frames),
         compiler_params=pltpu.CompilerParams(
             collective_id=0, has_side_effects=True, vmem_limit_bytes=56 << 20
         ),
     )(
-        latents.reshape(cells, CHAN),
+        jnp.swapaxes(latents[0], 1, 2),
         conv_weight.reshape(9, CHAN, CHAN),
         query_weight,
         key_weight,
         value_weight,
         out_weight,
-        norm_gain.reshape(1, CHAN),
-        out_grad.reshape(cells, CHAN),
+        norm_gain,
+        jnp.swapaxes(out_grad[0], 1, 2),
     )
-    factor = (cells * frames * lax.axis_size("row")) ** (-0.5)
-    small = [
-        small_sum[at * CHAN : (at + 1) * CHAN].astype(F32) * factor for at in range(4)
-    ]
-    gains = jnp.concatenate([gain_sum[0, 0], gain_sum[0, 1], gain_sum[1, 0, :64]])
+    factor = (ROWS * COLS * frames * lax.axis_size("row")) ** (-0.5)
+    weight = jax.ShapeDtypeStruct((CHAN, CHAN), F32)
+    outs = pl.pallas_call(
+        functools.partial(finish_kernel, factor),
+        out_shape=[
+            field,
+            field,
+            jax.ShapeDtypeStruct((9, CHAN, CHAN), F32),
+            weight,
+            weight,
+            weight,
+            weight,
+            jax.ShapeDtypeStruct((CHAN,), F32),
+        ],
+        in_specs=[anywhere] * 4,
+        out_specs=[anywhere] * 7 + [inside],
+        scratch_shapes=[
+            pltpu.VMEM((CONV_TILES, 16, 128), BF16),
+            pltpu.VMEM((SMALL_TILES, 16, 128), BF16),
+            pltpu.VMEM((13, CHAN, CHAN), F32),
+            pltpu.VMEM((2, ROWS, CHAN, COLS), BF16),
+            pltpu.SemaphoreType.DMA((4,)),
+            pltpu.SemaphoreType.DMA((14,)),
+            pltpu.SemaphoreType.DMA((13,)),
+        ],
+        compiler_params=pltpu.CompilerParams(vmem_limit_bytes=56 << 20),
+    )(block_out, latents_grad, conv_sum, small_sum)
     return (
-        block_out.reshape(shape),
-        latents_grad.reshape(shape),
-        conv_sum.astype(F32).reshape(3, 3, CHAN, CHAN) * factor,
-        *small,
-        gains.astype(F32) * factor,
+        jnp.swapaxes(outs[0], 1, 2)[None],
+        jnp.swapaxes(outs[1], 1, 2)[None],
+        outs[2].reshape(3, 3, CHAN, CHAN),
+        *outs[3:7],
+        outs[7],
     )
 
 

time: 122 us -> 106 us (0.87)
  local copies, waits for them, and re-layouts: 10.3 us -> 0 us
  other arithmetic: 6 us -> 0 us
    unnamed x6 -> x0, local copies, waits for them, and re-layouts: 7.65 us -> none
    mul x3 -> x0, other arithmetic: 6 us -> none  [the longest x1 4.1 us: on_device(): conv_sum.astype(F32).reshape(3, 3, CHAN, CHAN) * factor]
    squeeze x2 -> x0, local copies, waits for them, and re-layouts: 1.41 us -> none  [the longest x1 0.75 us: on_device(): gain_sum[0, 0]]
    reshape x1 -> x0, local copies, waits for them, and re-layouts: 1.24 us -> none  [on_device(): norm_gain.reshape(1, CHAN)]
    pallas_call x1 -> x2, Pallas kernels: 104 us -> 105 us  [the longest x1 100 us: on_device(): pl.pallas_call(functools.partial(block_kernel, sizes), out_shape=[field,...]
where the time goes in v3:
time: 106 us
  Pallas kernels  105 us (99%)
    pallas_call x1, Pallas kernels, on_device(): pl.pallas_call(functools.partial(block_kernel, sizes), out_shape=[field,...  100 us
    pallas_call x1, Pallas kernels, on_device(): pl.pallas_call(functools.partial(finish_kernel, factor), out_shape=[field...  5.15 us

profile of v3, /device:TPU:1, one launch (start us, length us, event | category | flops | bytes accessed | tf_op | source)
XLA Modules:
  0.0 106.0 jit_solution(15591680743408779019)
XLA Ops:
  0.6 100.2 %shard_map.143 = (bf16[4,320,128]{2,1,0:T(8,128)(2,1)}, bf16[4,320,128]{2,1,0:T(8,128)(2,1)}, bf16[512,16,128]{2,1,0:T(8,128)(2,1)}, bf16[256,16,128]{2,1,0:T(8,128)(2,1)}) custom-call(bf16[4,320,128]{2,1,0:T(8,128)(2,1)} %bitcast.15, bf16[9,320,320]{2,1,0:T(8,128)(2,1)} %bitcast.14, bf16[320,320]{1,0:T(8,128)(2,1)} %query_w.1, bf16[320,320]{1,0:T(8,128)(2,1)} %key_w.1, ...), custom_call_target="tpu_custom_call" | custom-call | tf_op jit(solution)/shard_map/pallas_call | solution.py:836
  100.8 5.2 %shard_map.144 = (bf16[4,320,128]{2,1,0:T(8,128)(2,1)}, bf16[4,320,128]{2,1,0:T(8,128)(2,1)}, f32[9,320,320]{2,1,0:T(8,128)}, f32[320,320]{1,0:T(8,128)}, f32[32...) custom-call(bf16[4,320,128]{2,1,0:T(8,128)(2,1)} %get-tuple-element.20.block_in, ...), custom_call_target="tpu_custom_call" | custom-call | tf_op jit(solution)/shard_map/pallas_call | solution.py:862

commit v4 on v3

--- a/solution.py
+++ b/solution.py
@@ -18,7 +18,9 @@
 SMALL_TILES = 256
 PART = 256
 MATRIX_TILES = 50
-GAIN_TILE = 450
+GAIN_TILE = 230
+HALF_CHAN = 160
+HALF_TILES = 25
 BLOCK = 16
 F32 = jnp.float32
 BF16 = jnp.bfloat16
@@ -101,8 +103,8 @@
     def __init__(self, place, sizes, terms, total, scratch):
         self.place, self.sizes, self.terms, self.total = place, sizes, terms, total
         (
-            self.core_in, self.held0, self.inbox0, self.held1, self.inbox1, self.held2, self.inbox2,
-            self.core_sems, self.scatter0, self.scatter1, self.scatter2,
+            self.inbox0, self.held1, self.inbox1, self.held2, self.inbox2,
+            self.scatter0, self.scatter1, self.scatter2,
             self.gather2, self.gather1, self.gather0, self.back, self.sends,
         ) = scratch
         self.unit = PART // (2 * sizes["x"] * sizes["y"] * sizes["z"])
@@ -119,59 +121,33 @@
     def device(self, axis, step):
         return along(self.place, axis, step, self.sizes)
 
-    def tile(self, part, chunk, core, group, unit=0):
+    def local(self, part, chunk, group, unit=0):
         span = self.n2[part] * self.group
-        return part * PART + (chunk * 2 + core) * span + group * self.group + unit * self.unit
-
-    def core_start(self, piece):
-        n1, span = self.n1[0], self.n2[0] * self.group
-        start = piece * 2 * span + (1 - self.place["c"]) * span
-        remote(
-            self.terms.at[pl.ds(start, span)],
-            self.core_in.at[pl.ds(piece * span, span)],
-            self.sends.at[0],
-            self.core_sems.at[piece],
-            self.device("c", 1),
-        )
-
-    def core_wait(self, part, chunk):
-        span = self.n2[part] * self.group
-        wait_bytes(self.core_in.at[pl.ds(0, span)], self.core_sems.at[part * self.n1[part] + chunk])
-
-    def core_sum(self, part, chunk, group):
-        own = self.tile(part, chunk, self.place["c"], group)
-        there = (part * self.n1[part] + chunk) * self.n2[part] * self.group + group * self.group
-        total = self.terms[pl.ds(own, self.group)].astype(F32)
-        return total + self.core_in[pl.ds(there, self.group)].astype(F32)
-
-    def scatter_first(self):
+        return part * (PART // 2) + chunk * span + group * self.group + unit * self.unit
+
+    def tile(self, part, chunk, group, unit=0):
+        return self.place["c"] * PART + self.local(part, chunk, group, unit)
+
+    def scatter_first(self, part):
         for step2 in range(self.n2[0]):
             step2 = (step2 + 1) % self.n2[0]
             for step in range(1, self.n1[0]):
-                for part in range(2):
-                    chunk, group = self.peer(part, 0, step), self.peer(part, 1, step2)
-                    if step2 == 1:
-                        self.core_wait(part, chunk)
-                    slot = part * self.n1[part] * self.n2[part] + chunk * self.n2[part] + group
-                    held = self.held0.at[pl.ds(slot * self.group, self.group)]
-                    held[...] = self.core_sum(part, chunk, group).astype(BF16)
-                    remote(
-                        held,
-                        self.inbox0.at[part, group, pl.ds((step - 1) * self.group, self.group)],
-                        self.sends.at[1],
-                        self.scatter0.at[part, step2],
-                        self.device(self.ORDERS[part][0], step),
-                    )
+                chunk, group = self.peer(part, 0, step), self.peer(part, 1, step2)
+                remote(
+                    self.terms.at[pl.ds(self.local(part, chunk, group), self.group)],
+                    self.inbox0.at[part, group, pl.ds((step - 1) * self.group, self.group)],
+                    self.sends.at[part],
+                    self.scatter0.at[part, step2],
+                    self.device(self.ORDERS[part][0], step),
+                )
 
     def scatter_second(self):
         for step2 in range(self.n2[0]):
             step2 = (step2 + 1) % self.n2[0]
             for part in range(2):
                 chunk, group = self.at(part, 0), self.peer(part, 1, step2)
-                if step2 == 1:
-                    self.core_wait(part, chunk)
                 wait_bytes(self.inbox0.at[part, group], self.scatter0.at[part, step2])
-                total = self.core_sum(part, chunk, group)
+                total = self.terms[pl.ds(self.local(part, chunk, group), self.group)].astype(F32)
                 for step in range(self.n1[part] - 1):
                     span = pl.ds(step * self.group, self.group)
                     total = total + self.inbox0[part, group, span].astype(F32)
@@ -210,7 +186,7 @@
             total = self.held2[part, pl.ds(z * self.unit, self.unit)].astype(F32)
             for step in range(self.sizes["z"] - 1):
                 total = total + self.inbox2[part, pl.ds(step * self.unit, self.unit)].astype(F32)
-            mine = self.tile(part, self.at(part, 0), self.place["c"], self.at(part, 1), z)
+            mine = self.tile(part, self.at(part, 0), self.at(part, 1), z)
             self.total[pl.ds(mine, self.unit)] = total.astype(BF16)
             span = self.total.at[pl.ds(mine, self.unit)]
             for step in range(1, self.sizes["z"]):
@@ -219,11 +195,11 @@
                 )
 
     def spread(self, part, chunk, group, axis, steps, send, sem):
-        span = self.total.at[pl.ds(self.tile(part, chunk, self.place["c"], group), self.group)]
+        span = self.total.at[pl.ds(self.tile(part, chunk, group), self.group)]
         for step in steps:
             remote(span, span, self.sends.at[send], sem, self.device(axis, step))
 
-    def gather_rest(self):
+    def gather_rest(self, between):
         n1, n2 = self.n1[0], self.n2[0]
         for part in range(2):
             wait_bytes(
@@ -246,6 +222,7 @@
                     part, chunk, group, first, range(1, n1), 6, self.gather0.at[part, step2]
                 )
                 self.spread(part, chunk, group, "c", [1], 7, self.back.at[0])
+        between()
         for step2 in range(n2):
             for part in range(2):
                 wait_bytes(
@@ -260,7 +237,7 @@
         wait_bytes(self.total.at[pl.ds(0, PART)], self.back.at[0])
         n1, n2, nz = self.n1[0], self.n2[0], self.sizes["z"]
         counts = (
-            PART, 2 * n2 * (n1 - 1) * self.group, 2 * (n2 - 1) * self.group,
+            n2 * (n1 - 1) * self.group, n2 * (n1 - 1) * self.group, 2 * (n2 - 1) * self.group,
             2 * (nz - 1) * self.unit, 2 * (nz - 1) * self.unit, 2 * (n2 - 1) * self.group,
             2 * n2 * (n1 - 1) * self.group, PART,
         )
@@ -273,10 +250,10 @@
     group = unit * sizes["z"]
     n1, n2 = sizes["x"], sizes["y"]
     tiles = [
-        (PART,), (PART,), (2, n2, (n1 - 1) * group), (2, n2, group), (2, (n2 - 1) * group),
+        (2, n2, (n1 - 1) * group), (2, n2, group), (2, (n2 - 1) * group),
         (2, group), (2, (sizes["z"] - 1) * unit),
     ]
-    sems = [(2 * n1,), (2, n2), (2,), (2,), (2,), (2, n2), (2, n2), (1,), (8,)]
+    sems = [(2, n2), (2,), (2,), (2,), (2, n2), (2, n2), (1,), (8,)]
     return [pltpu.VMEM(shape + (16, 128), BF16) for shape in tiles] + [
         pltpu.SemaphoreType.DMA(shape) for shape in sems
     ]
@@ -384,6 +361,25 @@
     tiles[pl.ds(base + 40, 10)] = tail.reshape(10, 16, 128)
 
 
+def pack_half(matrix, tiles, base):
+    held = matrix.astype(BF16)
+    for block in range(2):
+        cut = held[:, block * 128 : block * 128 + 128]
+        tiles[pl.ds(base + 10 * block, 10)] = cut.reshape(10, 16, 128)
+    tail = jnp.concatenate([held[:80, 256:], held[80:, 256:]], axis=1)
+    tiles[pl.ds(base + 20, 5)] = tail.reshape(5, 16, 128)
+
+
+def unpack_half(tiles, base, target, at, row, factor):
+    span = pl.ds(row, HALF_CHAN)
+    for block in range(2):
+        cut = tiles[pl.ds(base + 10 * block, 10)].reshape(HALF_CHAN, 128)
+        target[at, span, block * 128 : block * 128 + 128] = cut.astype(F32) * factor
+    tail = tiles[pl.ds(base + 20, 5)].reshape(80, 128).astype(F32) * factor
+    target[at, pl.ds(row, 80), 256:] = tail[:, :64]
+    target[at, pl.ds(row + 80, 80), 256:] = tail[:, 64:]
+
+
 def unpack(tiles, base, target, at, factor):
     for block in range(2):
         cut = tiles[pl.ds(base + 20 * block, 20)].reshape(CHAN, 128)
@@ -412,30 +408,32 @@
 
     for at in range(4):
         pltpu.make_async_copy(*load(at, small_in, small), load_sems.at[9 + at]).start()
-    for at in range(9):
-        pltpu.make_async_copy(*load(at, conv_in, conv), load_sems.at[at]).start()
-    last = pl.ds(GAIN_TILE, 2)
-    gain_load = pltpu.make_async_copy(conv_in.at[last], conv.at[last], load_sems.at[13])
-    gain_load.start()
+    conv_load = pltpu.make_async_copy(conv_in, conv, load_sems.at[0])
+    conv_load.start()
     for at in range(4):
         pltpu.make_async_copy(*load(at, small_in, small), load_sems.at[9 + at]).wait()
         unpack(small, at * MATRIX_TILES, wide, 9 + at, factor)
         pltpu.make_async_copy(wide.at[9 + at], small_outs[at], store_sems.at[9 + at]).start()
 
     def conv_tap(at, carry):
-        pltpu.make_async_copy(*load(at, conv_in, conv), load_sems.at[at]).wait()
-        unpack(conv, at * MATRIX_TILES, wide, at, factor)
+        for core in range(2):
+            start = core * PART + at * HALF_TILES
+            unpack_half(conv, start, wide, at, core * HALF_CHAN, factor)
         pltpu.make_async_copy(wide.at[at], conv_out.at[at], store_sems.at[at]).start()
         return carry
 
     for move in moves:
         move[0].wait()
         move[1].start()
+    conv_load.wait()
     lax.fori_loop(0, 9, conv_tap, 0)
-    gain_load.wait()
-    gain_out[0:128] = (conv[GAIN_TILE].astype(F32) * factor)[0]
-    gain_out[128:256] = (conv[GAIN_TILE].astype(F32) * factor)[1]
-    gain_out[256:] = (conv[GAIN_TILE + 1].astype(F32) * factor)[0, :64]
+    pieces = []
+    for at in range(2):
+        tiles = [conv[core * PART + GAIN_TILE + at].astype(F32) for core in range(2)]
+        pieces.append((tiles[0] + tiles[1]) * factor)
+    gain_out[0:128] = pieces[0][0]
+    gain_out[128:256] = pieces[0][1]
+    gain_out[256:] = pieces[1][0, :64]
     for move in moves:
         move[1].wait()
     for at in range(9):
@@ -449,6 +447,30 @@
     left = jnp.where(column == 0, 0.0, pltpu.roll(cells, 1, 0))
     right = jnp.where(column == COLS - 1, 0.0, pltpu.roll(cells, COLS - 1, 0))
     return [left, cells, right]
+
+
+def store_chunks(target, half, at, cells):
+    count = cells.shape[0] // 16
+    span = pl.ds(at, count)
+    for block in range(2):
+        cut = cells[:, block * 128 : block * 128 + 128].reshape(count, 16, 128)
+        target[half, span, 16 * block : 16 * block + 16] = cut
+    tail = cells[:, 256:].astype(F32).reshape(count, 2, 8, 64)
+    low, high = tail[:, 0].reshape(count * 8, 64), tail[:, 1].reshape(count * 8, 64)
+    tail = jnp.concatenate([low, high], axis=1).reshape(count, 8, 128)
+    target[half, span, 32:40] = tail.astype(BF16)
+
+
+def load_chunks(source, half, at, count, target):
+    span = pl.ds(at, count)
+    for block in range(2):
+        cut = source[half, span, 16 * block : 16 * block + 16].reshape(16 * count, 128)
+        target[:, block * 128 : block * 128 + 128] = cut
+    tail = source[half, span, 32:40].astype(F32).reshape(count * 8, 128)
+    low = tail[:, :64].reshape(count, 1, 8, 64)
+    high = tail[:, 64:].reshape(count, 1, 8, 64)
+    tail = jnp.concatenate([low, high], axis=1).reshape(16 * count, 64)
+    target[:, 256:] = tail.astype(BF16)
 
 
 class Swap:
@@ -487,28 +509,50 @@
     return jnp.where(at < 2, at * 64, HALF + at * 64)
 
 
-def attention(q_s, k_s, v_s, d_s, bias, mixed_s, qp_s, kp_s, vp_s):
-    lane = lax.broadcasted_iota(jnp.int32, (1, 128), 1)
-    low = lane < 64
-    masks = [jnp.where(low, 1.0, 0.0).astype(BF16), jnp.where(low, 0.0, 1.0).astype(BF16)]
+def head_masks():
+    low = lax.broadcasted_iota(jnp.int32, (1, 128), 1) < 64
+    return low, [jnp.where(low, 1.0, 0.0).astype(BF16), jnp.where(low, 0.0, 1.0).astype(BF16)]
+
+
+def attend(q_s, k_s, v_s, bias, probs_s, mixed_s):
+    low, masks = head_masks()
+
+    def tile(at, carry):
+        span = pl.ds(pl.multiple_of(at * 128, 128), 128)
+        queries, keys, values = q_s[:, span], k_s[:, span], v_s[:, span]
+        found = []
+        for head, mask in enumerate(masks):
+            scores = dot_nt(queries * mask, keys) * 0.125 + bias[...]
+            expo = jnp.exp(scores)
+            probs = expo * (1.0 / jnp.sum(expo, axis=-1, keepdims=True))
+            probs_s[2 * at + head] = probs
+            found.append(dot(probs.astype(BF16), values))
+        mixed_s[:, span] = jnp.where(low, *found).astype(BF16)
+        return carry
+
+    lax.fori_loop(0, 3, tile, 0)
+
+
+def attend_back(q_s, k_s, v_s, d_s, probs_s, qp_s, kp_s, vp_s):
+    low, masks = head_masks()
 
     def tile(at, carry):
         span = pl.ds(pl.multiple_of(at * 128, 128), 128)
         queries, keys, values, grads = q_s[:, span], k_s[:, span], v_s[:, span], d_s[:, span]
         found = []
-        for mask in masks:
-            scores = dot_nt(queries * mask, keys) * 0.125 + bias[...]
-            expo = jnp.exp(scores)
-            probs = expo * (1.0 / jnp.sum(expo, axis=-1, keepdims=True))
-            probs_b = probs.astype(BF16)
-            mixed = dot(probs_b, values)
+        for head, mask in enumerate(masks):
+            probs = probs_s[2 * at + head]
             prob_grad = dot_nt(grads * mask, values)
             inner = jnp.sum(probs * prob_grad, axis=-1, keepdims=True)
             score_b = (probs * (prob_grad - inner) * 0.125).astype(BF16)
             found.append(
-                (mixed, dot(score_b, keys), dot_tn(score_b, queries), dot_tn(probs_b, grads))
+                (
+                    dot(score_b, keys),
+                    dot_tn(score_b, queries),
+                    dot_tn(probs.astype(BF16), grads),
+                )
             )
-        for target, first, second in zip((mixed_s, qp_s, kp_s, vp_s), *found):
+        for target, first, second in zip((qp_s, kp_s, vp_s), *found):
             target[:, span] = jnp.where(low, first, second).astype(BF16)
         return carry
 
@@ -519,12 +563,13 @@
     (block_out, latents_grad, conv_total, small_total), refs = refs[:4], refs[4:]
     (
         lat_in, grad_in, lat, grad, weights, wq, wk, wv, wo, gain_v, in_sems,
-        padded, halo, halo_send, halo_recv, acc, resid, act_t,
+        padded, halo, halo_send, halo_recv, acc, resid, act_c, act_in, act_t,
         normed_out, normed_in, og_out, og_in, ng_out, ng_in, mix_out, mix_in,
         swap_send, swap_recv,
-        q_s, k_s, v_s, d_s, bias, mixed_s, qp_s, kp_s, vp_s, parts, flip,
-        resid_grad, grad_pad, gain_acc, conv_terms, small_terms,
-    ), refs = refs[:44], refs[44:]
+        og_n, normed_n, mixed_n, back_n,
+        q_s, k_s, v_s, d_s, bias, probs_s, out_acc, mixed_s, qp_s, kp_s, vp_s, parts, flip,
+        resid_grad, rg_in, conv_acc, pair_send, pair_recv, grad_pad, gain_acc, conv_terms, small_terms,
+    ), refs = refs[:56], refs[56:]
     frames = lax.axis_size("frame")
     rows_n = lax.axis_size("row")
     chunk = HALF // frames
@@ -565,6 +610,16 @@
         return carry
 
     lax.fori_loop(0, ROWS, activate, 0)
+    loads[1].wait()
+
+    def flip_grad(at, carry):
+        cells = grad_in[at].astype(F32).T.astype(BF16)
+        grad[pl.ds(at * COLS, COLS)] = cells
+        half = jnp.where((at == 0) | (at == ROWS - 1), 1, 0)
+        store_chunks(og_out, half, jnp.where(at >= 2, 8, 0), cells)
+        return carry
+
+    lax.fori_loop(0, ROWS, flip_grad, 0)
     pl.semaphore_wait(barrier, len(partners))
 
     def halo_start(source, kind):
@@ -593,18 +648,6 @@
         swaps.append(Swap(source, target, swap_send.at[at], swap_recv.at[at], peers, me))
     og_swap, normed_swap, ng_swap, mix_swap = swaps
 
-    loads[1].wait()
-
-    def flip_grad(at, carry):
-        grad[pl.ds(at * COLS, COLS)] = grad_in[at].astype(F32).T.astype(BF16)
-        return carry
-
-    lax.fori_loop(0, ROWS, flip_grad, 0)
-    og_out[0] = grad[COLS : COLS + HALF].reshape(frames, chunk, CHAN)
-    og_out[1, : frames // 2] = grad[:COLS].reshape(frames // 2, chunk, CHAN)
-    og_out[1, frames // 2 :] = grad[COLS + HALF :].reshape(frames // 2, chunk, CHAN)
-    og_swap.start(0)
-    og_swap.start(1)
     loads[2].wait()
     loads[3].wait()
 
@@ -631,16 +674,18 @@
             resid[half, pl.ds(at * 64, 64)] = held
             held = held.astype(F32)
             normed = (held * norm_of(held) * gain_v[...].reshape(1, CHAN)).astype(BF16)
-            normed_out[half, pl.ds(at * count, count)] = normed.reshape(count, chunk, CHAN)
+            store_chunks(normed_out, half, at * count, normed)
             return carry
 
         lax.fori_loop(0, 4, finish, 0)
 
+    og_swap.start(0)
     conv_half(0)
     normed_swap.start(0)
     halo_end(act_halo, 0, padded)
     conv_half(1)
     normed_swap.start(1)
+    og_swap.start(1)
 
     position = lax.broadcasted_iota(jnp.int32, (HALF, HALF), 0)
     other = lax.broadcasted_iota(jnp.int32, (HALF, HALF), 1)
@@ -648,35 +693,59 @@
     bias[...] = jnp.where(same, 0.0, -1e30)
     for field in (q_s, k_s, v_s, d_s):
         field[:, 256:] = jnp.zeros((HALF, 128), BF16)
-    for shift in range(3):
-        act_t[shift] = padded[shift].astype(F32).T.astype(BF16)
+    act_c[...] = padded[1].astype(F32).T.astype(BF16)
+    core = place["c"]
+    partner = along(place, "c", 1, sizes)
+    mine = pl.ds(pl.multiple_of(core * HALF_CHAN, HALF_CHAN), HALF_CHAN)
+    theirs = pl.ds(pl.multiple_of((1 - core) * HALF_CHAN, HALF_CHAN), HALF_CHAN)
+    pair = [remote(act_c.at[theirs], act_in, pair_send.at[0], pair_recv.at[0], partner)]
+
+    def shift_lanes(at, carry, source, side):
+        span = pl.ds(pl.multiple_of(at * COLS, COLS), COLS)
+        cells = source[:, span].astype(F32)
+        column = lax.broadcasted_iota(jnp.int32, cells.shape, 1)
+        left = jnp.where(column == 0, 0.0, pltpu.roll(cells, 1, 1))
+        right = jnp.where(column == COLS - 1, 0.0, pltpu.roll(cells, COLS - 1, 1))
+        for shift, copy in enumerate((left, cells, right)):
+            act_t[side, shift, :, span] = copy.astype(BF16)
+        return carry
+
+    own_rows = functools.partial(shift_lanes, source=act_c.at[mine], side=0)
+    lax.fori_loop(0, ROWS + 2, own_rows, 0)
     for load in loads[4:]:
         load.wait()
 
     for half in range(2):
+        normed_swap.wait(half)
+        load_chunks(normed_in, half, 0, frames, normed_n.at[half])
+        q_s[:, :CHAN] = dot(normed_n[half], wq[...]).astype(BF16)
+        k_s[:, :CHAN] = dot(normed_n[half], wk[...]).astype(BF16)
+        v_s[:, :CHAN] = dot(normed_n[half], wv[...]).astype(BF16)
+        attend(q_s, k_s, v_s, bias, probs_s, mixed_s)
+        mixed_n[half] = mixed_s[:, :CHAN]
+        store_chunks(mix_out, half, 0, mixed_s[:, :CHAN])
         og_swap.wait(half)
-        d_s[:, :CHAN] = dot_nt(og_in[half].reshape(HALF, CHAN), wo[...]).astype(BF16)
-        normed_swap.wait(half)
-        normed = normed_in[half].reshape(HALF, CHAN)
-        q_s[:, :CHAN] = dot(normed, wq[...]).astype(BF16)
-        k_s[:, :CHAN] = dot(normed, wk[...]).astype(BF16)
-        v_s[:, :CHAN] = dot(normed, wv[...]).astype(BF16)
-        attention(q_s, k_s, v_s, d_s, bias, mixed_s, qp_s, kp_s, vp_s)
+        load_chunks(og_in, half, 0, frames, og_n.at[half])
+        d_s[:, :CHAN] = dot_nt(og_n[half], wo[...]).astype(BF16)
+        attend_back(q_s, k_s, v_s, d_s, probs_s, qp_s, kp_s, vp_s)
         back = dot_nt(qp_s[:, :CHAN], wq[...])
         back = back + dot_nt(kp_s[:, :CHAN], wk[...])
         back = back + dot_nt(vp_s[:, :CHAN], wv[...])
-        ng_out[half] = back.astype(BF16).reshape(frames, chunk, CHAN)
+        store_chunks(ng_out, half, 0, back.astype(BF16))
         ng_swap.start(half)
-        mix_out[half] = mixed_s[:, :CHAN].reshape(frames, chunk, CHAN)
-        mix_swap.start(half)
         for at, field in enumerate((qp_s, kp_s, vp_s)):
             parts[at, pl.ds(half * HALF, HALF)] = field[:, :CHAN]
 
-    flip[0] = normed_in[...].reshape(2 * HALF, CHAN).astype(F32).T.astype(BF16)
-    flip[1] = mix_out[...].reshape(2 * HALF, CHAN).astype(F32).T.astype(BF16)
+    mix_swap.start(0)
+    mix_swap.start(1)
+    pair[0].wait_recv()
+    other_rows = functools.partial(shift_lanes, source=act_in, side=1)
+    lax.fori_loop(0, ROWS + 2, other_rows, 0)
+    flip[0] = normed_n[...].reshape(2 * HALF, CHAN).astype(F32).T.astype(BF16)
+    flip[1] = mixed_n[...].reshape(2 * HALF, CHAN).astype(F32).T.astype(BF16)
     for at in range(3):
         pack(dot(flip[0], parts[at]), small_terms, at * MATRIX_TILES)
-    pack(dot(flip[1], og_in[...].reshape(2 * HALF, CHAN)), small_terms, 3 * MATRIX_TILES)
+    pack(dot(flip[1], og_n[...].reshape(2 * HALF, CHAN)), small_terms, 3 * MATRIX_TILES)
     spare = SMALL_TILES - 4 * MATRIX_TILES
     small_terms[pl.ds(4 * MATRIX_TILES, spare)] = jnp.zeros((spare, 16, 128), BF16)
 
@@ -687,12 +756,12 @@
     gain_acc[...] = jnp.zeros((8, CHAN), F32)
     for half in range(2):
         ng_swap.wait(half)
+        load_chunks(ng_in, half, 0, frames, back_n)
 
         def undo_norm(at, carry, half=half):
-            count = 64 // chunk
             begin = pl.multiple_of(cell_start(half, at), 64)
             held = resid[half, pl.ds(at * 64, 64)].astype(F32)
-            back = ng_in[half, pl.ds(at * count, count)].reshape(64, CHAN).astype(F32)
+            back = back_n[pl.ds(at * 64, 64)].astype(F32)
             inv = norm_of(held)
             product = back * held
             total = jnp.sum((product * inv).reshape(8, 8, CHAN), axis=0)
@@ -702,61 +771,91 @@
             value = grad[pl.ds(begin, 64)].astype(F32) + (
                 inv * tangent - held * (inv * inv * inv) * mean
             )
-            resid_grad[pl.ds(begin, 64)] = value.astype(BF16)
+            resid_grad[half, pl.ds(at * 64, 64)] = value.astype(BF16)
             return carry
 
         lax.fori_loop(0, 4, undo_norm, 0)
-    small.core_end()
-    small.scatter_start(0)
+        pair.append(
+            remote(
+                resid_grad.at[half],
+                rg_in.at[half],
+                pair_send.at[1 + half],
+                pair_recv.at[1 + half],
+                partner,
+            )
+        )
+        if half == 0:
+            pair[1].wait_recv()
+
+            def first_taps(at, carry):
+                a, b = at // 3, lax.rem(at, 3)
+                span = pl.ds(pl.multiple_of((a + 1) * COLS, COLS), HALF)
+                conv_acc[at] = dot(act_t[0, b, :, span], resid_grad[0]) + dot(
+                    act_t[1, b, :, span], rg_in[0]
+                )
+                return carry
+
+            lax.fori_loop(0, 9, first_taps, 0)
+            small.core_end()
+            small.scatter_start(0)
 
     def pad_grad(at, carry):
-        cells = resid_grad[pl.ds(at * COLS, COLS)].astype(F32)
+        half = jnp.where((at == 0) | (at == ROWS - 1), 1, 0)
+        side = jnp.where(at >= 2, 1, 0)
+        cells = resid_grad[half, pl.ds(side * COLS, COLS)].astype(F32)
         for shift, copy in enumerate(shifts(cells)):
             grad_pad[shift, pl.ds((at + 1) * COLS, COLS)] = copy.astype(BF16)
         return carry
 
+    def edge_cells(side, b, a):
+        spans = [pl.ds(pl.multiple_of((a + gap) * COLS, COLS), COLS) for gap in (0, ROWS - 1)]
+        return jnp.concatenate([act_t[side, b, :, span] for span in spans], axis=1)
+
+    def second_taps(at, carry):
+        a, b = at // 3, lax.rem(at, 3)
+        conv_acc[at] += dot(edge_cells(0, b, a), resid_grad[1])
+        return carry
+
+    lax.fori_loop(0, 9, second_taps, 0)
     lax.fori_loop(0, ROWS, pad_grad, 0)
     grad_halo = halo_start(grad_pad.at[1], 1)
 
-    span = 2 * (PART // 8)
-    spare = CONV_TILES - GAIN_TILE
-    conv_terms[pl.ds(GAIN_TILE, spare)] = jnp.zeros((spare, 16, 128), BF16)
+    spare = PART - 9 * HALF_TILES
+    conv_terms[pl.ds(9 * HALF_TILES, spare)] = jnp.zeros((spare, 16, 128), BF16)
     gains = jnp.sum(gain_acc[...], axis=0, keepdims=True)
     line = lax.broadcasted_iota(jnp.int32, (16, 128), 0)
     gain_tile = jnp.where(line == 0, gains[:, :128], jnp.where(line == 1, gains[:, 128:256], 0.0))
     conv_terms[GAIN_TILE] = gain_tile.astype(BF16)
     tail = jnp.where(line[:, :64] == 0, gains[:, 256:], 0.0)
     conv_terms[GAIN_TILE + 1, :, :64] = tail.astype(BF16)
-
-    def conv_tap(at, carry):
+    pair[2].wait_recv()
+
+    def last_taps(at, carry):
         a, b = at // 3, lax.rem(at, 3)
-        cells = act_t[b, :, pl.ds(pl.multiple_of(a * COLS, COLS), ROWS * COLS)]
-        pack(dot(cells, resid_grad[...]), conv_terms, at * MATRIX_TILES)
-        done = ((at + 1) * MATRIX_TILES) // span
-
-        @pl.when(done > (at * MATRIX_TILES) // span)
-        def _():
-            conv.core_start(done - 1)
-
-        return carry
-
-    lax.fori_loop(0, 9, conv_tap, 0)
-    conv.core_start(7)
-    conv.scatter_first()
+        total = conv_acc[at] + dot(edge_cells(1, b, a), rg_in[1])
+        pack_half(total, conv_terms, at * HALF_TILES)
+        return carry
+
+    lax.fori_loop(0, 6, last_taps, 0)
+    conv.scatter_first(0)
+    lax.fori_loop(6, 9, last_taps, 0)
+    conv.scatter_first(1)
     small.scatter_end(0)
     small.scatter_start(1)
-    for half in range(2):
+
+    def project_out(half):
         mix_swap.wait(half)
-        acc[pl.ds(0, HALF)] = dot(mix_in[half].reshape(HALF, CHAN), wo[...])
-
-        def write_out(at, carry, half=half):
+        load_chunks(mix_in, half, 0, frames, back_n)
+        out_acc[...] = dot(back_n[...], wo[...])
+
+        def write_out(at, carry):
             held = resid[half, pl.ds(at * COLS, COLS)].astype(F32)
-            total = held + acc[pl.ds(at * COLS, COLS)]
-            row_at = at + 1 if half == 0 else at * 3
-            block_out[row_at] = total.T.astype(BF16)
+            total = held + out_acc[pl.ds(at * COLS, COLS)]
+            block_out[at + 1 if half == 0 else at * 3] = total.T.astype(BF16)
             return carry
 
         lax.fori_loop(0, 2, write_out, 0)
+
     halo_end(grad_halo, 1, grad_pad)
     acc[...] = jnp.zeros((2 * HALF, CHAN), F32)
 
@@ -766,44 +865,48 @@
         acc[...] += dot_nt(cells, weights[at])
         return carry
 
-    conv.scatter_second()
+    lax.fori_loop(0, 5, back_tap, 0)
     small.scatter_end(1)
     small.scatter_start(2)
-    lax.fori_loop(0, 3, back_tap, 0)
-    conv.scatter_third()
-    lax.fori_loop(3, 7, back_tap, 0)
-    conv.gather_third()
+    conv.scatter_second()
     small.scatter_end(2)
     small.gather_start(2)
-    lax.fori_loop(7, 9, back_tap, 0)
+    project_out(0)
+    project_out(1)
+    conv.scatter_third()
+    small.arrive()
+    small.gather_start(1)
+    lax.fori_loop(5, 9, back_tap, 0)
+    conv.gather_third()
+    small.arrive()
+    small.gather_start(0)
     def write_back(at, carry):
         cells = lat[pl.ds(at * COLS, COLS)].astype(F32)
         sigma = jax.nn.sigmoid(cells)
         slope = sigma * (1.0 + cells * (1.0 - sigma))
-        value = resid_grad[pl.ds(at * COLS, COLS)].astype(F32) + acc[pl.ds(at * COLS, COLS)] * slope
+        half = jnp.where((at == 0) | (at == ROWS - 1), 1, 0)
+        side = jnp.where(at >= 2, 1, 0)
+        value = resid_grad[half, pl.ds(side * COLS, COLS)].astype(F32) + acc[pl.ds(at * COLS, COLS)] * slope
         latents_grad[at] = value.T.astype(BF16)
         return carry
 
     lax.fori_loop(0, ROWS, write_back, 0)
-    small.arrive()
-    small.gather_start(1)
-    conv.gather_rest()
-    small.arrive()
-    small.gather_start(0)
-    small.arrive()
-    small.core_back()
+    def return_small():
+        small.arrive()
+        small.core_back()
+
+    conv.gather_rest(return_small)
     small.arrive()
     small.finish()
     conv.finish()
     for swap in swaps:
         swap.finish()
-    for copy in act_halo + grad_halo:
+    for copy in act_halo + grad_halo + pair:
         copy.wait_send()
 
 
 def block_scratch(sizes, frames):
-    chunk = HALF // frames
-    field = (2, frames, chunk, CHAN)
+    field = (2, frames, 40, 128)
     vmem = pltpu.VMEM
     dma = pltpu.SemaphoreType.DMA
     weight = vmem((CHAN, CHAN), BF16)
@@ -813,15 +916,20 @@
         vmem((9, CHAN, CHAN), BF16), weight, weight, weight, weight, vmem((CHAN,), F32), dma((8,)),
         vmem((3, (ROWS + 2) * COLS, CHAN), BF16), vmem((2, 2, COLS, CHAN), BF16),
         dma((2, 2)), dma((2, 2)), vmem((2 * HALF, CHAN), F32), vmem((2, HALF, CHAN), BF16),
-        vmem((3, CHAN, (ROWS + 2) * COLS), BF16),
+        vmem((CHAN, (ROWS + 2) * COLS), BF16), vmem((HALF_CHAN, (ROWS + 2) * COLS), BF16),
+        vmem((2, 3, HALF_CHAN, (ROWS + 2) * COLS), BF16),
     ]
     shapes += [vmem(field, BF16)] * 8 + [dma((4, 2)), dma((4, 2))]
+    shapes += [vmem((2, HALF, CHAN), BF16)] * 3 + [vmem((HALF, CHAN), BF16)]
     shapes += [vmem((HALF, WIDE), BF16)] * 4 + [vmem((HALF, HALF), F32)]
+    shapes += [vmem((6, HALF, HALF), F32), vmem((HALF, CHAN), F32)]
     shapes += [vmem((HALF, WIDE), BF16)] * 4
     shapes += [vmem((3, 2 * HALF, CHAN), BF16), vmem((2, CHAN, 2 * HALF), BF16)]
-    shapes += [vmem((ROWS * COLS, CHAN), BF16), vmem((3, (ROWS + 2) * COLS, CHAN), BF16)]
+    shapes += [vmem((2, HALF, CHAN), BF16), vmem((2, HALF, CHAN), BF16)]
+    shapes += [vmem((9, HALF_CHAN, CHAN), F32), dma((3,)), dma((3,))]
+    shapes += [vmem((3, (ROWS + 2) * COLS, CHAN), BF16)]
     shapes += [vmem((8, CHAN), F32)]
-    shapes += [vmem((CONV_TILES, 16, 128), BF16), vmem((SMALL_TILES, 16, 128), BF16)]
+    shapes += [vmem((PART, 16, 128), BF16), vmem((SMALL_TILES, 16, 128), BF16)]
     return shapes + summer_scratch("yxz", sizes) + conv_summer_scratch(sizes)
 
 

time: 106 us -> 96.4 us (0.909)
  Pallas kernels: 105 us -> 95.6 us
    pallas_call x1, Pallas kernels: 100 us -> 90.1 us  [on_device(): pl.pallas_call(functools.partial(block_kernel, sizes), out_shape=[field,...]
where the time goes in v4:
time: 96.4 us; the launch traced here: 96.3 us
  Pallas kernels  95.6 us (99%)
    pallas_call x1, Pallas kernels, on_device(): pl.pallas_call(functools.partial(block_kernel, sizes), out_shape=[field,...  90.1 us
    pallas_call x1, Pallas kernels, on_device(): pl.pallas_call(functools.partial(finish_kernel, factor), out_shape=[field...  5.56 us

profile of v4, /device:TPU:1, one launch (start us, length us, event | category | flops | bytes accessed | tf_op | source)
XLA Modules:
  0.0 96.3 jit_solution(17656779149769044405)
XLA Ops:
  0.6 90.1 %shard_map.143 = (bf16[4,320,128]{2,1,0:T(8,128)(2,1)}, bf16[4,320,128]{2,1,0:T(8,128)(2,1)}, bf16[512,16,128]{2,1,0:T(8,128)(2,1)}, bf16[256,16,128]{2,1,0:T(8,128)(2,1)}) custom-call(bf16[4,320,128]{2,1,0:T(8,128)(2,1)} %bitcast.15, bf16[9,320,320]{2,1,0:T(8,128)(2,1)} %bitcast.14, bf16[320,320]{1,0:T(8,128)(2,1)} %query_w.1, bf16[320,320]{1,0:T(8,128)(2,1)} %key_w.1, ...), custom_call_target="tpu_custom_call" | custom-call | tf_op jit(solution)/shard_map/pallas_call | solution.py:944
  90.7 5.6 %shard_map.144 = (bf16[4,320,128]{2,1,0:T(8,128)(2,1)}, bf16[4,320,128]{2,1,0:T(8,128)(2,1)}, f32[9,320,320]{2,1,0:T(8,128)}, f32[320,320]{1,0:T(8,128)}, f32[32...) custom-call(bf16[4,320,128]{2,1,0:T(8,128)(2,1)} %get-tuple-element.20.block_in, ...), custom_call_target="tpu_custom_call" | custom-call | tf_op jit(solution)/shard_map/pallas_call | solution.py:970

commit v5 on v4

--- a/solution.py
+++ b/solution.py
@@ -233,8 +233,10 @@
                     chunk = self.peer(part, 0, n1 - step)
                     self.spread(part, chunk, group, "c", [1], 7, self.back.at[0])
 
+    def back_wait(self):
+        wait_bytes(self.total.at[pl.ds(0, PART)], self.back.at[0])
+
     def finish(self):
-        wait_bytes(self.total.at[pl.ds(0, PART)], self.back.at[0])
         n1, n2, nz = self.n1[0], self.n2[0], self.sizes["z"]
         counts = (
             n2 * (n1 - 1) * self.group, n2 * (n1 - 1) * self.group, 2 * (n2 - 1) * self.group,
@@ -391,7 +393,7 @@
 
 def finish_kernel(factor, block_in, back_in, conv_in, small_in, *refs):
     (block_out, back_out, conv_out), small_outs, gain_out = refs[:3], refs[3:7], refs[7]
-    conv, small, wide, fields, through, load_sems, store_sems = refs[8:]
+    conv, small, wide, fields, through, load_sems, half_sems, store_sems = refs[8:]
     moves = []
     for at, (source, target) in enumerate(((block_in, block_out), (back_in, back_out))):
         moves.append(
@@ -408,8 +410,20 @@
 
     for at in range(4):
         pltpu.make_async_copy(*load(at, small_in, small), load_sems.at[9 + at]).start()
-    conv_load = pltpu.make_async_copy(conv_in, conv, load_sems.at[0])
-    conv_load.start()
+    def load_half(at, core):
+        span = pl.ds(core * PART + at * HALF_TILES, HALF_TILES)
+        return pltpu.make_async_copy(conv_in.at[span], conv.at[span], half_sems.at[at, core])
+
+    for at in range(9):
+        for core in range(2):
+            load_half(at, core).start()
+    gain_loads = []
+    for core in range(2):
+        span = pl.ds(core * PART + GAIN_TILE, 2)
+        gain_loads.append(
+            pltpu.make_async_copy(conv_in.at[span], conv.at[span], half_sems.at[9, core])
+        )
+        gain_loads[-1].start()
     for at in range(4):
         pltpu.make_async_copy(*load(at, small_in, small), load_sems.at[9 + at]).wait()
         unpack(small, at * MATRIX_TILES, wide, 9 + at, factor)
@@ -417,6 +431,7 @@
 
     def conv_tap(at, carry):
         for core in range(2):
+            load_half(at, core).wait()
             start = core * PART + at * HALF_TILES
             unpack_half(conv, start, wide, at, core * HALF_CHAN, factor)
         pltpu.make_async_copy(wide.at[at], conv_out.at[at], store_sems.at[at]).start()
@@ -425,8 +440,9 @@
     for move in moves:
         move[0].wait()
         move[1].start()
-    conv_load.wait()
     lax.fori_loop(0, 9, conv_tap, 0)
+    for copy in gain_loads:
+        copy.wait()
     pieces = []
     for at in range(2):
         tiles = [conv[core * PART + GAIN_TILE + at].astype(F32) for core in range(2)]
@@ -449,30 +465,6 @@
     return [left, cells, right]
 
 
-def store_chunks(target, half, at, cells):
-    count = cells.shape[0] // 16
-    span = pl.ds(at, count)
-    for block in range(2):
-        cut = cells[:, block * 128 : block * 128 + 128].reshape(count, 16, 128)
-        target[half, span, 16 * block : 16 * block + 16] = cut
-    tail = cells[:, 256:].astype(F32).reshape(count, 2, 8, 64)
-    low, high = tail[:, 0].reshape(count * 8, 64), tail[:, 1].reshape(count * 8, 64)
-    tail = jnp.concatenate([low, high], axis=1).reshape(count, 8, 128)
-    target[half, span, 32:40] = tail.astype(BF16)
-
-
-def load_chunks(source, half, at, count, target):
-    span = pl.ds(at, count)
-    for block in range(2):
-        cut = source[half, span, 16 * block : 16 * block + 16].reshape(16 * count, 128)
-        target[:, block * 128 : block * 128 + 128] = cut
-    tail = source[half, span, 32:40].astype(F32).reshape(count * 8, 128)
-    low = tail[:, :64].reshape(count, 1, 8, 64)
-    high = tail[:, 64:].reshape(count, 1, 8, 64)
-    tail = jnp.concatenate([low, high], axis=1).reshape(16 * count, 64)
-    target[:, 256:] = tail.astype(BF16)
-
-
 class Swap:
     def __init__(self, source, target, send_sems, recv_sems, peers, me):
         self.source, self.target, self.peers, self.me = source, target, peers, me
@@ -511,40 +503,47 @@
 
 def head_masks():
     low = lax.broadcasted_iota(jnp.int32, (1, 128), 1) < 64
-    return low, [jnp.where(low, 1.0, 0.0).astype(BF16), jnp.where(low, 0.0, 1.0).astype(BF16)]
+    return low, [jnp.where(low, 0.125, 0.0).astype(BF16), jnp.where(low, 0.0, 0.125).astype(BF16)]
 
 
 def attend(q_s, k_s, v_s, bias, probs_s, mixed_s):
     low, masks = head_masks()
 
-    def tile(at, carry):
-        span = pl.ds(pl.multiple_of(at * 128, 128), 128)
+    def tile(at, masks):
+        start = at * 128
+        span = pl.ds(start if isinstance(at, int) else pl.multiple_of(start, 128), 128)
         queries, keys, values = q_s[:, span], k_s[:, span], v_s[:, span]
         found = []
         for head, mask in enumerate(masks):
-            scores = dot_nt(queries * mask, keys) * 0.125 + bias[...]
+            scores = dot_nt(queries * mask, keys) + bias[...]
             expo = jnp.exp(scores)
             probs = expo * (1.0 / jnp.sum(expo, axis=-1, keepdims=True))
             probs_s[2 * at + head] = probs
             found.append(dot(probs.astype(BF16), values))
-        mixed_s[:, span] = jnp.where(low, *found).astype(BF16)
-        return carry
-
-    lax.fori_loop(0, 3, tile, 0)
+        total = found[0] if len(found) == 1 else jnp.where(low, *found)
+        mixed_s[:, span] = total.astype(BF16)
+
+    def pair(at, carry):
+        tile(at, masks)
+        return carry
+
+    lax.fori_loop(0, 2, pair, 0)
+    tile(2, masks[:1])
 
 
 def attend_back(q_s, k_s, v_s, d_s, probs_s, qp_s, kp_s, vp_s):
     low, masks = head_masks()
 
-    def tile(at, carry):
-        span = pl.ds(pl.multiple_of(at * 128, 128), 128)
+    def tile(at, masks):
+        start = at * 128
+        span = pl.ds(start if isinstance(at, int) else pl.multiple_of(start, 128), 128)
         queries, keys, values, grads = q_s[:, span], k_s[:, span], v_s[:, span], d_s[:, span]
         found = []
         for head, mask in enumerate(masks):
             probs = probs_s[2 * at + head]
             prob_grad = dot_nt(grads * mask, values)
             inner = jnp.sum(probs * prob_grad, axis=-1, keepdims=True)
-            score_b = (probs * (prob_grad - inner) * 0.125).astype(BF16)
+            score_b = (probs * (prob_grad - inner)).astype(BF16)
             found.append(
                 (
                     dot(score_b, keys),
@@ -552,24 +551,31 @@
                     dot_tn(probs.astype(BF16), grads),
                 )
             )
-        for target, first, second in zip((qp_s, kp_s, vp_s), *found):
-            target[:, span] = jnp.where(low, first, second).astype(BF16)
-        return carry
-
-    lax.fori_loop(0, 3, tile, 0)
+        for place, target in enumerate((qp_s, kp_s, vp_s)):
+            parts = [part[place] for part in found]
+            total = parts[0] if len(parts) == 1 else jnp.where(low, *parts)
+            target[:, span] = total.astype(BF16)
+
+    def pair(at, carry):
+        tile(at, masks)
+        return carry
+
+    lax.fori_loop(0, 2, pair, 0)
+    tile(2, masks[:1])
 
 
 def block_kernel(sizes, latents, conv_w, query_w, key_w, value_w, out_w, gain, out_grad, *refs):
-    (block_out, latents_grad, conv_total, small_total), refs = refs[:4], refs[4:]
+    (block_hbm, back_hbm, conv_hbm, small_hbm), refs = refs[:4], refs[4:]
     (
         lat_in, grad_in, lat, grad, weights, wq, wk, wv, wo, gain_v, in_sems,
-        padded, halo, halo_send, halo_recv, acc, resid, act_c, act_in, act_t,
+        padded, wide, halo, halo_send, halo_recv, acc, resid, act_c, act_in, act_t,
         normed_out, normed_in, og_out, og_in, ng_out, ng_in, mix_out, mix_in,
         swap_send, swap_recv,
         og_n, normed_n, mixed_n, back_n,
         q_s, k_s, v_s, d_s, bias, probs_s, out_acc, mixed_s, qp_s, kp_s, vp_s, parts, flip,
         resid_grad, rg_in, conv_acc, pair_send, pair_recv, grad_pad, gain_acc, conv_terms, small_terms,
-    ), refs = refs[:56], refs[56:]
+        block_out, latents_grad, conv_total, small_total, out_sems,
+    ), refs = refs[:62], refs[62:]
     frames = lax.axis_size("frame")
     rows_n = lax.axis_size("row")
     chunk = HALF // frames
@@ -605,8 +611,10 @@
         cells = lat_in[at].astype(F32).T
         lat[span] = cells.astype(BF16)
         act = (cells * jax.nn.sigmoid(cells)).astype(BF16).astype(F32)
+        span = pl.ds((at + 1) * COLS, COLS)
         for shift, copy in enumerate(shifts(act)):
-            padded[shift, pl.ds((at + 1) * COLS, COLS)] = copy.astype(BF16)
+            wide[span, shift * CHAN : shift * CHAN + CHAN] = copy.astype(BF16)
+        padded[span] = act.astype(BF16)
         return carry
 
     lax.fori_loop(0, ROWS, activate, 0)
@@ -616,7 +624,9 @@
         cells = grad_in[at].astype(F32).T.astype(BF16)
         grad[pl.ds(at * COLS, COLS)] = cells
         half = jnp.where((at == 0) | (at == ROWS - 1), 1, 0)
-        store_chunks(og_out, half, jnp.where(at >= 2, 8, 0), cells)
+        span = pl.ds(jnp.where(at >= 2, frames // 2, 0), frames // 2)
+        og_out[half, span] = cells[:, :256].reshape(frames // 2, chunk, 256)
+        normed_out[half, span, :, CHAN:] = cells[:, 256:].reshape(frames // 2, chunk, 64)
         return carry
 
     lax.fori_loop(0, ROWS, flip_grad, 0)
@@ -630,17 +640,25 @@
                    halo_send.at[kind, 1], halo_recv.at[kind, 1], below),
         ]
 
-    def halo_end(copies, kind, target):
+    def halo_end(copies, kind, store):
         for copy in copies:
             copy.wait_recv()
         ends = (row > 0, row < rows_n - 1)
         for side, inside in enumerate(ends):
             keep = jnp.where(inside, 1.0, 0.0).astype(F32)
             cells = halo[kind, side].astype(F32) * keep
-            for shift, copy in enumerate(shifts(cells)):
-                target[shift, pl.ds(side * (ROWS + 1) * COLS, COLS)] = copy.astype(BF16)
-
-    act_halo = halo_start(padded.at[1], 0)
+            store(pl.ds(side * (ROWS + 1) * COLS, COLS), cells)
+
+    def store_act(span, cells):
+        for shift, copy in enumerate(shifts(cells)):
+            wide[span, shift * CHAN : shift * CHAN + CHAN] = copy.astype(BF16)
+        padded[span] = cells.astype(BF16)
+
+    def store_grad(span, cells):
+        for shift, copy in enumerate(shifts(cells)):
+            grad_pad[shift, span] = copy.astype(BF16)
+
+    act_halo = halo_start(padded, 0)
 
     swaps = []
     buffers = ((og_out, og_in), (normed_out, normed_in), (ng_out, ng_in), (mix_out, mix_in))
@@ -652,20 +670,17 @@
     loads[3].wait()
 
     def conv_half(half):
-        acc[pl.ds(0, HALF)] = jnp.zeros((HALF, CHAN), F32)
-
-        def tap(at, carry):
-            a, b = at // 3, lax.rem(at, 3)
+        total = None
+        for a in range(3):
             if half == 0:
-                cells = padded[b, pl.ds((a + 1) * COLS, HALF)]
+                cells = wide[(a + 1) * COLS : (a + 1) * COLS + HALF]
             else:
                 cells = jnp.concatenate(
-                    [padded[b, pl.ds(a * COLS, COLS)], padded[b, pl.ds((a + 3) * COLS, COLS)]]
+                    [wide[a * COLS : (a + 1) * COLS], wide[(a + 3) * COLS : (a + 4) * COLS]]
                 )
-            acc[pl.ds(0, HALF)] += dot(cells, weights[at])
-            return carry
-
-        lax.fori_loop(0, 9, tap, 0)
+            term = dot(cells, weights[3 * a : 3 * a + 3].reshape(3 * CHAN, CHAN))
+            total = term if total is None else total + term
+        acc[pl.ds(0, HALF)] = total
         count = 64 // chunk
 
         def finish(at, carry):
@@ -674,7 +689,7 @@
             resid[half, pl.ds(at * 64, 64)] = held
             held = held.astype(F32)
             normed = (held * norm_of(held) * gain_v[...].reshape(1, CHAN)).astype(BF16)
-            store_chunks(normed_out, half, at * count, normed)
+            normed_out[half, pl.ds(at * count, count), :, :CHAN] = normed.reshape(count, chunk, CHAN)
             return carry
 
         lax.fori_loop(0, 4, finish, 0)
@@ -682,7 +697,7 @@
     og_swap.start(0)
     conv_half(0)
     normed_swap.start(0)
-    halo_end(act_halo, 0, padded)
+    halo_end(act_halo, 0, store_act)
     conv_half(1)
     normed_swap.start(1)
     og_swap.start(1)
@@ -693,7 +708,7 @@
     bias[...] = jnp.where(same, 0.0, -1e30)
     for field in (q_s, k_s, v_s, d_s):
         field[:, 256:] = jnp.zeros((HALF, 128), BF16)
-    act_c[...] = padded[1].astype(F32).T.astype(BF16)
+    act_c[...] = padded[...].astype(F32).T.astype(BF16)
     core = place["c"]
     partner = along(place, "c", 1, sizes)
     mine = pl.ds(pl.multiple_of(core * HALF_CHAN, HALF_CHAN), HALF_CHAN)
@@ -707,7 +722,7 @@
         left = jnp.where(column == 0, 0.0, pltpu.roll(cells, 1, 1))
         right = jnp.where(column == COLS - 1, 0.0, pltpu.roll(cells, COLS - 1, 1))
         for shift, copy in enumerate((left, cells, right)):
-            act_t[side, shift, :, span] = copy.astype(BF16)
+            act_t[side, shift * HALF_CHAN : (shift + 1) * HALF_CHAN, span] = copy.astype(BF16)
         return carry
 
     own_rows = functools.partial(shift_lanes, source=act_c.at[mine], side=0)
@@ -717,30 +732,28 @@
 
     for half in range(2):
         normed_swap.wait(half)
-        load_chunks(normed_in, half, 0, frames, normed_n.at[half])
+        arrived = normed_in[half].reshape(HALF, WIDE)
+        normed_n[half] = arrived[:, :CHAN]
+        og_n[half, :, 256:] = arrived[:, CHAN:]
         q_s[:, :CHAN] = dot(normed_n[half], wq[...]).astype(BF16)
         k_s[:, :CHAN] = dot(normed_n[half], wk[...]).astype(BF16)
         v_s[:, :CHAN] = dot(normed_n[half], wv[...]).astype(BF16)
         attend(q_s, k_s, v_s, bias, probs_s, mixed_s)
         mixed_n[half] = mixed_s[:, :CHAN]
-        store_chunks(mix_out, half, 0, mixed_s[:, :CHAN])
+        mix_out[half] = mixed_s[:, :256].reshape(frames, chunk, 256)
+        ng_out[half, :, :, CHAN:] = mixed_s[:, 256:CHAN].reshape(frames, chunk, 64)
         og_swap.wait(half)
-        load_chunks(og_in, half, 0, frames, og_n.at[half])
+        og_n[half, :, :256] = og_in[half].reshape(HALF, 256)
         d_s[:, :CHAN] = dot_nt(og_n[half], wo[...]).astype(BF16)
         attend_back(q_s, k_s, v_s, d_s, probs_s, qp_s, kp_s, vp_s)
         back = dot_nt(qp_s[:, :CHAN], wq[...])
         back = back + dot_nt(kp_s[:, :CHAN], wk[...])
         back = back + dot_nt(vp_s[:, :CHAN], wv[...])
-        store_chunks(ng_out, half, 0, back.astype(BF16))
+        ng_out[half, :, :, :CHAN] = back.astype(BF16).reshape(frames, chunk, CHAN)
         ng_swap.start(half)
         for at, field in enumerate((qp_s, kp_s, vp_s)):
             parts[at, pl.ds(half * HALF, HALF)] = field[:, :CHAN]
 
-    mix_swap.start(0)
-    mix_swap.start(1)
-    pair[0].wait_recv()
-    other_rows = functools.partial(shift_lanes, source=act_in, side=1)
-    lax.fori_loop(0, ROWS + 2, other_rows, 0)
     flip[0] = normed_n[...].reshape(2 * HALF, CHAN).astype(F32).T.astype(BF16)
     flip[1] = mixed_n[...].reshape(2 * HALF, CHAN).astype(F32).T.astype(BF16)
     for at in range(3):
@@ -756,12 +769,12 @@
     gain_acc[...] = jnp.zeros((8, CHAN), F32)
     for half in range(2):
         ng_swap.wait(half)
-        load_chunks(ng_in, half, 0, frames, back_n)
 
         def undo_norm(at, carry, half=half):
+            count = 64 // chunk
             begin = pl.multiple_of(cell_start(half, at), 64)
             held = resid[half, pl.ds(at * 64, 64)].astype(F32)
-            back = back_n[pl.ds(at * 64, 64)].astype(F32)
+            back = ng_in[half, pl.ds(at * count, count), :, :CHAN].reshape(64, CHAN).astype(F32)
             inv = norm_of(held)
             product = back * held
             total = jnp.sum((product * inv).reshape(8, 8, CHAN), axis=0)
@@ -785,19 +798,30 @@
             )
         )
         if half == 0:
-            pair[1].wait_recv()
-
-            def first_taps(at, carry):
-                a, b = at // 3, lax.rem(at, 3)
-                span = pl.ds(pl.multiple_of((a + 1) * COLS, COLS), HALF)
-                conv_acc[at] = dot(act_t[0, b, :, span], resid_grad[0]) + dot(
-                    act_t[1, b, :, span], rg_in[0]
-                )
+            pair[0].wait_recv()
+            other_rows = functools.partial(shift_lanes, source=act_in, side=1)
+            lax.fori_loop(0, ROWS + 2, other_rows, 0)
+
+            def inner_taps(at, carry, side, cells):
+                span = pl.ds(pl.multiple_of((at + 1) * COLS, COLS), HALF)
+                total = dot(act_t[side, :, span], cells[0])
+                if side == 0:
+                    conv_acc[at] = total
+                else:
+                    conv_acc[at] += total
                 return carry
 
-            lax.fori_loop(0, 9, first_taps, 0)
+            lax.fori_loop(
+                0, 3, functools.partial(inner_taps, side=0, cells=resid_grad), 0
+            )
             small.core_end()
             small.scatter_start(0)
+            pair[1].wait_recv()
+            lax.fori_loop(0, 3, functools.partial(inner_taps, side=1, cells=rg_in), 0)
+        else:
+            mix_swap.start(0)
+            mix_swap.start(1)
+
 
     def pad_grad(at, carry):
         half = jnp.where((at == 0) | (at == ROWS - 1), 1, 0)
@@ -807,16 +831,15 @@
             grad_pad[shift, pl.ds((at + 1) * COLS, COLS)] = copy.astype(BF16)
         return carry
 
-    def edge_cells(side, b, a):
-        spans = [pl.ds(pl.multiple_of((a + gap) * COLS, COLS), COLS) for gap in (0, ROWS - 1)]
-        return jnp.concatenate([act_t[side, b, :, span] for span in spans], axis=1)
+    def edge_cells(side, at):
+        spans = [pl.ds(pl.multiple_of((at + gap) * COLS, COLS), COLS) for gap in (0, ROWS - 1)]
+        return jnp.concatenate([act_t[side, :, span] for span in spans], axis=1)
 
     def second_taps(at, carry):
-        a, b = at // 3, lax.rem(at, 3)
-        conv_acc[at] += dot(edge_cells(0, b, a), resid_grad[1])
-        return carry
-
-    lax.fori_loop(0, 9, second_taps, 0)
+        conv_acc[at] += dot(edge_cells(0, at), resid_grad[1])
+        return carry
+
+    lax.fori_loop(0, 3, second_taps, 0)
     lax.fori_loop(0, ROWS, pad_grad, 0)
     grad_halo = halo_start(grad_pad.at[1], 1)
 
@@ -831,21 +854,23 @@
     pair[2].wait_recv()
 
     def last_taps(at, carry):
-        a, b = at // 3, lax.rem(at, 3)
-        total = conv_acc[at] + dot(edge_cells(1, b, a), rg_in[1])
-        pack_half(total, conv_terms, at * HALF_TILES)
-        return carry
-
-    lax.fori_loop(0, 6, last_taps, 0)
+        total = conv_acc[at] + dot(edge_cells(1, at), rg_in[1])
+        for b in range(3):
+            part = total[b * HALF_CHAN : (b + 1) * HALF_CHAN]
+            pack_half(part, conv_terms, (at * 3 + b) * HALF_TILES)
+        return carry
+
+    lax.fori_loop(0, 2, last_taps, 0)
     conv.scatter_first(0)
-    lax.fori_loop(6, 9, last_taps, 0)
+    lax.fori_loop(2, 3, last_taps, 0)
     conv.scatter_first(1)
     small.scatter_end(0)
     small.scatter_start(1)
 
     def project_out(half):
         mix_swap.wait(half)
-        load_chunks(mix_in, half, 0, frames, back_n)
+        back_n[:, :256] = mix_in[half].reshape(HALF, 256)
+        back_n[:, 256:] = ng_in[half, :, :, CHAN:].reshape(HALF, 64)
         out_acc[...] = dot(back_n[...], wo[...])
 
         def write_out(at, carry):
@@ -856,7 +881,7 @@
 
         lax.fori_loop(0, 2, write_out, 0)
 
-    halo_end(grad_halo, 1, grad_pad)
+    halo_end(grad_halo, 1, store_grad)
     acc[...] = jnp.zeros((2 * HALF, CHAN), F32)
 
     def back_tap(at, carry):
@@ -865,14 +890,22 @@
         acc[...] += dot_nt(cells, weights[at])
         return carry
 
-    lax.fori_loop(0, 5, back_tap, 0)
+    lax.fori_loop(0, 3, back_tap, 0)
     small.scatter_end(1)
     small.scatter_start(2)
+    lax.fori_loop(3, 5, back_tap, 0)
     conv.scatter_second()
     small.scatter_end(2)
     small.gather_start(2)
+    stores = []
+
+    def store(source, target):
+        stores.append(pltpu.make_async_copy(source, target, out_sems.at[len(stores)]))
+        stores[-1].start()
+
     project_out(0)
     project_out(1)
+    store(block_out, block_hbm)
     conv.scatter_third()
     small.arrive()
     small.gather_start(1)
@@ -891,22 +924,31 @@
         return carry
 
     lax.fori_loop(0, ROWS, write_back, 0)
+    store(latents_grad, back_hbm)
     def return_small():
         small.arrive()
         small.core_back()
 
     conv.gather_rest(return_small)
+    own_half = pl.ds(place["c"] * PART, PART)
+    store(conv_total.at[own_half], conv_hbm.at[own_half])
     small.arrive()
+    store(small_total, small_hbm)
+    conv.back_wait()
+    other_half = pl.ds((1 - place["c"]) * PART, PART)
+    store(conv_total.at[other_half], conv_hbm.at[other_half])
     small.finish()
     conv.finish()
     for swap in swaps:
         swap.finish()
     for copy in act_halo + grad_halo + pair:
         copy.wait_send()
+    for copy in stores:
+        copy.wait()
 
 
 def block_scratch(sizes, frames):
-    field = (2, frames, 40, 128)
+    narrow, wide = (2, frames, HALF // frames, 256), (2, frames, HALF // frames, WIDE)
     vmem = pltpu.VMEM
     dma = pltpu.SemaphoreType.DMA
     weight = vmem((CHAN, CHAN), BF16)
@@ -914,22 +956,26 @@
         vmem((ROWS, CHAN, COLS), BF16), vmem((ROWS, CHAN, COLS), BF16),
         vmem((ROWS * COLS, CHAN), BF16), vmem((ROWS * COLS, CHAN), BF16),
         vmem((9, CHAN, CHAN), BF16), weight, weight, weight, weight, vmem((CHAN,), F32), dma((8,)),
-        vmem((3, (ROWS + 2) * COLS, CHAN), BF16), vmem((2, 2, COLS, CHAN), BF16),
+        vmem(((ROWS + 2) * COLS, CHAN), BF16), vmem(((ROWS + 2) * COLS, 3 * CHAN), BF16),
+        vmem((2, 2, COLS, CHAN), BF16),
         dma((2, 2)), dma((2, 2)), vmem((2 * HALF, CHAN), F32), vmem((2, HALF, CHAN), BF16),
         vmem((CHAN, (ROWS + 2) * COLS), BF16), vmem((HALF_CHAN, (ROWS + 2) * COLS), BF16),
-        vmem((2, 3, HALF_CHAN, (ROWS + 2) * COLS), BF16),
+        vmem((2, 3 * HALF_CHAN, (ROWS + 2) * COLS), BF16),
     ]
-    shapes += [vmem(field, BF16)] * 8 + [dma((4, 2)), dma((4, 2))]
+    shapes += [vmem(shape, BF16) for shape in (wide, wide, narrow, narrow, wide, wide, narrow, narrow)]
+    shapes += [dma((4, 2)), dma((4, 2))]
     shapes += [vmem((2, HALF, CHAN), BF16)] * 3 + [vmem((HALF, CHAN), BF16)]
     shapes += [vmem((HALF, WIDE), BF16)] * 4 + [vmem((HALF, HALF), F32)]
-    shapes += [vmem((6, HALF, HALF), F32), vmem((HALF, CHAN), F32)]
+    shapes += [vmem((5, HALF, HALF), F32), vmem((HALF, CHAN), F32)]
     shapes += [vmem((HALF, WIDE), BF16)] * 4
     shapes += [vmem((3, 2 * HALF, CHAN), BF16), vmem((2, CHAN, 2 * HALF), BF16)]
     shapes += [vmem((2, HALF, CHAN), BF16), vmem((2, HALF, CHAN), BF16)]
-    shapes += [vmem((9, HALF_CHAN, CHAN), F32), dma((3,)), dma((3,))]
+    shapes += [vmem((3, 3 * HALF_CHAN, CHAN), F32), dma((3,)), dma((3,))]
     shapes += [vmem((3, (ROWS + 2) * COLS, CHAN), BF16)]
     shapes += [vmem((8, CHAN), F32)]
     shapes += [vmem((PART, 16, 128), BF16), vmem((SMALL_TILES, 16, 128), BF16)]
+    shapes += [vmem((ROWS, CHAN, COLS), BF16)] * 2
+    shapes += [vmem((CONV_TILES, 16, 128), BF16), vmem((SMALL_TILES, 16, 128), BF16), dma((5,))]
     return shapes + summer_scratch("yxz", sizes) + conv_summer_scratch(sizes)
 
 
@@ -950,7 +996,7 @@
             jax.ShapeDtypeStruct((SMALL_TILES, 16, 128), BF16),
         ],
         in_specs=[anywhere] * 8,
-        out_specs=[inside] * 4,
+        out_specs=[anywhere] * 4,
         scratch_shapes=block_scratch(sizes, frames),
         compiler_params=pltpu.CompilerParams(
             collective_id=0, has_side_effects=True, vmem_limit_bytes=56 << 20
@@ -987,7 +1033,8 @@
             pltpu.VMEM((13, CHAN, CHAN), F32),
             pltpu.VMEM((2, ROWS, CHAN, COLS), BF16),
             pltpu.SemaphoreType.DMA((4,)),
-            pltpu.SemaphoreType.DMA((14,)),
+            pltpu.SemaphoreType.DMA((13,)),
+            pltpu.SemaphoreType.DMA((10, 2)),
             pltpu.SemaphoreType.DMA((13,)),
         ],
         compiler_params=pltpu.CompilerParams(vmem_limit_bytes=56 << 20),

time: 96.4 us -> 93.2 us (0.967)
  Pallas kernels: 95.6 us -> 92.3 us
    pallas_call x1, Pallas kernels: 90.1 us -> 86.8 us  [on_device(): pl.pallas_call(functools.partial(block_kernel, sizes), out_shape=[field,...]
where the time goes in v5:
time: 93.2 us; the launch traced here: 93.1 us
  Pallas kernels  92.3 us (99%)
    pallas_call x1, Pallas kernels, on_device(): pl.pallas_call(functools.partial(block_kernel, sizes), out_shape=[field,...  86.8 us
    pallas_call x1, Pallas kernels, on_device(): pl.pallas_call(functools.partial(finish_kernel, factor), out_shape=[field...  5.52 us

profile of v5, /device:TPU:1, one launch (start us, length us, event | category | flops | bytes accessed | tf_op | source)
XLA Modules:
  0.0 93.1 jit_solution(1501795372666288045)
XLA Ops:
  0.6 86.8 %shard_map.143 = (bf16[4,320,128]{2,1,0:T(8,128)(2,1)}, bf16[4,320,128]{2,1,0:T(8,128)(2,1)}, bf16[512,16,128]{2,1,0:T(8,128)(2,1)}, bf16[256,16,128]{2,1,0:T(8,128)(2,1)}) custom-call(bf16[4,320,128]{2,1,0:T(8,128)(2,1)} %bitcast.15, bf16[9,320,320]{2,1,0:T(8,128)(2,1)} %bitcast.14, bf16[320,320]{1,0:T(8,128)(2,1)} %query_w.1, bf16[320,320]{1,0:T(8,128)(2,1)} %key_w.1, ...), custom_call_target="tpu_custom_call" | custom-call | tf_op jit(solution)/shard_map/pallas_call | solution.py:990
  87.4 5.5 %shard_map.144 = (bf16[4,320,128]{2,1,0:T(8,128)(2,1)}, bf16[4,320,128]{2,1,0:T(8,128)(2,1)}, f32[9,320,320]{2,1,0:T(8,128)}, f32[320,320]{1,0:T(8,128)}, f32[32...) custom-call(bf16[4,320,128]{2,1,0:T(8,128)(2,1)} %get-tuple-element.20.block_in, ...), custom_call_target="tpu_custom_call" | custom-call | tf_op jit(solution)/shard_map/pallas_call | solution.py:1016

commit v6 on v5

--- a/solution.py
+++ b/solution.py
@@ -53,6 +53,12 @@
     return device_of(moved)
 
 
+def aslant(place, axis, step, depth, sizes):
+    moved = dict(place)
+    moved["z"] = lax.rem(place["z"] + depth, sizes["z"])
+    return along(moved, axis, step, sizes)
+
+
 def remote(source, target, send_sem, recv_sem, device):
     copy = pltpu.make_async_remote_copy(
         src_ref=source,
@@ -103,8 +109,8 @@
     def __init__(self, place, sizes, terms, total, scratch):
         self.place, self.sizes, self.terms, self.total = place, sizes, terms, total
         (
-            self.inbox0, self.held1, self.inbox1, self.held2, self.inbox2,
-            self.scatter0, self.scatter1, self.scatter2,
+            self.inbox0, self.held1, self.inbox2,
+            self.scatter0, self.scatter2,
             self.gather2, self.gather1, self.gather0, self.back, self.sends,
         ) = scratch
         self.unit = PART // (2 * sizes["x"] * sizes["y"] * sizes["z"])
@@ -153,39 +159,27 @@
                     total = total + self.inbox0[part, group, span].astype(F32)
                 held = self.held1.at[part, group]
                 held[...] = total.astype(BF16)
-                if step2 > 0:
+                nz = self.sizes["z"]
+                for depth in range(nz):
+                    if step2 + depth == 0:
+                        continue
+                    peer = lax.rem(self.place["z"] + depth, nz)
+                    slot = step2 * nz + depth - 1
                     remote(
-                        held,
-                        self.inbox1.at[part, pl.ds((step2 - 1) * self.group, self.group)],
+                        held.at[pl.ds(peer * self.unit, self.unit)],
+                        self.inbox2.at[part, pl.ds(slot * self.unit, self.unit)],
                         self.sends.at[2],
-                        self.scatter1.at[part],
-                        self.device(self.ORDERS[part][1], step2),
+                        self.scatter2.at[part],
+                        aslant(self.place, self.ORDERS[part][1], step2, depth, self.sizes),
                     )
-
-    def scatter_third(self):
-        for part in range(2):
-            wait_bytes(self.inbox1.at[part], self.scatter1.at[part])
-            total = self.held1[part, self.at(part, 1)].astype(F32)
-            for step in range(self.n2[part] - 1):
-                total = total + self.inbox1[part, pl.ds(step * self.group, self.group)].astype(F32)
-            self.held2[part] = total.astype(BF16)
-            for step in range(1, self.sizes["z"]):
-                peer = lax.rem(self.place["z"] + step, self.sizes["z"])
-                remote(
-                    self.held2.at[part, pl.ds(peer * self.unit, self.unit)],
-                    self.inbox2.at[part, pl.ds((step - 1) * self.unit, self.unit)],
-                    self.sends.at[3],
-                    self.scatter2.at[part],
-                    self.device("z", step),
-                )
 
     def gather_third(self):
         for part in range(2):
             wait_bytes(self.inbox2.at[part], self.scatter2.at[part])
             z = self.place["z"]
-            total = self.held2[part, pl.ds(z * self.unit, self.unit)].astype(F32)
-            for step in range(self.sizes["z"] - 1):
-                total = total + self.inbox2[part, pl.ds(step * self.unit, self.unit)].astype(F32)
+            own = self.held1[part, self.at(part, 1), pl.ds(z * self.unit, self.unit)].astype(F32)
+            others = self.inbox2[part].astype(F32).reshape(-1, self.unit, 16, 128)
+            total = own + jnp.sum(others, axis=0)
             mine = self.tile(part, self.at(part, 0), self.at(part, 1), z)
             self.total[pl.ds(mine, self.unit)] = total.astype(BF16)
             span = self.total.at[pl.ds(mine, self.unit)]
@@ -239,12 +233,13 @@
     def finish(self):
         n1, n2, nz = self.n1[0], self.n2[0], self.sizes["z"]
         counts = (
-            n2 * (n1 - 1) * self.group, n2 * (n1 - 1) * self.group, 2 * (n2 - 1) * self.group,
-            2 * (nz - 1) * self.unit, 2 * (nz - 1) * self.unit, 2 * (n2 - 1) * self.group,
+            n2 * (n1 - 1) * self.group, n2 * (n1 - 1) * self.group, 2 * (n2 * nz - 1) * self.unit,
+            0, 2 * (nz - 1) * self.unit, 2 * (n2 - 1) * self.group,
             2 * n2 * (n1 - 1) * self.group, PART,
         )
         for at, count in enumerate(counts):
-            wait_bytes(self.total.at[pl.ds(0, count)], self.sends.at[at])
+            if count:
+                wait_bytes(self.total.at[pl.ds(0, count)], self.sends.at[at])
 
 
 def conv_summer_scratch(sizes):
@@ -252,10 +247,10 @@
     group = unit * sizes["z"]
     n1, n2 = sizes["x"], sizes["y"]
     tiles = [
-        (2, n2, (n1 - 1) * group), (2, n2, group), (2, (n2 - 1) * group),
-        (2, group), (2, (sizes["z"] - 1) * unit),
+        (2, n2, (n1 - 1) * group), (2, n2, group),
+        (2, (n2 * sizes["z"] - 1) * unit),
     ]
-    sems = [(2, n2), (2,), (2,), (2,), (2, n2), (2, n2), (1,), (8,)]
+    sems = [(2, n2), (2,), (2,), (2, n2), (2, n2), (1,), (8,)]
     return [pltpu.VMEM(shape + (16, 128), BF16) for shape in tiles] + [
         pltpu.SemaphoreType.DMA(shape) for shape in sems
     ]
@@ -515,11 +510,11 @@
         queries, keys, values = q_s[:, span], k_s[:, span], v_s[:, span]
         found = []
         for head, mask in enumerate(masks):
-            scores = dot_nt(queries * mask, keys) + bias[...]
+            scores = dot_nt(keys, queries * mask) + bias[...]
             expo = jnp.exp(scores)
-            probs = expo * (1.0 / jnp.sum(expo, axis=-1, keepdims=True))
+            probs = expo * (1.0 / jnp.sum(expo, axis=0, keepdims=True))
             probs_s[2 * at + head] = probs
-            found.append(dot(probs.astype(BF16), values))
+            found.append(dot_tn(probs.astype(BF16), values))
         total = found[0] if len(found) == 1 else jnp.where(low, *found)
         mixed_s[:, span] = total.astype(BF16)
 
@@ -541,14 +536,14 @@
         found = []
         for head, mask in enumerate(masks):
             probs = probs_s[2 * at + head]
-            prob_grad = dot_nt(grads * mask, values)
-            inner = jnp.sum(probs * prob_grad, axis=-1, keepdims=True)
+            prob_grad = dot_nt(values, grads * mask)
+            inner = jnp.sum(probs * prob_grad, axis=0, keepdims=True)
             score_b = (probs * (prob_grad - inner)).astype(BF16)
             found.append(
                 (
-                    dot(score_b, keys),
-                    dot_tn(score_b, queries),
-                    dot_tn(probs.astype(BF16), grads),
+                    dot_tn(score_b, keys),
+                    dot(score_b, queries),
+                    dot(probs.astype(BF16), grads),
                 )
             )
         for place, target in enumerate((qp_s, kp_s, vp_s)):
@@ -592,6 +587,11 @@
     partners = [device for _, device in peers] + [above, below]
     for axis in "cxy":
         partners += [along(place, axis, step, sizes) for step in range(1, sizes[axis])]
+    for axis in "xy":
+        for step in range(1, sizes[axis]):
+            partners += [
+                aslant(place, axis, step, depth, sizes) for depth in range(1, sizes["z"])
+            ]
     for device in partners:
         pl.semaphore_signal(barrier, inc=1, device_id=device, device_id_type=MESH)
 
@@ -906,7 +906,6 @@
     project_out(0)
     project_out(1)
     store(block_out, block_hbm)
-    conv.scatter_third()
     small.arrive()
     small.gather_start(1)
     lax.fori_loop(5, 9, back_tap, 0)

time: 93.2 us -> 96.6 us (1.036)
  Pallas kernels: 92.3 us -> 95.7 us
    pallas_call x1, Pallas kernels: 86.8 us -> 90.2 us  [on_device(): pl.pallas_call(functools.partial(block_kernel, sizes), out_shape=[field,...]
where the time goes in v6:
time: 96.6 us; the launch traced here: 96.5 us
  Pallas kernels  95.7 us (99%)
    pallas_call x1, Pallas kernels, on_device(): pl.pallas_call(functools.partial(block_kernel, sizes), out_shape=[field,...  90.2 us
    pallas_call x1, Pallas kernels, on_device(): pl.pallas_call(functools.partial(finish_kernel, factor), out_shape=[field...  5.52 us

profile of v6, /device:TPU:1, one launch (start us, length us, event | category | flops | bytes accessed | tf_op | source)
XLA Modules:
  0.0 96.5 jit_solution(7853885514008734771)
XLA Ops:
  0.6 90.2 %shard_map.143 = (bf16[4,320,128]{2,1,0:T(8,128)(2,1)}, bf16[4,320,128]{2,1,0:T(8,128)(2,1)}, bf16[512,16,128]{2,1,0:T(8,128)(2,1)}, bf16[256,16,128]{2,1,0:T(8,128)(2,1)}) custom-call(bf16[4,320,128]{2,1,0:T(8,128)(2,1)} %bitcast.15, bf16[9,320,320]{2,1,0:T(8,128)(2,1)} %bitcast.14, bf16[320,320]{1,0:T(8,128)(2,1)} %query_w.1, bf16[320,320]{1,0:T(8,128)(2,1)} %key_w.1, ...), custom_call_target="tpu_custom_call" | custom-call | tf_op jit(solution)/shard_map/pallas_call | solution.py:989
  90.8 5.5 %shard_map.144 = (bf16[4,320,128]{2,1,0:T(8,128)(2,1)}, bf16[4,320,128]{2,1,0:T(8,128)(2,1)}, f32[9,320,320]{2,1,0:T(8,128)}, f32[320,320]{1,0:T(8,128)}, f32[32...) custom-call(bf16[4,320,128]{2,1,0:T(8,128)(2,1)} %get-tuple-element.20.block_in, ...), custom_call_target="tpu_custom_call" | custom-call | tf_op jit(solution)/shard_map/pallas_call | solution.py:1015

commit v7 on v5

--- a/solution.py
+++ b/solution.py
@@ -515,11 +515,11 @@
         queries, keys, values = q_s[:, span], k_s[:, span], v_s[:, span]
         found = []
         for head, mask in enumerate(masks):
-            scores = dot_nt(queries * mask, keys) + bias[...]
+            scores = dot_nt(keys, queries * mask) + bias[...]
             expo = jnp.exp(scores)
-            probs = expo * (1.0 / jnp.sum(expo, axis=-1, keepdims=True))
+            probs = expo * (1.0 / jnp.sum(expo, axis=0, keepdims=True))
             probs_s[2 * at + head] = probs
-            found.append(dot(probs.astype(BF16), values))
+            found.append(dot_tn(probs.astype(BF16), values))
         total = found[0] if len(found) == 1 else jnp.where(low, *found)
         mixed_s[:, span] = total.astype(BF16)
 
@@ -541,14 +541,14 @@
         found = []
         for head, mask in enumerate(masks):
             probs = probs_s[2 * at + head]
-            prob_grad = dot_nt(grads * mask, values)
-            inner = jnp.sum(probs * prob_grad, axis=-1, keepdims=True)
+            prob_grad = dot_nt(values, grads * mask)
+            inner = jnp.sum(probs * prob_grad, axis=0, keepdims=True)
             score_b = (probs * (prob_grad - inner)).astype(BF16)
             found.append(
                 (
-                    dot(score_b, keys),
-                    dot_tn(score_b, queries),
-                    dot_tn(probs.astype(BF16), grads),
+                    dot_tn(score_b, keys),
+                    dot(score_b, queries),
+                    dot(probs.astype(BF16), grads),
                 )
             )
         for place, target in enumerate((qp_s, kp_s, vp_s)):
@@ -818,9 +818,6 @@
             small.scatter_start(0)
             pair[1].wait_recv()
             lax.fori_loop(0, 3, functools.partial(inner_taps, side=1, cells=rg_in), 0)
-        else:
-            mix_swap.start(0)
-            mix_swap.start(1)
 
 
     def pad_grad(at, carry):
@@ -864,6 +861,8 @@
     conv.scatter_first(0)
     lax.fori_loop(2, 3, last_taps, 0)
     conv.scatter_first(1)
+    mix_swap.start(0)
+    mix_swap.start(1)
     small.scatter_end(0)
     small.scatter_start(1)
 
@@ -903,13 +902,13 @@
         stores.append(pltpu.make_async_copy(source, target, out_sems.at[len(stores)]))
         stores[-1].start()
 
+    lax.fori_loop(5, 9, back_tap, 0)
+    conv.scatter_third()
+    small.arrive()
+    small.gather_start(1)
     project_out(0)
     project_out(1)
     store(block_out, block_hbm)
-    conv.scatter_third()
-    small.arrive()
-    small.gather_start(1)
-    lax.fori_loop(5, 9, back_tap, 0)
     conv.gather_third()
     small.arrive()
     small.gather_start(0)

time: 93.2 us -> 95 us (1.019)
  Pallas kernels: 92.3 us -> 94.1 us
    pallas_call x1, Pallas kernels: 86.8 us -> 88.6 us  [on_device(): pl.pallas_call(functools.partial(block_kernel, sizes), out_shape=[field,...]
where the time goes in v7:
time: 95 us; the launch traced here: 94.9 us
  Pallas kernels  94.1 us (99%)
    pallas_call x1, Pallas kernels, on_device(): pl.pallas_call(functools.partial(block_kernel, sizes), out_shape=[field,...  88.6 us
    pallas_call x1, Pallas kernels, on_device(): pl.pallas_call(functools.partial(finish_kernel, factor), out_shape=[field...  5.52 us

profile of v7, /device:TPU:1, one launch (start us, length us, event | category | flops | bytes accessed | tf_op | source)
XLA Modules:
  0.0 94.9 jit_solution(13977196782316787014)
XLA Ops:
  0.6 88.6 %shard_map.143 = (bf16[4,320,128]{2,1,0:T(8,128)(2,1)}, bf16[4,320,128]{2,1,0:T(8,128)(2,1)}, bf16[512,16,128]{2,1,0:T(8,128)(2,1)}, bf16[256,16,128]{2,1,0:T(8,128)(2,1)}) custom-call(bf16[4,320,128]{2,1,0:T(8,128)(2,1)} %bitcast.15, bf16[9,320,320]{2,1,0:T(8,128)(2,1)} %bitcast.14, bf16[320,320]{1,0:T(8,128)(2,1)} %query_w.1, bf16[320,320]{1,0:T(8,128)(2,1)} %key_w.1, ...), custom_call_target="tpu_custom_call" | custom-call | tf_op jit(solution)/shard_map/pallas_call | solution.py:989
  89.2 5.5 %shard_map.144 = (bf16[4,320,128]{2,1,0:T(8,128)(2,1)}, bf16[4,320,128]{2,1,0:T(8,128)(2,1)}, f32[9,320,320]{2,1,0:T(8,128)}, f32[320,320]{1,0:T(8,128)}, f32[32...) custom-call(bf16[4,320,128]{2,1,0:T(8,128)(2,1)} %get-tuple-element.20.block_in, ...), custom_call_target="tpu_custom_call" | custom-call | tf_op jit(solution)/shard_map/pallas_call | solution.py:1015

commit v8 on v7

--- a/solution.py
+++ b/solution.py
@@ -818,6 +818,9 @@
             small.scatter_start(0)
             pair[1].wait_recv()
             lax.fori_loop(0, 3, functools.partial(inner_taps, side=1, cells=rg_in), 0)
+        else:
+            mix_swap.start(0)
+            mix_swap.start(1)
 
 
     def pad_grad(at, carry):
@@ -861,8 +864,6 @@
     conv.scatter_first(0)
     lax.fori_loop(2, 3, last_taps, 0)
     conv.scatter_first(1)
-    mix_swap.start(0)
-    mix_swap.start(1)
     small.scatter_end(0)
     small.scatter_start(1)
 
@@ -902,13 +903,13 @@
         stores.append(pltpu.make_async_copy(source, target, out_sems.at[len(stores)]))
         stores[-1].start()
 
-    lax.fori_loop(5, 9, back_tap, 0)
+    project_out(0)
+    project_out(1)
+    store(block_out, block_hbm)
     conv.scatter_third()
     small.arrive()
     small.gather_start(1)
-    project_out(0)
-    project_out(1)
-    store(block_out, block_hbm)
+    lax.fori_loop(5, 9, back_tap, 0)
     conv.gather_third()
     small.arrive()
     small.gather_start(0)

time: 95 us -> 92.7 us (0.976)
  Pallas kernels: 94.1 us -> 91.8 us
    pallas_call x1, Pallas kernels: 88.6 us -> 86.3 us  [on_device(): pl.pallas_call(functools.partial(block_kernel, sizes), out_shape=[field,...]
where the time goes in v8:
time: 92.7 us; the launch traced here: 92.6 us
  Pallas kernels  91.8 us (99%)
    pallas_call x1, Pallas kernels, on_device(): pl.pallas_call(functools.partial(block_kernel, sizes), out_shape=[field,...  86.3 us
    pallas_call x1, Pallas kernels, on_device(): pl.pallas_call(functools.partial(finish_kernel, factor), out_shape=[field...  5.52 us

profile of v8, /device:TPU:1, one launch (start us, length us, event | category | flops | bytes accessed | tf_op | source)
XLA Modules:
  0.0 92.6 jit_solution(11301720998633782303)
XLA Ops:
  0.6 86.3 %shard_map.143 = (bf16[4,320,128]{2,1,0:T(8,128)(2,1)}, bf16[4,320,128]{2,1,0:T(8,128)(2,1)}, bf16[512,16,128]{2,1,0:T(8,128)(2,1)}, bf16[256,16,128]{2,1,0:T(8,128)(2,1)}) custom-call(bf16[4,320,128]{2,1,0:T(8,128)(2,1)} %bitcast.15, bf16[9,320,320]{2,1,0:T(8,128)(2,1)} %bitcast.14, bf16[320,320]{1,0:T(8,128)(2,1)} %query_w.1, bf16[320,320]{1,0:T(8,128)(2,1)} %key_w.1, ...), custom_call_target="tpu_custom_call" | custom-call | tf_op jit(solution)/shard_map/pallas_call | solution.py:990
  87.0 5.5 %shard_map.144 = (bf16[4,320,128]{2,1,0:T(8,128)(2,1)}, bf16[4,320,128]{2,1,0:T(8,128)(2,1)}, f32[9,320,320]{2,1,0:T(8,128)}, f32[320,320]{1,0:T(8,128)}, f32[32...) custom-call(bf16[4,320,128]{2,1,0:T(8,128)(2,1)} %get-tuple-element.20.block_in, ...), custom_call_target="tpu_custom_call" | custom-call | tf_op jit(solution)/shard_map/pallas_call | solution.py:1016
